TPU v7x, 32 devices: a whole 2x2x4 slice. The times are simulated.
32 devices in a mesh: dp: 16 (over z, x, core), mp: 2 (over y).
Axes of the slice: x: 2, y: 2, z: 4, core: 2. Of those that a mesh axis runs over, the one named last changes fastest.
Arguments:
- tokens: bfloat16 [16384, 768], P(('dp', 'mp')), may hold values from -6 to 6
- pair_left: bfloat16 [16384, 256], P(('dp', 'mp')), may hold values from -6 to 6
- pair_right: bfloat16 [16384, 256], P(('dp', 'mp')), may hold values from -6 to 6
- chain_len: int32 [16, 8], P('dp'), may hold values from 0 to 800, as said below
- chain_time: float32 [16, 8], P('dp'), may hold values from 0 to 1
- chain_arch: int32 [16, 8], P('dp'), may hold values from 0 to 42
- cath_table: bfloat16 [43, 256], replicated, may hold values from -6 to 6
- time_weight: bfloat16 [256, 256], replicated, may hold values from -0.375 to 0.375
- mod_weight: bfloat16 [256, 4608], replicated, may hold values from -0.1875 to 0.1875
- mod_bias: bfloat16 [4608], replicated, may hold values from -3 to 3
- qkv_weight: bfloat16 [3, 768, 768], P(None, None, 'mp'), may hold values from -0.21875 to 0.21875
- pair_weight: bfloat16 [256, 12], P(None, 'mp'), may hold values from -0.375 to 0.375
- out_weight: bfloat16 [768, 768], P('mp'), may hold values from -1.25 to 1.25
- gate_up_weight: bfloat16 [2, 768, 3072], P(None, None, 'mp'), may hold values from -0.21875 to 0.21875
- down_weight: bfloat16 [3072, 768], P('mp'), may hold values from -0.21875 to 0.21875
- cotangent: bfloat16 [16384, 768], P(('dp', 'mp')), may hold values from -6 to 6
Outputs:
- mixed: bfloat16 [16384, 768], P(('dp', 'mp'))
- tokens_grad: bfloat16 [16384, 768], P(('dp', 'mp'))
- left_grad: bfloat16 [16384, 256], P(('dp', 'mp'))
- right_grad: bfloat16 [16384, 256], P(('dp', 'mp'))
- cath_grad: float32 [43, 256], replicated
- time_grad: float32 [256, 256], replicated
- mod_weight_grad: float32 [256, 4608], replicated
- mod_bias_grad: float32 [4608], replicated
- qkv_grad: float32 [3, 768, 768], P(None, 'dp', 'mp')
- pair_weight_grad: float32 [256, 12], P('dp', 'mp')
- out_weight_grad: float32 [768, 768], P('mp', 'dp')
- gate_up_grad: float32 [2, 768, 3072], P(None, 'dp', 'mp')
- down_grad: float32 [3072, 768], P('mp', 'dp')
Inputs may be any that keep to these rules, and one draw needn't show every extreme that they name: `chain_len`: row g gives the lengths of the chains packed one after another from the first position of group g; the first is the row's longest and exceeds 1024/2; zeros are empty slots; a row sums to at most 1024, positions after its sum are padding; some row's first length is exactly 800.
All inputs are finite; a program needn't handle non-finite values.
Results may differ from a plain program's by a relative error of at most 0.019.
Values may be sent and summed in bfloat16 or wider, within the bound.
No kernel may reach another device: no remote copies, remote signals or barrier semaphores. Data moves between devices by JAX's collectives and lax.ppermute only.
A program may use at most 192 MiB of HBM per device.

v0:
```python
import math

import jax
import jax.numpy as jnp
from jax import lax
from jax.sharding import PartitionSpec as P

EPSILON = 1e-06


def apply_norm(values):
    centered = values - jnp.mean(values, axis=-1, keepdims=True)
    inverse = lax.rsqrt(jnp.mean(centered * centered, axis=-1, keepdims=True) + EPSILON)
    return (centered * inverse, inverse)


def norm_backward(d_hat, x_hat, inverse):
    return inverse * (
        d_hat
        - jnp.mean(d_hat, axis=-1, keepdims=True)
        - x_hat * jnp.mean(d_hat * x_hat, axis=-1, keepdims=True)
    )


def highest_dot(left_side, right_side):
    return jnp.dot(left_side, right_side, precision=lax.Precision.HIGHEST)


def silu_parts(values):
    sigma = jax.nn.sigmoid(values)
    return (values * sigma, sigma * (1.0 + values * (1.0 - sigma)))


def reduce_ffn(d_gate_up, d_down):
    return (
        lax.psum_scatter(d_gate_up, "dp", scatter_dimension=1, tiled=True),
        lax.psum_scatter(d_down, "dp", scatter_dimension=1, tiled=True),
    )


def shards(
    tokens,
    pair_left,
    pair_right,
    chain_len,
    chain_time,
    chain_arch,
    cath_table,
    time_weight,
    mod_weight,
    mod_bias,
    qkv_weight,
    pair_weight,
    out_weight,
    gate_up_weight,
    down_weight,
    cotangent,
):
    tok_rows = tokens.shape[0]
    model_count = lax.axis_size("mp")
    group_rows = tok_rows * model_count
    chain_slots = chain_len.shape[1]
    heads_here = pair_weight.shape[1]
    head_width = qkv_weight.shape[2] // heads_here
    pair_width = pair_left.shape[1]
    cond_width = time_weight.shape[0]
    score_scale = head_width ** (-0.5)
    block_rows = min(512, group_rows)
    block_count = group_rows // block_rows
    chain_ends = jnp.cumsum(chain_len[0])
    positions = jnp.arange(group_rows, dtype=jnp.int32)
    chain_ids = jnp.sum((positions[:, None] >= chain_ends[None, :]).astype(jnp.int32), axis=1)
    local_ids = lax.dynamic_slice_in_dim(chain_ids, lax.axis_index("mp") * tok_rows, tok_rows, 0)
    membership = (local_ids[:, None] == jnp.arange(chain_slots, dtype=jnp.int32)[None, :]).astype(
        jnp.float32
    )
    valid_rows = (local_ids < chain_slots).astype(jnp.float32)[:, None]
    half_cond = cond_width // 2
    frequency = jnp.exp(jnp.arange(half_cond, dtype=jnp.float32) * (-math.log(10000.0) / half_cond))
    angles = chain_time[0][:, None] * 1000.0 * frequency[None, :]
    time_embed = jnp.concatenate([jnp.sin(angles), jnp.cos(angles)], axis=1).astype(jnp.bfloat16)
    arch_onehot = (
        chain_arch[0][:, None] == jnp.arange(cath_table.shape[0], dtype=jnp.int32)[None, :]
    ).astype(jnp.float32)
    cond_pre = jnp.dot(time_embed, time_weight, preferred_element_type=jnp.float32) + highest_dot(
        arch_onehot, cath_table.astype(jnp.float32)
    )
    cond_value, cond_slope = silu_parts(cond_pre)
    cond_act = cond_value.astype(jnp.bfloat16)
    chain_mod = (
        jnp.dot(cond_act, mod_weight, preferred_element_type=jnp.float32)
        + mod_bias.astype(jnp.float32)[None, :]
    )
    token_mod = highest_dot(membership, chain_mod)
    (
        attention_offset,
        attention_scale,
        gate_attn,
        feedforward_offset,
        feedforward_scale,
        gate_ffn,
    ) = jnp.split(token_mod, 6, axis=1)
    layer_input = tokens.astype(jnp.float32)
    attention_centered_input, attention_inverse_norm = apply_norm(layer_input)
    attention_normed = (
        attention_centered_input * (1.0 + attention_scale) + attention_offset
    ).astype(jnp.bfloat16)
    normed_all, left_all, right_all = (
        lax.all_gather(attention_normed, "mp", axis=0, tiled=True),
        lax.all_gather(pair_left, "mp", axis=0, tiled=True),
        lax.all_gather(pair_right, "mp", axis=0, tiled=True),
    )
    projected = jnp.einsum(
        "td,kdf->ktf", normed_all, qkv_weight, preferred_element_type=jnp.float32
    ).astype(jnp.bfloat16)
    queries = projected[0].reshape(group_rows, heads_here, head_width)
    keys_all = projected[1].reshape(group_rows, heads_here, head_width)
    values_all = projected[2].reshape(group_rows, heads_here, head_width)
    pair_mix = pair_weight.astype(jnp.float32)
    pair_query = (
        left_all.astype(jnp.float32)[:, None, :] * jnp.transpose(pair_mix)[None, :, :]
    ).astype(jnp.bfloat16)

    def scores_for(block_index):
        row_start = block_index * block_rows
        query_block = lax.dynamic_slice_in_dim(queries, row_start, block_rows, 0)
        pair_block = lax.dynamic_slice_in_dim(pair_query, row_start, block_rows, 0)
        ids_block = lax.dynamic_slice_in_dim(chain_ids, row_start, block_rows, 0)
        raw_scores = score_scale * jnp.einsum(
            "qhd,khd->hqk", query_block, keys_all, preferred_element_type=jnp.float32
        )
        raw_scores = raw_scores + jnp.einsum(
            "qhc,kc->hqk", pair_block, right_all, preferred_element_type=jnp.float32
        )
        allowed = ids_block[:, None] == chain_ids[None, :]
        return (jnp.where(allowed[None, :, :], raw_scores, -1e30), query_block, pair_block)

    def forward_block(block_index):
        masked, query_block, pair_block = scores_for(block_index)
        row_max = jnp.max(masked, axis=-1, keepdims=True)
        exponent = jnp.exp(masked - row_max)
        row_sum = jnp.sum(exponent, axis=-1, keepdims=True)
        probs_low = (exponent / row_sum).astype(jnp.bfloat16)
        block_out = jnp.einsum(
            "hqk,khd->qhd", probs_low, values_all, preferred_element_type=jnp.float32
        ).astype(jnp.bfloat16)
        return (
            block_out.reshape(block_rows, heads_here * head_width),
            (row_max + jnp.log(row_sum))[..., 0],
        )

    attended, log_total = lax.map(forward_block, jnp.arange(block_count))
    attended = attended.reshape(group_rows, heads_here * head_width)
    attn_branch = lax.psum_scatter(
        jnp.dot(attended, out_weight, preferred_element_type=jnp.float32),
        "mp",
        scatter_dimension=0,
        tiled=True,
    )
    middle_residual = layer_input + valid_rows * gate_attn * attn_branch
    feedforward_centered_input, feedforward_inverse_norm = apply_norm(middle_residual)
    feedforward_normed = (
        feedforward_centered_input * (1.0 + feedforward_scale) + feedforward_offset
    ).astype(jnp.bfloat16)
    output_gradient = cotangent.astype(jnp.float32)
    d_ffn = (valid_rows * gate_ffn * output_gradient).astype(jnp.bfloat16)
    normed_group = lax.all_gather(feedforward_normed, "mp", axis=0, tiled=True)
    gate_up = jnp.einsum(
        "td,kdf->ktf", normed_group, gate_up_weight, preferred_element_type=jnp.float32
    )
    gate_value, gate_slope = silu_parts(gate_up[0])
    hidden = (gate_value * gate_up[1]).astype(jnp.bfloat16)
    ffn_branch = lax.psum_scatter(
        jnp.dot(hidden, down_weight, preferred_element_type=jnp.float32).astype(jnp.bfloat16),
        "mp",
        scatter_dimension=0,
        tiled=True,
    ).astype(jnp.float32)
    d_ffn_group = lax.all_gather(d_ffn, "mp", axis=0, tiled=True)
    d_hidden = jnp.einsum("tm,fm->tf", d_ffn_group, down_weight, preferred_element_type=jnp.float32)
    d_down = jnp.einsum("tf,tm->fm", hidden, d_ffn_group, preferred_element_type=jnp.float32)
    d_gate_up_act = jnp.stack([d_hidden * gate_up[1] * gate_slope, d_hidden * gate_value]).astype(
        jnp.bfloat16
    )
    d_gate_up = jnp.einsum(
        "td,ktf->kdf", normed_group, d_gate_up_act, preferred_element_type=jnp.float32
    )
    feedforward_normed_gradient = lax.psum_scatter(
        jnp.einsum(
            "ktf,kdf->td", d_gate_up_act, gate_up_weight, preferred_element_type=jnp.float32
        ).astype(jnp.bfloat16),
        "mp",
        scatter_dimension=0,
        tiled=True,
    ).astype(jnp.float32)
    mixed = (middle_residual + valid_rows * gate_ffn * ffn_branch).astype(jnp.bfloat16)
    middle_gradient = output_gradient + norm_backward(
        feedforward_normed_gradient * (1.0 + feedforward_scale),
        feedforward_centered_input,
        feedforward_inverse_norm,
    )
    d_attn = (valid_rows * gate_attn * middle_gradient).astype(jnp.bfloat16)
    d_attn_group = lax.all_gather(d_attn, "mp", axis=0, tiled=True)
    d_attended = jnp.einsum(
        "tm,fm->tf", d_attn_group, out_weight, preferred_element_type=jnp.float32
    ).astype(jnp.bfloat16)
    d_out = jnp.einsum("tf,tm->fm", attended, d_attn_group, preferred_element_type=jnp.float32)
    d_attended_heads = d_attended.reshape(group_rows, heads_here, head_width)

    def backward_block(carry, block_index):
        d_keys, d_values, d_right = carry
        masked, query_block, pair_block = scores_for(block_index)
        probs_full = jnp.exp(masked - log_total[block_index][..., None])
        grad_block = lax.dynamic_slice_in_dim(
            d_attended_heads, block_index * block_rows, block_rows, 0
        )
        d_probs = jnp.einsum(
            "qhd,khd->hqk", grad_block, values_all, preferred_element_type=jnp.float32
        )
        row_dot = jnp.sum(probs_full * d_probs, axis=-1, keepdims=True)
        d_scores = (probs_full * (d_probs - row_dot)).astype(jnp.bfloat16)
        d_values = d_values + jnp.einsum(
            "hqk,qhd->khd",
            probs_full.astype(jnp.bfloat16),
            grad_block,
            preferred_element_type=jnp.float32,
        )
        d_query_block = score_scale * jnp.einsum(
            "hqk,khd->qhd", d_scores, keys_all, preferred_element_type=jnp.float32
        )
        d_pair_block = jnp.einsum(
            "hqk,kc->qhc", d_scores, right_all, preferred_element_type=jnp.float32
        )
        d_keys = d_keys + score_scale * jnp.einsum(
            "hqk,qhd->khd", d_scores, query_block, preferred_element_type=jnp.float32
        )
        d_right = d_right + jnp.einsum(
            "hqk,qhc->kc", d_scores, pair_block, preferred_element_type=jnp.float32
        )
        return ((d_keys, d_values, d_right), (d_query_block, d_pair_block))

    zero_heads = jnp.zeros((group_rows, heads_here, head_width), jnp.float32)
    zero_pair = jnp.zeros((group_rows, pair_width), jnp.float32)
    (d_keys, d_values, d_right), (d_queries, d_pair_query) = lax.scan(
        backward_block, (zero_heads, zero_heads, zero_pair), jnp.arange(block_count)
    )
    d_projected = jnp.stack(
        [
            d_queries.reshape(group_rows, -1),
            d_keys.reshape(group_rows, -1),
            d_values.reshape(group_rows, -1),
        ]
    ).astype(jnp.bfloat16)
    d_pair_query = d_pair_query.reshape(group_rows, heads_here, pair_width)
    d_qkv = jnp.einsum("td,ktf->kdf", normed_all, d_projected, preferred_element_type=jnp.float32)
    d_normed_part = jnp.einsum(
        "ktf,kdf->td", d_projected, qkv_weight, preferred_element_type=jnp.float32
    )
    d_left_part = jnp.sum(d_pair_query * jnp.transpose(pair_mix)[None, :, :], axis=1)
    d_pair_weight = jnp.einsum(
        "thc,tc->ch", d_pair_query, left_all.astype(jnp.float32), precision=lax.Precision.HIGHEST
    )
    attention_normed_gradient, d_left, d_right_mine = (
        lax.psum_scatter(
            d_normed_part.astype(jnp.bfloat16), "mp", scatter_dimension=0, tiled=True
        ).astype(jnp.float32),
        lax.psum_scatter(
            d_left_part.astype(jnp.bfloat16), "mp", scatter_dimension=0, tiled=True
        ).astype(jnp.float32),
        lax.psum_scatter(
            d_right.astype(jnp.bfloat16), "mp", scatter_dimension=0, tiled=True
        ).astype(jnp.float32),
    )
    token_gradient = middle_gradient + norm_backward(
        attention_normed_gradient * (1.0 + attention_scale),
        attention_centered_input,
        attention_inverse_norm,
    )
    d_token_mod = jnp.concatenate(
        [
            attention_normed_gradient,
            attention_normed_gradient * attention_centered_input,
            valid_rows * middle_gradient * attn_branch,
            feedforward_normed_gradient,
            feedforward_normed_gradient * feedforward_centered_input,
            valid_rows * output_gradient * ffn_branch,
        ],
        axis=1,
    )
    d_chain_mod = highest_dot(jnp.transpose(membership), d_token_mod)
    d_mod_bias = jnp.sum(d_chain_mod, axis=0)
    d_mod_weight = highest_dot(jnp.transpose(cond_act.astype(jnp.float32)), d_chain_mod)
    d_cond_pre = (
        highest_dot(d_chain_mod, jnp.transpose(mod_weight.astype(jnp.float32))) * cond_slope
    )
    d_time = highest_dot(jnp.transpose(time_embed.astype(jnp.float32)), d_cond_pre)
    d_cath = highest_dot(jnp.transpose(arch_onehot), d_cond_pre)
    cath_sum, time_sum, mod_weight_sum, mod_bias_sum = lax.psum(
        (d_cath, d_time, d_mod_weight, d_mod_bias), ("dp", "mp")
    )
    qkv_sum, pair_sum, out_sum = (
        lax.psum_scatter(d_qkv, "dp", scatter_dimension=1, tiled=True),
        lax.psum_scatter(d_pair_weight, "dp", scatter_dimension=0, tiled=True),
        lax.psum_scatter(d_out, "dp", scatter_dimension=1, tiled=True),
    )
    ffn_grads = reduce_ffn(d_gate_up, d_down)
    gate_up_sum, down_sum = ffn_grads
    return (
        mixed,
        token_gradient.astype(jnp.bfloat16),
        d_left.astype(jnp.bfloat16),
        d_right_mine.astype(jnp.bfloat16),
        cath_sum,
        time_sum,
        mod_weight_sum,
        mod_bias_sum,
        qkv_sum,
        pair_sum,
        out_sum,
        gate_up_sum,
        down_sum,
    )


def solution(mesh):
    placed = (
        P(("dp", "mp"), None),
        P(("dp", "mp"), None),
        P(("dp", "mp"), None),
        P("dp", None),
        P("dp", None),
        P("dp", None),
        P(),
        P(),
        P(),
        P(),
        P(None, None, "mp"),
        P(None, "mp"),
        P("mp", None),
        P(None, None, "mp"),
        P("mp", None),
        P(("dp", "mp"), None),
    )
    return jax.shard_map(
        shards,
        mesh=mesh,
        in_specs=placed,
        out_specs=(
            P(("dp", "mp"), None),
            P(("dp", "mp"), None),
            P(("dp", "mp"), None),
            P(("dp", "mp"), None),
            P(),
            P(),
            P(),
            P(),
            P(None, "dp", "mp"),
            P("dp", "mp"),
            P("mp", "dp"),
            P(None, "dp", "mp"),
            P("mp", "dp"),
        ),
        check_vma=False,
    )
```

profile of v0, /device:TPU:1, one launch (start us, length us, event | category | flops | bytes accessed | tf_op | source)
XLA Modules:
  0.0 1153.2 jit_solution(14201549693674456606)
XLA Ops:
  26.3 8.9 all_gather.20
  35.2 14.4 %all_gather.19 = bf16[1024,256]{1,0:T(8,128)(2,1)S(1)} all-gather(bf16[512,256]{1,0:T(8,128)(2,1)S(1)} %copy-done.36), channel_id=1, replica_groups=mesh['dp'=16,'mp'=2] {'mp'}, dimensions={0}, use_global_device_ids=true | all-gather | bytes 786432 | tf_op jit(solution)/shard_map/all_gather | solution.py:110
  53.1 8.4 all-gather.5.cloned.1.call-done
  61.5 4.0 convert_bitcast_fusion
  67.0 49.8 %while.31 = (s32[]{:T(128)}, bf16[2,512,384]{2,1,0:T(8,128)(2,1)}, f32[2,6,512]{2,1,0:T(8,128)}, s32[2]{0:T(128)S(1)}, s32[1024]{0:T(1024)S(1)}, /*index=5*/bf16...) while((s32[]{:T(128)}, bf16[2,512,384]{2,1,0:T(8,128)(2,1)}, ...), condition=%wide.region_7.8_spmd, body=%wide.region_4.7_spmd.sunk | while | flops 2444948480 | bytes 87931176 | solution.py:152
  68.7 7.5 fusion.161
  76.2 6.2 fusion.162
  85.3 4.0 fusion.164
  93.6 7.5 fusion.161
  101.2 6.2 fusion.162
  110.2 4.0 fusion.164
  120.8 43.2 %reduce-scatter.12.cloned.1.call-done = f32[512,768]{1,0:T(8,128)} async-done(((f32[1024,768]{1,0:T(8,128)}), f32[512,768]{1,0:T(8,128)}) %reduce-scatter.12.cloned.1.call-update) | async-done | bytes 1572880 | tf_op jit(solution)/shard_map/reduce_scatter | solution.py:154
  164.0 4.2 fusion.91
  173.3 26.6 %all-gather.7.cloned.1.call-done = bf16[1024,768]{1,0:T(8,128)(2,1)} async-done(((bf16[512,768]{1,0:T(8,128)(2,1)}), bf16[1024,768]{1,0:T(8,128)(2,1)}) %all-gather.7.cloned.1.call-update) | async-done | bytes 1572880 | tf_op jit(solution)/shard_map/all_gather | solution.py:167
  199.9 10.1 convolution_bitcast_fusion
  210.0 19.2 %all-gather.9.cloned.1.call-done = bf16[1024,768]{1,0:T(8,128)(2,1)} async-done(((bf16[512,768]{1,0:T(8,128)(2,1)}), bf16[1024,768]{1,0:T(8,128)(2,1)}) %all-gather.9.cloned.1.call-update) | async-done | bytes 1572880 | tf_op jit(solution)/shard_map/all_gather | solution.py:179
  229.2 9.0 fusion.46
  240.8 8.6 bitcast_convert_fusion.1
  249.5 5.6 convolution_convert_fusion
  255.2 20.5 %reduce-scatter.16.cloned.1.call-done = bf16[512,768]{1,0:T(8,128)(2,1)} async-done(((bf16[1024,768]{1,0:T(8,128)(2,1)}), bf16[512,768]{1,0:T(8,128)(2,1)}) %reduce-scatter.16.cloned.1.call-update) | async-done | bytes 786448 | tf_op jit(solution)/shard_map/reduce_scatter | solution.py:188
  277.9 26.0 %reduce-scatter.14.cloned.1.call-done = bf16[512,768]{1,0:T(8,128)(2,1)} async-done(((bf16[1024,768]{1,0:T(8,128)(2,1)}), bf16[512,768]{1,0:T(8,128)(2,1)}) %reduce-scatter.14.cloned.1.call-update) | async-done | bytes 786448 | tf_op jit(solution)/shard_map/reduce_scatter | solution.py:173
  303.9 4.5 multiply_convert_fusion.5
  308.5 27.3 %all-gather.11.cloned.1.call-done = bf16[1024,768]{1,0:T(8,128)(2,1)} async-done(((bf16[512,768]{1,0:T(8,128)(2,1)}), bf16[1024,768]{1,0:T(8,128)(2,1)}) %all-gather.11.cloned.1.call-update) | async-done | bytes 1572880 | tf_op jit(solution)/shard_map/all_gather | solution.py:203
  339.0 115.6 %while.32 = (s32[]{:T(128)}, f32[1024,6,64]{0,2,1:T(8,128)S(1)}, f32[1024,6,64]{0,2,1:T(8,128)}, f32[1024,256]{1,0:T(8,128)}, bf16[2,512,6,64]{1,3,2,0:T(8,128)(...) while((s32[]{:T(128)}, f32[1024,6,64]{0,2,1:T(8,128)S(1)}, ...), condition=%wide.region_17.18_spmd.clone, body=%wide.region_15.17_spmd.clone.sunk | while | flops 6879769600 | bytes 287910528 | solution.py:244
  343.6 7.7 fusion.179
  351.3 6.4 fusion.180
  357.7 13.7 %multiply_reduce_fusion.5 = (f32[6,512]{1,0:T(8,128)S(1)}, f32[6,512,1024]{2,1,0:T(8,128)}) fusion(f32[6,512,1024]{2,1,0:T(8,128)} %fusion.179, f32[6,512]{1,0:T(8,128)S(1)} %dynamic-slice_bitcast_fusion.2, bf16[1024,256]{1,0:T(8,128)(2,1)S(1)} %get-tuple-element.596, bf16[1024,6,256]{2,0,1:T(8,128)(2,1)S(1)} %copy-done.4, s32[]{:T(128)S(6)} %select_n.38, ...), kind=kOutput, calls=%fused_computation.21.clone.1 | convolution fusion | flops 1629484032 | bytes 40398852 | tf_op jit(solution)/shard_map/while/body/eval_jaxpr/qhc,kc->hqk/dot_general | solution.py:132
  371.4 9.1 multiply_convert_fusion.10
  401.0 7.7 fusion.179
  408.8 6.4 fusion.180
  415.1 13.7 %multiply_reduce_fusion.5 = (f32[6,512]{1,0:T(8,128)S(1)}, f32[6,512,1024]{2,1,0:T(8,128)}) fusion(f32[6,512,1024]{2,1,0:T(8,128)} %fusion.179, f32[6,512]{1,0:T(8,128)S(1)} %dynamic-slice_bitcast_fusion.2, bf16[1024,256]{1,0:T(8,128)(2,1)S(1)} %get-tuple-element.596, bf16[1024,6,256]{2,0,1:T(8,128)(2,1)S(1)} %copy-done.4, s32[]{:T(128)S(6)} %select_n.38, ...), kind=kOutput, calls=%fused_computation.21.clone.1 | convolution fusion | flops 1629484032 | bytes 40398852 | tf_op jit(solution)/shard_map/while/body/eval_jaxpr/qhc,kc->hqk/dot_general | solution.py:132
  428.9 9.1 multiply_convert_fusion.10
  460.4 5.3 bitcast_convert_fusion
  465.7 10.0 convolution_bitcast_fusion.1
  475.8 15.0 %copy.75 = f32[2,768,1536]{2,0,1:T(2,128)} copy(f32[2,768,1536]{1,2,0:T(8,128)} %convolution_bitcast_fusion.1) | data formatting | bytes 18874368 | tf_op jit(solution)/shard_map/td,ktf->kdf/transpose | solution.py:185
  496.3 5.5 convolution_bitcast_fusion.2
  501.8 6.3 copy.72
  508.9 4.3 multiply_reduce_fusion.1
  518.0 7.1 fusion.97
  541.9 4.2 fusion.90
  551.2 44.9 %all-reduce.2 = (f32[43,256]{1,0:T(8,128)}, f32[4608]{0:T(1024)}) all-reduce(f32[43,256]{1,0:T(8,128)S(1)} %fusion.79, f32[4608]{0:T(1024)S(1)} %get-tuple-element.339), channel_id=1, replica_groups=mesh['dp'=16,'mp'=2] {'dp','mp'}, use_global_device_ids=true, to_apply=%region_24.25 | all-reduce | flops 15616 | bytes 124928 | tf_op jit(solution)/shard_map/psum | solution.py:298
  596.0 216.2 %all-reduce.10.cloned.1.call-done = (f32[3,768,384]{2,0,1:T(4,128)}, f32[2,768,1536]{2,0,1:T(2,128)}) async-done(((f32[3,768,384]{2,0,1:T(4,128)}, f32[2,768,1536]{2,0,1:T(2,128)}), (f32[3,768,384]{2,0,1:T(4,128)}, f32[2,768,1536]{2,0,1:T(2,128)})) %all-reduce.10.cloned.1.call-update) | async-done | bytes 12976144
  816.0 14.1 %reduce-scatter.20.cloned.1.call-done = bf16[512,256]{1,0:T(8,128)(2,1)} async-done(((bf16[1024,256]{1,0:T(8,128)(2,1)}), bf16[512,256]{1,0:T(8,128)(2,1)}) %reduce-scatter.20.cloned.1.call-update) | async-done | bytes 262160 | tf_op jit(solution)/shard_map/reduce_scatter | solution.py:267
  830.2 17.3 %reduce-scatter.22.cloned.1.call-done = bf16[512,256]{1,0:T(8,128)(2,1)} async-done(((bf16[1024,256]{1,0:T(8,128)(2,1)}), bf16[512,256]{1,0:T(8,128)(2,1)}) %reduce-scatter.22.cloned.1.call-update) | async-done | bytes 262160 | tf_op jit(solution)/shard_map/reduce_scatter | solution.py:270
  847.5 60.4 %reduce-scatter.24.cloned.1.call-done = f32[384,48]{0,1:T(8,128)} async-done(((f32[384,768]{0,1:T(8,128)}), f32[384,48]{0,1:T(8,128)}) %reduce-scatter.24.cloned.1.call-update) | async-done | bytes 73744 | tf_op jit(solution)/shard_map/reduce_scatter | solution.py:304
  907.9 79.7 %reduce-scatter.26.cloned.1.call-done = f32[1536,48]{0,1:T(8,128)} async-done(((f32[1536,768]{0,1:T(8,128)}), f32[1536,48]{0,1:T(8,128)}) %reduce-scatter.26.cloned.1.call-update) | async-done | bytes 294928 | tf_op jit(solution)/shard_map/reduce_scatter | solution.py:37
  987.7 152.2 %all-reduce.8.cloned.1.call-done = (f32[256,256]{1,0:T(8,128)}, f32[256,4608]{1,0:T(8,128)}) async-done(((f32[256,256]{1,0:T(8,128)}, f32[256,4608]{1,0:T(8,128)}), (f32[256,256]{1,0:T(8,128)}, f32[256,4608]{1,0:T(8,128)})) %all-reduce.8.cloned.1.call-update) | async-done | bytes 4980752 | tf_op jit(solution)/shard_map/psum | solution.py:298
  1141.5 5.0 copy.137
  (290 shorter events, 133.1 us)
Async XLA Ops:
  7.2 222.0 %copy-start = (bf16[1536,768]{1,0:T(8,128)(2,1)S(1)}, bf16[1536,768]{1,0:T(8,128)(2,1)}, u32[]{:S(2)}) copy-start(bf16[1536,768]{1,0:T(8,128)(2,1)} %param.34) | copy-start | bytes 7077892
  7.2 54.3 %all-gather.5.cloned.1.call-start = ((), (), s32[]{:S(2)}) async-start(), calls=%async_computation.9 | async-start | bytes 2359296 | tf_op jit(solution)/shard_map/all_gather | solution.py:109
  10.2 11.1 copy-start.45
  11.7 9.6 copy-start.51
  13.3 4.1 copy-start.39
  17.4 7.5 copy-start.18
  24.9 10.3 copy-start.36
  26.2 23.4 %copy-start.57 = (bf16[256,6]{0,1:T(8,128)(2,1)S(1)}, bf16[256,6]{0,1:T(8,128)(2,1)}, u32[]{:S(2)}) copy-start(bf16[256,6]{0,1:T(8,128)(2,1)} %param.31) | copy-start | bytes 9220
  26.2 137.8 %reduce-scatter.12.cloned.1.call-start = ((), (), s32[]{:S(2)}) async-start(), calls=%async_computation.10 | async-start | bytes 4718592 | tf_op jit(solution)/shard_map/reduce_scatter | solution.py:154
  68.7 7.6 copy-start.3
  68.7 7.6 copy-start.6
  93.6 7.6 copy-start.3
  93.6 7.6 copy-start.6
  120.7 43.3 %copy-start.49 = (f32[512]{0:T(512)S(1)}, f32[512]{0:T(512)}, u32[]{:S(2)}) copy-start(f32[512]{0:T(512)} %get-tuple-element.318) | copy-start | bytes 6148
  120.7 79.2 %all-gather.7.cloned.1.call-start = ((), (), s32[]{:S(2)}) async-start(), calls=%async_computation.11 | async-start | bytes 2359296 | tf_op jit(solution)/shard_map/all_gather | solution.py:167
  168.2 135.7 %copy-start.43 = (f32[512]{0:T(512)}, f32[512]{0:T(512)S(1)}, u32[]{:S(2)}) copy-start(f32[512]{0:T(512)S(1)} %broadcast_multiply_fusion.4) | copy-start | bytes 6148
  169.4 134.5 %copy-start.47 = (f32[512]{0:T(512)}, f32[512]{0:T(512)S(1)}, u32[]{:S(2)}) copy-start(f32[512]{0:T(512)S(1)} %add_rsqrt_fusion) | copy-start | bytes 6148
  172.5 56.7 %all-gather.9.cloned.1.call-start = ((), (), s32[]{:S(2)}) async-start(), calls=%async_computation.13 | async-start | bytes 2359296 | tf_op jit(solution)/shard_map/all_gather | solution.py:179
  173.1 102.6 %reduce-scatter.16.cloned.1.call-start = ((), (), s32[]{:S(2)}) async-start(), calls=%async_computation.14 | async-start | bytes 2359296 | tf_op jit(solution)/shard_map/reduce_scatter | solution.py:188
  249.4 54.5 %reduce-scatter.14.cloned.1.call-start = ((), (), s32[]{:S(2)}) async-start(), calls=%async_computation.12 | async-start | bytes 2359296 | tf_op jit(solution)/shard_map/reduce_scatter | solution.py:173
  255.1 20.5 %copy-start.10 = (f32[512,768]{1,0:T(8,128)S(1)}, f32[512,768]{1,0:T(8,128)}, u32[]{:S(2)}) copy-start(f32[512,768]{1,0:T(8,128)} %copy-done.9) | copy-start | bytes 4718596
  255.2 80.6 %all-gather.11.cloned.1.call-start = ((), (), s32[]{:S(2)}) async-start(), calls=%async_computation.15 | async-start | bytes 2359296 | tf_op jit(solution)/shard_map/all_gather | solution.py:203
  275.7 28.2 %copy-start.23 = (bf16[512,768]{1,0:T(8,128)(2,1)S(1)}, bf16[512,768]{1,0:T(8,128)(2,1)}, u32[]{:S(2)}) copy-start(bf16[512,768]{1,0:T(8,128)(2,1)} %reduce-scatter.16.cloned.1.call-done) | copy-start | bytes 2359300
  308.4 30.6 %copy-start.7 = (bf16[1024,256]{1,0:T(8,128)(2,1)S(1)}, bf16[1024,256]{1,0:T(8,128)(2,1)}, u32[]{:S(2)}) copy-start(bf16[1024,256]{1,0:T(8,128)(2,1)} %get-tuple-element.641) | copy-start | bytes 1572868
  308.4 216.9 %reduce-scatter.18.cloned.1.call-start = ((), (), s32[]{:S(2)}) async-start(), calls=%async_computation.16 | async-start | bytes 2359296 | tf_op jit(solution)/shard_map/reduce_scatter | solution.py:264
  343.5 7.7 copy-start.8
  351.3 6.4 copy-start.4
  371.4 11.8 %copy-start.2 = (f32[6,512,1024]{2,1,0:T(8,128)S(1)}, f32[6,512,1024]{2,1,0:T(8,128)}, u32[]{:S(2)}) copy-start(f32[6,512,1024]{2,1,0:T(8,128)} %get-tuple-element.501) | copy-start | bytes 37748740 | tf_op jit(solution)/shard_map/while
  371.4 12.2 %copy-start.12 = (f32[1024,6,64]{0,2,1:T(8,128)S(1)}, f32[1024,6,64]{0,2,1:T(8,128)}, u32[]{:S(2)}) copy-start(f32[1024,6,64]{0,2,1:T(8,128)} %get-tuple-element.567) | copy-start | bytes 4718596 | tf_op jit(solution)/shard_map/while
  371.4 12.4 %copy-start.22 = (bf16[1024,6,64]{0,2,1:T(8,128)(2,1)S(1)}, bf16[1024,6,64]{0,2,1:T(8,128)(2,1)}, u32[]{:S(2)}) copy-start(bf16[1024,6,64]{0,2,1:T(8,128)(2,1)} %get-tuple-element.598) | copy-start | bytes 2359300 | tf_op jit(solution)/shard_map/while
  388.0 3.7 slice-start
  401.0 7.7 copy-start.8
  408.8 6.4 copy-start.4
  428.8 11.8 %copy-start.2 = (f32[6,512,1024]{2,1,0:T(8,128)S(1)}, f32[6,512,1024]{2,1,0:T(8,128)}, u32[]{:S(2)}) copy-start(f32[6,512,1024]{2,1,0:T(8,128)} %get-tuple-element.501) | copy-start | bytes 37748740 | tf_op jit(solution)/shard_map/while
  428.8 12.2 %copy-start.12 = (f32[1024,6,64]{0,2,1:T(8,128)S(1)}, f32[1024,6,64]{0,2,1:T(8,128)}, u32[]{:S(2)}) copy-start(f32[1024,6,64]{0,2,1:T(8,128)} %get-tuple-element.567) | copy-start | bytes 4718596 | tf_op jit(solution)/shard_map/while
  428.8 12.4 %copy-start.22 = (bf16[1024,6,64]{0,2,1:T(8,128)(2,1)S(1)}, bf16[1024,6,64]{0,2,1:T(8,128)(2,1)}, u32[]{:S(2)}) copy-start(bf16[1024,6,64]{0,2,1:T(8,128)(2,1)} %get-tuple-element.598) | copy-start | bytes 2359300 | tf_op jit(solution)/shard_map/while
  460.4 5.3 copy-start.33
  465.7 83.8 %reduce-scatter.28.cloned.1.call-start = ((), (), s32[]{:S(2)}) async-start(), calls=%async_computation.21 | async-start | bytes 139264
  490.8 3.7 copy-start.30
  496.2 316.0 %all-reduce.10.cloned.1.call-start = ((), (), s32[]{:S(2)}) async-start(), calls=%async_computation.23 | async-start | bytes 28311552
  508.2 5.0 copy-start.17
  508.2 322.0 %reduce-scatter.20.cloned.1.call-start = ((), (), s32[]{:S(2)}) async-start(), calls=%async_computation.17 | async-start | bytes 786432 | tf_op jit(solution)/shard_map/reduce_scatter | solution.py:267
  513.2 334.3 %reduce-scatter.22.cloned.1.call-start = ((), (), s32[]{:S(2)}) async-start(), calls=%async_computation.18 | async-start | bytes 786432 | tf_op jit(solution)/shard_map/reduce_scatter | solution.py:270
  514.1 393.8 %reduce-scatter.24.cloned.1.call-start = ((), (), s32[]{:S(2)}) async-start(), calls=%async_computation.19 | async-start | bytes 1253376 | tf_op jit(solution)/shard_map/reduce_scatter | solution.py:304
  518.0 469.7 %reduce-scatter.26.cloned.1.call-start = ((), (), s32[]{:S(2)}) async-start(), calls=%async_computation.20 | async-start | bytes 5013504 | tf_op jit(solution)/shard_map/reduce_scatter | solution.py:37
  525.2 614.6 %all-reduce.8.cloned.1.call-start = ((), (), s32[]{:S(2)}) async-start(), calls=%async_computation.22 | async-start | bytes 9961472 | tf_op jit(solution)/shard_map/psum | solution.py:298
  546.2 4.7 copy-start.58
  1141.5 5.0 copy-start.1
  (45 other events, 91.0 us)
Sparse Core Ops, SparseCore 0:
  26.4 35.1 all-gather.4
  120.9 43.1 reduce-scatter.11
  172.6 27.2 all-gather.6
  201.9 27.2 all-gather.8
  249.5 26.0 reduce-scatter.15
  277.8 26.0 reduce-scatter.13
  308.5 27.2 all-gather.10
  465.8 26.0 reduce-scatter.17
  496.4 53.1 reduce-scatter.27
  553.5 258.7 all-reduce.9
  815.1 15.0 reduce-scatter.19
  832.9 14.5 reduce-scatter.21
  851.7 56.1 reduce-scatter.23
  912.2 75.4 reduce-scatter.25
  995.0 144.7 all-reduce.7
where the time goes:
time: 1160 us; the launch traced here: 1150 us
  waiting for transfers between devices  713 us (61%)
  matrix products  205 us (18%)
  local copies, waits for them, and re-layouts  77.4 us (7%)
  blocking collectives  68.2 us (6%)
  other arithmetic  65.4 us (6%)
  between operations  15.3 us (1%)
    unnamed x17, waiting for transfers between devices  218 us
    psum x1, waiting for transfers between devices, shards(): lax.psum((d_cath, d_time, d_mod_weight, d_mod_bias), ('dp', 'mp'))  152 us
    reduce_scatter x1, waiting for transfers between devices, reduce_ffn(): lax.psum_scatter(d_down, 'dp', scatter_dimension=1, tiled=True)  79.7 us
    reduce_scatter x1, waiting for transfers between devices, shards(): lax.psum_scatter(d_out, 'dp', scatter_dimension=1, tiled=True)  60.4 us
    psum x1, blocking collectives, shards(): lax.psum((d_cath, d_time, d_mod_weight, d_mod_bias), ('dp', 'mp'))  44.9 us
    reduce_scatter x1, waiting for transfers between devices, shards(): lax.psum_scatter(jnp.dot(attended, out_weight, preferred_element_type=jnp...  43.2 us
    dot_general x4, matrix products, scores_for(): jnp.einsum('qhc,kc->hqk', pair_block, right_all, preferred_element_type=j...  39.8 us
    dot_general x4, matrix products, scores_for(): jnp.einsum('qhd,khd->hqk', query_block, keys_all, preferred_element_type=...  27.8 us
  transfers between devices with their start and end apart: 15, of which 14 were waited for; matrix products, arithmetic and copies ran while one was open for 9% of the time, Pallas kernels for 0%

commit v1 on v0

v1 whole, which is shorter than its diff:
```python
import math

import jax
import jax.numpy as jnp
from jax import lax
from jax.sharding import PartitionSpec as P

EPSILON = 1e-06
AXES = ("dp", "mp")
BF16 = jnp.bfloat16
F32 = jnp.float32


def apply_norm(values):
    centered = values - jnp.mean(values, axis=-1, keepdims=True)
    inverse = lax.rsqrt(jnp.mean(centered * centered, axis=-1, keepdims=True) + EPSILON)
    return (centered * inverse, inverse)


def norm_backward(d_hat, x_hat, inverse):
    return inverse * (
        d_hat
        - jnp.mean(d_hat, axis=-1, keepdims=True)
        - x_hat * jnp.mean(d_hat * x_hat, axis=-1, keepdims=True)
    )


def highest_dot(left_side, right_side):
    return jnp.dot(left_side, right_side, precision=lax.Precision.HIGHEST)


def silu_parts(values):
    sigma = jax.nn.sigmoid(values)
    return (values * sigma, sigma * (1.0 + values * (1.0 - sigma)))


def dot_f32(left_side, right_side):
    return jnp.dot(left_side, right_side, preferred_element_type=F32)


def dot_nt(left_side, right_side):
    return lax.dot_general(
        left_side, right_side, (((1,), (1,)), ((), ())), preferred_element_type=F32
    )


def make_moves(dp_count):
    def pairs(target):
        moved = []
        for d in range(dp_count):
            for m in range(2):
                to_d, to_m = target(d, m)
                moved.append((d * 2 + m, to_d * 2 + to_m))
        return moved

    def mover(target):
        table = pairs(target)
        return lambda array: lax.ppermute(array, AXES, table)

    turn = mover(lambda d, m: ((d & ~1) | m, d & 1))
    across = mover(lambda d, m: (d, 1 - m))

    def flip(bit):
        return mover(lambda d, m: (d ^ (1 << bit), m))

    return turn, across, flip


def shards(
    tokens,
    pair_left,
    pair_right,
    chain_len,
    chain_time,
    chain_arch,
    cath_table,
    time_weight,
    mod_weight,
    mod_bias,
    qkv_weight,
    pair_weight,
    out_weight,
    gate_up_weight,
    down_weight,
    cotangent,
):
    dp_count = lax.axis_size("dp")
    bits = dp_count.bit_length() - 1
    turn, across, flip = make_moves(dp_count)
    core_swap = flip(0)
    dp_at = lax.axis_index("dp")
    mp_at = lax.axis_index("mp")
    core = dp_at & 1
    rows, width = tokens.shape
    slots = chain_len.shape[1]
    half_heads = pair_weight.shape[1]
    heads = 2 * half_heads
    head_width = qkv_weight.shape[2] // half_heads
    cond_width = time_weight.shape[0]
    score_scale = head_width ** (-0.5)

    held_chains = jnp.concatenate(
        [chain_len.astype(F32), chain_time, chain_arch.astype(F32)], axis=0
    )
    near_chains = core_swap(held_chains)
    chains = jnp.where(core == mp_at, held_chains, near_chains)
    lengths = chains[0].astype(jnp.int32)
    times = chains[1]
    arches = chains[2].astype(jnp.int32)
    ends = jnp.cumsum(lengths)

    def ids_of(half):
        positions = jnp.arange(rows, dtype=jnp.int32) + half * rows
        return jnp.sum((positions[:, None] >= ends[None, :]).astype(jnp.int32), axis=1)

    own_ids = ids_of(core)
    key_ids = jnp.concatenate([own_ids, ids_of(1 - core)])
    membership = own_ids[:, None] == jnp.arange(slots, dtype=jnp.int32)[None, :]
    member_low = membership.astype(BF16)
    membership = membership.astype(F32)
    valid = (own_ids < slots).astype(F32)[:, None]

    half_cond = cond_width // 2
    frequency = jnp.exp(jnp.arange(half_cond, dtype=F32) * (-math.log(10000.0) / half_cond))
    angles = times[:, None] * 1000.0 * frequency[None, :]
    time_embed = jnp.concatenate([jnp.sin(angles), jnp.cos(angles)], axis=1).astype(BF16)
    arch_onehot = (
        arches[:, None] == jnp.arange(cath_table.shape[0], dtype=jnp.int32)[None, :]
    ).astype(F32)
    cond_pre = dot_f32(time_embed, time_weight) + highest_dot(arch_onehot, cath_table.astype(F32))
    cond_value, cond_slope = silu_parts(cond_pre)
    cond_act = cond_value.astype(BF16)
    chain_mod = dot_f32(cond_act, mod_weight) + mod_bias.astype(F32)[None, :]
    token_mod = highest_dot(membership, chain_mod)
    shift_a, scale_a, gate_a, shift_f, scale_f, gate_f = jnp.split(token_mod, 6, axis=1)

    layer_in = turn(tokens).astype(F32)
    pair_own = turn(jnp.concatenate([pair_left, pair_right], axis=1))
    left_own, right_own = jnp.split(pair_own, 2, axis=1)
    dout = turn(cotangent).astype(F32)

    def other_half(weight, axis):
        size = weight.shape[axis] // 2
        piece = lax.dynamic_slice_in_dim(weight, core * size, size, axis)
        mine = across(piece)
        near = core_swap(mine)
        return jnp.where(
            core == 0,
            jnp.concatenate([mine, near], axis=axis),
            jnp.concatenate([near, mine], axis=axis),
        )

    qkv_all = jnp.concatenate([qkv_weight, other_half(qkv_weight, 2)], axis=2)
    pair_mix = jnp.concatenate([pair_weight, across(pair_weight)], axis=1).astype(F32)
    out_all = jnp.concatenate([out_weight, other_half(out_weight, 0)], axis=0)
    gate_up_all = jnp.concatenate([gate_up_weight, other_half(gate_up_weight, 2)], axis=2)
    down_all = jnp.concatenate([down_weight, other_half(down_weight, 0)], axis=0)

    x_hat, x_inverse = apply_norm(layer_in)
    normed_a = (x_hat * (1.0 + scale_a) + shift_a).astype(BF16)
    projected = jnp.einsum("td,kdf->ktf", normed_a, qkv_all, preferred_element_type=F32).astype(
        BF16
    )
    sent = jnp.concatenate([projected[1], projected[2], right_own], axis=1)
    near = core_swap(sent)
    keys = jnp.concatenate([projected[1], near[:, :width]]).reshape(-1, heads, head_width)
    values = jnp.concatenate([projected[2], near[:, width : 2 * width]]).reshape(
        -1, heads, head_width
    )
    right_all = jnp.concatenate([right_own, near[:, 2 * width :]])
    queries = projected[0].reshape(rows, heads, head_width)
    pair_query = (
        left_own.astype(F32)[:, None, :] * jnp.transpose(pair_mix)[None, :, :]
    ).astype(BF16)
    scores = score_scale * jnp.einsum("qhd,khd->hqk", queries, keys, preferred_element_type=F32)
    scores = scores + jnp.einsum(
        "qhc,kc->hqk", pair_query, right_all, preferred_element_type=F32
    )
    allowed = own_ids[:, None] == key_ids[None, :]
    scores = jnp.where(allowed[None], scores, -1e30)
    exponent = jnp.exp(scores - jnp.max(scores, axis=-1, keepdims=True))
    probs = (exponent / jnp.sum(exponent, axis=-1, keepdims=True)).astype(BF16)
    attended = (
        jnp.einsum("hqk,khd->qhd", probs, values, preferred_element_type=F32)
        .astype(BF16)
        .reshape(rows, width)
    )
    attn_branch = dot_f32(attended, out_all)
    middle = layer_in + valid * gate_a * attn_branch

    m_hat, m_inverse = apply_norm(middle)
    normed_f = (m_hat * (1.0 + scale_f) + shift_f).astype(BF16)
    d_ffn = (valid * gate_f * dout).astype(BF16)
    gate_act = dot_f32(normed_f, gate_up_all[0])
    up_act = dot_f32(normed_f, gate_up_all[1])
    gate_value, gate_slope = silu_parts(gate_act)
    hidden = (gate_value * up_act).astype(BF16)
    ffn_branch = dot_f32(hidden, down_all)
    mixed = turn((middle + valid * gate_f * ffn_branch).astype(BF16))
    d_hidden = dot_nt(d_ffn, down_all)
    d_gate = (d_hidden * up_act * gate_slope).astype(BF16)
    d_up = (d_hidden * gate_value).astype(BF16)
    d_normed_f = dot_nt(d_gate, gate_up_all[0]) + dot_nt(d_up, gate_up_all[1])

    order = [int(format(p, "0%db" % bits)[::-1], 2) for p in range(dp_count)]
    block_at = jnp.array(order, jnp.int32) ^ dp_at

    def row_blocks(array):
        turned = jnp.transpose(array).reshape(dp_count, width // dp_count, rows)
        return jnp.take(turned, block_at, axis=0).reshape(width, rows)

    def reduce_grad(left_t, right_side, y_first):
        half = width // 2
        far = core_swap(dot_f32(left_t[half:], right_side).astype(BF16))
        total = (dot_f32(left_t[:half], right_side) + far.astype(F32)).astype(BF16)
        columns = right_side.shape[1] // 2

        def y_step(total):
            received = across(total[:, columns:])
            return (total[:, :columns].astype(F32) + received.astype(F32)).astype(BF16)

        if y_first:
            total = y_step(total)
        for bit in range(1, bits):
            half = total.shape[0] // 2
            received = flip(bit)(total[half:])
            total = (total[:half].astype(F32) + received.astype(F32)).astype(BF16)
        if not y_first:
            total = y_step(total)
        return total.astype(F32)

    def halves_first(arrays):
        cut = arrays[0].shape[1] // 2
        return jnp.concatenate([a[:, :cut] for a in arrays] + [a[:, cut:] for a in arrays], axis=1)

    gate_up_sum = reduce_grad(row_blocks(normed_f), halves_first([d_gate, d_up]), True)
    down_sum = reduce_grad(row_blocks(d_ffn), hidden, False)

    d_middle = dout + norm_backward(d_normed_f * (1.0 + scale_f), m_hat, m_inverse)
    d_attn = (valid * gate_a * d_middle).astype(BF16)
    d_attended = dot_nt(d_attn, out_all).astype(BF16).reshape(rows, heads, head_width)
    out_sum = reduce_grad(row_blocks(d_attn), attended, False)
    probs_wide = probs.astype(F32)
    d_probs = jnp.einsum("qhd,khd->hqk", d_attended, values, preferred_element_type=F32)
    row_dot = jnp.sum(probs_wide * d_probs, axis=-1, keepdims=True)
    d_scores = (probs_wide * (d_probs - row_dot)).astype(BF16)
    d_values = jnp.einsum("hqk,qhd->khd", probs, d_attended, preferred_element_type=F32)
    d_queries = score_scale * jnp.einsum(
        "hqk,khd->qhd", d_scores, keys, preferred_element_type=F32
    )
    d_keys = score_scale * jnp.einsum(
        "hqk,qhd->khd", d_scores, queries, preferred_element_type=F32
    )
    d_pair_query = jnp.einsum("hqk,kc->qhc", d_scores, right_all, preferred_element_type=F32)
    d_right = jnp.einsum("hqk,qhc->kc", d_scores, pair_query, preferred_element_type=F32)
    d_keyed = jnp.concatenate(
        [d_keys.reshape(-1, width), d_values.reshape(-1, width), d_right], axis=1
    )
    d_keyed = d_keyed[:rows] + core_swap(d_keyed[rows:].astype(BF16)).astype(F32)
    d_keyed = d_keyed.astype(BF16)
    d_proj = [
        d_queries.reshape(rows, width).astype(BF16),
        d_keyed[:, :width],
        d_keyed[:, width : 2 * width],
    ]
    d_left = jnp.sum(d_pair_query * jnp.transpose(pair_mix)[None], axis=1).astype(BF16)
    d_pair = turn(jnp.concatenate([d_left, d_keyed[:, 2 * width :]], axis=1))
    d_pair_weight = jnp.einsum(
        "thc,tc->ch", d_pair_query, left_own.astype(F32), precision=lax.Precision.HIGHEST
    )
    d_pair_weight = jnp.concatenate(
        [d_pair_weight[:, :half_heads], across(d_pair_weight[:, half_heads:])], axis=1
    )
    d_pair_weight = d_pair_weight[:, :half_heads] + d_pair_weight[:, half_heads:]
    pair_sum = lax.psum_scatter(d_pair_weight, "dp", scatter_dimension=0, tiled=True)
    d_normed_a = (
        dot_nt(d_proj[0], qkv_all[0]) + dot_nt(d_proj[1], qkv_all[1]) + dot_nt(d_proj[2], qkv_all[2])
    )
    qkv_sum = reduce_grad(row_blocks(normed_a), halves_first(d_proj), True)
    token_gradient = turn(
        (d_middle + norm_backward(d_normed_a * (1.0 + scale_a), x_hat, x_inverse)).astype(BF16)
    )

    d_token_mod = jnp.concatenate(
        [
            d_normed_a,
            d_normed_a * x_hat,
            valid * d_middle * attn_branch,
            d_normed_f,
            d_normed_f * m_hat,
            valid * dout * ffn_branch,
        ],
        axis=1,
    ).astype(BF16)
    d_chain_mod = dot_f32(jnp.transpose(member_low), d_token_mod)
    d_chain_mod = d_chain_mod + core_swap(d_chain_mod)
    arch_low = (
        arches[:, None] == jnp.arange(cath_table.shape[0], dtype=jnp.int32)[None, :]
    ).astype(BF16)
    gathered = jnp.concatenate(
        [d_chain_mod.astype(BF16), cond_act, time_embed, cond_slope.astype(BF16), arch_low], axis=1
    )
    gathered = jnp.concatenate([gathered, across(gathered)], axis=0)
    for bit in range(1, bits):
        gathered = jnp.concatenate([gathered, flip(bit)(gathered)], axis=0)
    modded = mod_weight.shape[1]
    cuts = [modded, modded + cond_width, modded + 2 * cond_width, modded + 3 * cond_width]
    d_all, cond_all, time_all, slope_all, arch_all = jnp.split(gathered, cuts, axis=1)
    mod_bias_sum = jnp.sum(d_all.astype(F32), axis=0)
    mod_weight_sum = dot_f32(jnp.transpose(cond_all), d_all)
    d_cond_pre = dot_nt(d_all, mod_weight) * slope_all.astype(F32)
    time_sum = highest_dot(jnp.transpose(time_all.astype(F32)), d_cond_pre)
    cath_sum = highest_dot(jnp.transpose(arch_all.astype(F32)), d_cond_pre)

    hidden_half = down_weight.shape[0]
    proj_half = qkv_weight.shape[2]
    return (
        mixed,
        token_gradient,
        d_pair[:, : pair_left.shape[1]],
        d_pair[:, pair_left.shape[1] :],
        cath_sum,
        time_sum,
        mod_weight_sum,
        mod_bias_sum,
        jnp.stack([qkv_sum[:, k * proj_half : (k + 1) * proj_half] for k in range(3)]),
        pair_sum,
        jnp.transpose(out_sum),
        jnp.stack([gate_up_sum[:, k * hidden_half : (k + 1) * hidden_half] for k in range(2)]),
        jnp.transpose(down_sum),
    )


def solution(mesh):
    by_rows = P(AXES, None)
    placed = (
        by_rows,
        by_rows,
        by_rows,
        P("dp", None),
        P("dp", None),
        P("dp", None),
        P(),
        P(),
        P(),
        P(),
        P(None, None, "mp"),
        P(None, "mp"),
        P("mp", None),
        P(None, None, "mp"),
        P("mp", None),
        by_rows,
    )
    return jax.shard_map(
        shards,
        mesh=mesh,
        in_specs=placed,
        out_specs=(
            by_rows,
            by_rows,
            by_rows,
            by_rows,
            P(),
            P(),
            P(),
            P(),
            P(None, "dp", "mp"),
            P("dp", "mp"),
            P("mp", "dp"),
            P(None, "dp", "mp"),
            P("mp", "dp"),
        ),
        check_vma=False,
    )
```

time: 1160 us -> 734 us (0.63)
  waiting for transfers between devices: 713 us -> 279 us
  starting transfers between devices: 0.96 us -> 71.8 us
  blocking collectives: 68.2 us -> 0 us
  other arithmetic: 65.4 us -> 82 us
    reduce_scatter x8 -> x0, waiting for transfers between devices: 261 us -> none  [the longest x1 79.7 us: reduce_ffn(): lax.psum_scatter(d_down, 'dp', scatter_dimension=1, tiled=True)]
    ppermute x0 -> x44, waiting for transfers between devices: none -> 228 us  [mover(): return lambda array: lax.ppermute(array, AXES, table)]
    unnamed x17 -> x2, waiting for transfers between devices: 218 us -> 51 us
    psum x1 -> x0, waiting for transfers between devices: 152 us -> none  [shards(): lax.psum((d_cath, d_time, d_mod_weight, d_mod_bias), ('dp', 'mp'))]
    all_gather x4 -> x0, waiting for transfers between devices: 81.5 us -> none  [the longest x1 27.3 us: shards(): d_attn_group = lax.all_gather(d_attn, 'mp', axis=0, tiled=True)]
    ppermute x0 -> x44, starting transfers between devices: none -> 71.8 us  [mover(): return lambda array: lax.ppermute(array, AXES, table)]
    psum x1 -> x0, blocking collectives: 44.9 us -> none  [shards(): lax.psum((d_cath, d_time, d_mod_weight, d_mod_bias), ('dp', 'mp'))]
    sub x0 -> x1, matrix products: none -> 23.3 us  [shards(): exponent = jnp.exp(scores - jnp.max(scores, axis=-1, keepdims=True))]
  transfers between devices with their start and end apart: 15 -> 45, of which waited for: 14 -> 19; matrix products, arithmetic and copies ran while one was open for 9% -> 31% of each run, Pallas kernels for 0% -> 0%
where the time goes in v1:
time: 734 us; the launch traced here: 722 us
  waiting for transfers between devices  279 us (38%)
  matrix products  197 us (27%)
  other arithmetic  82 us (11%)
  local copies, waits for them, and re-layouts  76.1 us (10%)
  starting transfers between devices  71.8 us (10%)
  between operations  16 us (2%)
    ppermute x44, waiting for transfers between devices, mover(): return lambda array: lax.ppermute(array, AXES, table)  228 us
    ppermute x44, starting transfers between devices, mover(): return lambda array: lax.ppermute(array, AXES, table)  71.8 us
    dot_general x16, matrix products, dot_f32(): return jnp.dot(left_side, right_side, preferred_element_type=F32)  63.1 us
    unnamed x2, waiting for transfers between devices  51 us
    unnamed x202, local copies, waits for them, and re-layouts  29.6 us
    dot_general x8, matrix products, dot_nt(): lax.dot_general(left_side, right_side, (((1,), (1,)), ((), ())), preferre...  23.5 us
    sub x1, matrix products, shards(): exponent = jnp.exp(scores - jnp.max(scores, axis=-1, keepdims=True))  23.3 us
    convert_element_type x1, other arithmetic, shards(): d_scores = (probs_wide * (d_probs - row_dot)).astype(BF16)  16.7 us
  transfers between devices with their start and end apart: 45, of which 19 were waited for; matrix products, arithmetic and copies ran while one was open for 31% of the time, Pallas kernels for 0%

profile of v1, /device:TPU:1, one launch (start us, length us, event | category | flops | bytes accessed | tf_op | source)
XLA Modules:
  0.0 722.3 jit_solution(13785022978267382245)
XLA Ops:
  12.4 4.5 collective-permute-start.4
  21.2 3.4 collective-permute-start.11
  24.6 3.8 copy.76
  30.8 3.3 constant_dynamic-slice_fusion.1
  36.9 3.9 fusion.76
  44.0 39.4 %collective-permute-done.2 = bf16[3,768,192]{1,2,0:T(8,128)(2,1)} collective-permute-done((bf16[3,768,192]{1,2,0:T(8,128)(2,1)}, bf16[3,768,192]{1,2,0:T(8,128)(2,1)}, u32[]{:S(2)}, u32[]{:S(2)}) %collective-permute-start.2) | collective-permute-done | bytes 884768 | tf_op jit(solution)/shard_map/ppermute | solution.py:58
  97.8 35.1 %collective-permute-done.7 = bf16[192,768]{1,0:T(8,128)(2,1)S(1)} collective-permute-done((bf16[192,768]{1,0:T(8,128)(2,1)S(1)}, bf16[192,768]{1,0:T(8,128)(2,1)S(1)}, u32[]{:S(2)}, u32[]{:S(2)}) %collective-permute-start.7) | collective-permute-done | bytes 294944 | tf_op jit(solution)/shard_map/ppermute | solution.py:58
  143.3 4.7 collective-permute-start.10
  148.0 3.8 maximum_select_fusion.1
  154.3 10.2 %fusion.56 = f32[12,512,1024]{2,1,0:T(8,128)} fusion(bf16[512,12,64]{0,2,1:T(8,128)(2,1)S(1)} %bitcast.165, bf16[512,12,64]{0,2,1:T(8,128)(2,1)S(1)} %bitcast.181, bf16[512,12,64]{0,2,1:T(8,128)(2,1)S(1)} %bitcast.178), kind=kOutput, calls=%fused_computation.133 | convolution fusion | flops 808452096 | bytes 27525120 | tf_op jit(solution)/shard_map/qhd,khd->hqk/dot_general | solution.py:175
  166.1 23.3 %fusion.132 = (f32[12,512]{1,0:T(8,128)S(1)}, f32[12,512,1024]{2,1,0:T(8,128)}) fusion(f32[12,512,1024]{2,1,0:T(8,128)} %fusion.56, pred[512,1024]{1,0:T(8,128)(4,1)} %broadcast_compare_fusion, f32[12,256]{1,0:T(8,128)S(1)} %convert_bitcast_fusion.3, f32[512,256]{0,1:T(8,128)} %get-tuple-element.81, bf16[512,256]{0,1:T(8,128)(2,1)} %slice.366, ...), kind=kOutput, calls=%fused_computation.299 | convolution fusion | flops 3256878080 | bytes 51941376 | tf_op jit(solution)/shard_map/sub | solution.py:181
  189.4 14.5 %divide_convert_fusion = bf16[12,512,1024]{2,1,0:T(8,128)(2,1)} fusion(f32[12,512,1024]{2,1,0:T(8,128)} %get-tuple-element.102, f32[12,512]{1,0:T(8,128)S(1)} %get-tuple-element.101), kind=kLoop, calls=%fused_computation.11 | loop fusion | flops 12582912 | bytes 37773312 | tf_op jit(solution)/shard_map/convert_element_type | solution.py:182
  204.0 8.6 %convolution_convert_fusion.4 = bf16[12,64,512]{2,1,0:T(8,128)(2,1)S(1)} fusion(bf16[12,512,1024]{2,1,0:T(8,128)(2,1)} %divide_convert_fusion, bf16[512,12,64]{0,2,1:T(8,128)(2,1)S(1)} %bitcast.183, bf16[512,12,64]{0,2,1:T(8,128)(2,1)S(1)} %bitcast.179), kind=kOutput, calls=%fused_computation.111 | convolution fusion | flops 808845312 | bytes 14942208 | tf_op jit(solution)/shard_map/hqk,khd->qhd/dot_general | solution.py:184
  212.6 4.6 fusion.122
  228.9 7.9 %fusion.17 = f32[512,3072]{1,0:T(8,128)} fusion(bf16[512,768]{1,0:T(8,128)(2,1)} %get-tuple-element.58, bf16[1536,768]{1,0:T(8,128)(2,1)} %maximum_select_fusion.1, bf16[1536,768]{1,0:T(8,128)(2,1)} %param.33), kind=kOutput, calls=%fused_computation.56 | convolution fusion | flops 2425356288 | bytes 11796480 | tf_op jit(solution)/shard_map/dot_general | solution.py:42
  236.7 4.8 maximum_select_fusion
  241.5 7.0 fusion.71
  248.5 9.9 %multiply_convert_fusion.1 = (bf16[512,3072]{1,0:T(8,128)(2,1)S(1)}, bf16[512,3072]{1,0:T(8,128)(2,1)S(1)}, bf16[512,3072]{1,0:T(8,128)(2,1)}) fusion(f32[512,3072]{1,0:T(8,128)} %fusion.17, f32[512,3072]{1,0:T(8,128)} %fusion.71, bf16[512,768]{1,0:T(8,128)(2,1)S(1)} %fusion.37, bf16[2,768,1536]{2,1,0:T(8,128)(2,1)S(1)} %bitcast.195, ...), kind=kOutput, calls=%fused_computation.23 | convolution fusion | flops 2448949248 | bytes 32243712 | tf_op jit(solution)/shard_map/dot_general | solution.py:38
  263.9 4.5 fusion.117
  268.5 8.9 %multiply_convert_fusion.9 = (bf16[512,768]{1,0:T(8,128)(2,1)S(1)}, f32[512,768]{1,0:T(8,128)}, bf16[512,768]{1,0:T(8,128)(2,1)}, f32[512,768]{1,0:T(8,128)}) fusion(f32[512,4608]{1,0:T(8,128)} %copy-done.2, f32[512]{0:T(512)S(1)} %compare_convert_fusion, f32[512]{0:T(512)S(1)} %get-tuple-element.113, f32[512,768]{1,0:T(8,128)S(1)} %copy-done.6, ...), kind=kOutput, calls=%fused_computation.104 | convolution fusion | flops 2432040960 | bytes 21243904 | tf_op jit(solution)/shard_map/dot_general | solution.py:38
  281.5 8.7 %fusion.133 = f32[12,64,1024]{2,1,0:T(8,128)} fusion(bf16[512,12,64]{0,2,1:T(8,128)(2,1)S(1)} %bitcast.172, bf16[12,512,1024]{2,1,0:T(8,128)(2,1)} %divide_convert_fusion), kind=kOutput, calls=%fused_computation.300 | convolution fusion | flops 805306368 | bytes 16515072 | tf_op jit(solution)/shard_map/hqk,qhd->khd/dot_general | solution.py:247
  290.1 12.9 %fusion.1 = (f32[12,512]{1,0:T(8,128)S(1)}, f32[12,512,1024]{2,1,0:T(8,128)}) fusion(bf16[12,512,1024]{2,1,0:T(8,128)(2,1)} %divide_convert_fusion, bf16[512,12,64]{0,2,1:T(8,128)(2,1)S(1)} %bitcast.173, bf16[512,12,64]{0,2,1:T(8,128)(2,1)S(1)} %bitcast.184, bf16[512,12,64]{0,2,1:T(8,128)(2,1)S(1)} %bitcast.180), kind=kOutput, calls=%fused_computation.7 | convolution fusion | flops 827320320 | bytes 40132608 | tf_op jit(solution)/shard_map/qhd,khd->hqk/dot_general | solution.py:244
  303.1 16.7 %fusion.2 = bf16[12,512,1024]{2,1,0:T(8,128)(2,1)S(1)} fusion(f32[12,512,1024]{2,1,0:T(8,128)} %get-tuple-element.107, f32[12,512]{1,0:T(8,128)S(1)} %get-tuple-element.106, f32[12,512,1024]{2,1,0:T(8,128)} %get-tuple-element.102, f32[12,512]{1,0:T(8,128)S(1)} %get-tuple-element.101), kind=kLoop, calls=%fused_computation.8 | loop fusion | flops 37748736 | bytes 62963712 | tf_op jit(solution)/shard_map/convert_element_type | solution.py:246
  319.8 4.9 fusion.40
  324.7 4.0 convolution_multiply_fusion
  328.7 11.5 %multiply_reduce_fusion = (bf16[512,256]{0,1:T(8,128)(2,1)}, f32[512,12,256]{0,2,1:T(8,128)}) fusion(f32[12,256]{1,0:T(8,128)S(1)} %convert_bitcast_fusion.3, bf16[12,512,1024]{2,1,0:T(8,128)(2,1)} %copy-done.1, bf16[512,256]{0,1:T(8,128)(2,1)S(1)} %copy-done.60, bf16[512,256]{0,1:T(8,128)(2,1)S(1)} %get-tuple-element.82), kind=kOutput, calls=%fused_computation.21 | convolution fusion | flops 3225288704 | bytes 19673088 | tf_op jit(solution)/shard_map/hqk,kc->qhc/dot_general | solution.py:254
  357.2 5.1 collective-permute-start.39
  362.4 6.0 convolution_convert_fusion
  374.7 10.3 %multiply_convert_fusion.8 = bf16[12,64,512]{2,1,0:T(8,128)(2,1)} fusion(bf16[12,512,1024]{2,1,0:T(8,128)(2,1)} %copy-done.1, bf16[512,12,64]{0,2,1:T(8,128)(2,1)} %bitcast.182, bf16[512,12,64]{0,2,1:T(8,128)(2,1)} %bitcast.177), kind=kOutput, calls=%fused_computation.103 | convolution fusion | flops 809238528 | bytes 14942208 | tf_op jit(solution)/shard_map/hqk,khd->qhd/dot_general | solution.py:248
  389.2 8.1 %fusion.4 = f32[256,1,12]{2,1,0:T(1,128)S(1)} fusion(f32[512,12,256]{0,2,1:T(8,128)S(1)} %bitcast.171, bf16[512,256,1]{0,1,2:T(8,128)(2,1)S(1)} %copy-done.37), kind=kOutput, calls=%fused_computation.17 | convolution fusion | flops 18874368 | bytes 6565888 | tf_op jit(solution)/shard_map/thc,tc->ch/dot_general | solution.py:268
  411.9 51.0 %reduce-scatter.4.cloned.1.call-done = f32[16,6]{1,0:T(8,128)} async-done(((f32[256,6]{1,0:T(8,128)}), f32[16,6]{1,0:T(8,128)}) %reduce-scatter.4.cloned.1.call-update) | async-done | bytes 400
  464.9 3.4 fusion.11
  472.0 5.6 collective-permute-start.17
  492.7 3.2 collective-permute-start.18
  513.9 3.1 add_convert_fusion.1
  518.2 4.4 collective-permute-done.21
  528.3 29.3 %collective-permute-done.22 = bf16[64,5419]{1,0:T(8,128)(2,1)} collective-permute-done((bf16[64,5419]{1,0:T(8,128)(2,1)}, bf16[64,5419]{1,0:T(8,128)(2,1)}, u32[]{:S(2)}, u32[]{:S(2)}) %collective-permute-start.22) | collective-permute-done | bytes 693664 | tf_op jit(solution)/shard_map/ppermute | solution.py:58
  562.0 3.2 fusion.58
  566.5 8.2 %add_convert_fusion = bf16[384,6144]{1,0:T(8,128)(2,1)S(1)} fusion(bf16[384,6144]{1,0:T(8,128)(2,1)} %collective-permute-done.34, bf16[384,512]{1,0:T(8,128)(2,1)S(1)} %bitcast.197, bf16[512,1536]{1,0:T(8,128)(2,1)S(1)} %copy-done.45, bf16[512,1536]{1,0:T(8,128)(2,1)S(1)} %copy-done.43, bf16[512,1536]{1,0:T(8,128)(2,1)S(1)} %copy-done.47, ...), kind=kOutput, calls=%fused_computation.15 | convolution fusion | flops 2448162816 | bytes 16121856 | tf_op jit(solution)/shard_map/dot_general | solution.py:38
  583.0 8.5 %collective-permute-done.41 = bf16[96,3072]{1,0:T(8,128)(2,1)S(1)} collective-permute-done((bf16[96,3072]{1,0:T(8,128)(2,1)S(1)}, bf16[96,3072]{1,0:T(8,128)(2,1)S(1)}, u32[]{:S(2)}, u32[]{:S(2)}) %collective-permute-start.41) | collective-permute-done | bytes 589856 | tf_op jit(solution)/shard_map/ppermute | solution.py:58
  592.2 53.0 %collective-permute-done.24 = bf16[384,1152]{1,0:T(8,128)(2,1)S(1)} collective-permute-done((bf16[384,1152]{1,0:T(8,128)(2,1)S(1)}, bf16[384,1152]{1,0:T(8,128)(2,1)S(1)}, u32[]{:S(2)}, u32[]{:S(2)}) %collective-permute-start.24) | collective-permute-done | bytes 884768 | tf_op jit(solution)/shard_map/ppermute | solution.py:58
  648.0 6.7 collective-permute-done.25
  657.0 3.1 collective-permute-done.26
  660.2 3.2 collective-permute-start.27
  663.4 16.7 %collective-permute-done.36 = bf16[192,3072]{1,0:T(8,128)(2,1)S(1)} collective-permute-done((bf16[192,3072]{1,0:T(8,128)(2,1)S(1)}, bf16[192,3072]{1,0:T(8,128)(2,1)S(1)}, u32[]{:S(2)}, u32[]{:S(2)}) %collective-permute-start.36) | collective-permute-done | bytes 1179680 | tf_op jit(solution)/shard_map/ppermute | solution.py:58
  682.9 9.8 %collective-permute-done.37 = bf16[96,3072]{1,0:T(8,128)(2,1)S(1)} collective-permute-done((bf16[96,3072]{1,0:T(8,128)(2,1)S(1)}, bf16[96,3072]{1,0:T(8,128)(2,1)S(1)}, u32[]{:S(2)}, u32[]{:S(2)}) %collective-permute-start.37) | collective-permute-done | bytes 589856 | tf_op jit(solution)/shard_map/ppermute | solution.py:58
  692.9 4.2 collective-permute-start.38
  697.8 12.1 %collective-permute-done.38 = bf16[48,3072]{1,0:T(8,128)(2,1)S(1)} collective-permute-done((bf16[48,3072]{1,0:T(8,128)(2,1)S(1)}, bf16[48,3072]{1,0:T(8,128)(2,1)S(1)}, u32[]{:S(2)}, u32[]{:S(2)}) %collective-permute-start.38) | collective-permute-done | bytes 294944 | tf_op jit(solution)/shard_map/ppermute | solution.py:58
  (414 shorter events, 183.2 us)
Async XLA Ops:
  7.2 455.7 %reduce-scatter.4.cloned.1.call-start = ((), (), s32[]{:S(2)}) async-start(), calls=%async_computation.1 | async-start | bytes 139264
  9.4 24.7 %collective-permute-start.1 = (f32[3,8]{1,0:T(4,128)S(1)}, f32[3,8]{1,0:T(4,128)S(1)}, u32[]{:S(2)}, u32[]{:S(2)}) collective-permute-start(f32[3,8]{1,0:T(4,128)S(1)} %pad_maximum_fusion.31), channel_id=1, source_target_pairs={{0,2},{1,3},{2,0},{3,1},{4,6},{5,7},{6,4},{7,5},{8,10},{9,11},{10,... | collective-permute-start | bytes 296 | tf_op jit(solution)/shard_map/ppermute | solution.py:58
  12.4 28.4 %collective-permute-start.4 = (bf16[512,512]{0,1:T(8,128)(2,1)}, bf16[512,512]{0,1:T(8,128)(2,1)}, u32[]{:S(2)}, u32[]{:S(2)}) collective-permute-start(bf16[512,512]{0,1:T(8,128)(2,1)} %pad_maximum_fusion.26), channel_id=1, source_target_pairs={{0,0},{1,2},{2,1},{3,3},{4,4},{5,6},{6,5},{7,7},{8,8},{9,10},{10,9... | collective-permute-start | bytes 1572872 | tf_op jit(solution)/shard_map/ppermute | solution.py:58
  16.9 26.8 %collective-permute-start = (bf16[512,768]{1,0:T(8,128)(2,1)}, bf16[512,768]{1,0:T(8,128)(2,1)S(1)}, u32[]{:S(2)}, u32[]{:S(2)}) collective-permute-start(bf16[512,768]{1,0:T(8,128)(2,1)} %param.19), channel_id=1, source_target_pairs={{0,0},{1,2},{2,1},{3,3},{4,4},{5,6},{6,5},{7,7},{8,8},{9,10},{10,9... | collective-permute-start | bytes 2359304 | tf_op jit(solution)/shard_map/ppermute | solution.py:58
  21.2 74.1 %collective-permute-start.11 = (bf16[768,768]{1,0:T(8,128)(2,1)}, bf16[768,768]{1,0:T(8,128)(2,1)}, u32[]{:S(2)}, u32[]{:S(2)}) collective-permute-start(bf16[768,768]{1,0:T(8,128)(2,1)} %constant_dynamic-slice_fusion), channel_id=1, source_target_pairs={{0,1},{1,0},{2,3},{3,2},{4,5},{5,4},{6,7},{7,6},{8,9},{9,8},{10,11... | collective-permute-start | bytes 3538952 | tf_op jit(solution)/shard_map/ppermute | solution.py:58
  30.7 52.7 %collective-permute-start.2 = (bf16[3,768,192]{1,2,0:T(8,128)(2,1)}, bf16[3,768,192]{1,2,0:T(8,128)(2,1)}, u32[]{:S(2)}, u32[]{:S(2)}) collective-permute-start(bf16[3,768,192]{1,2,0:T(8,128)(2,1)} %constant_dynamic-slice_fusion.3), channel_id=1, source_target_pairs={{0,1},{1,0},{2,3},{3,2},{4,5},{5,4},{6,7},{7,6},{8,9},{9,8},{10,11... | collective-permute-start | bytes 2654216 | tf_op jit(solution)/shard_map/ppermute | solution.py:58
  34.1 109.2 %collective-permute-start.9 = (bf16[2,768,768]{2,1,0:T(8,128)(2,1)}, bf16[2,768,768]{2,1,0:T(8,128)(2,1)}, u32[]{:S(2)}, u32[]{:S(2)}) collective-permute-start(bf16[2,768,768]{2,1,0:T(8,128)(2,1)} %constant_dynamic-slice_fusion.1), channel_id=1, source_target_pairs={{0,1},{1,0},{2,3},{3,2},{4,5},{5,4},{6,7},{7,6},{8,9},{9,8},{10,11... | collective-permute-start | bytes 7077896 | tf_op jit(solution)/shard_map/ppermute | solution.py:58
  36.9 97.4 %copy-start.62 = (s32[512]{0:T(512)}, s32[512]{0:T(512)S(1)}, u32[]{:S(2)}) copy-start(s32[512]{0:T(512)S(1)} %get-tuple-element.45) | copy-start | bytes 6148
  40.8 43.6 %copy-start.2 = (f32[512,4608]{1,0:T(8,128)}, f32[512,4608]{1,0:T(8,128)S(1)}, u32[]{:S(2)}) copy-start(f32[512,4608]{1,0:T(8,128)S(1)} %fusion.76) | copy-start | bytes 28311556
  43.8 168.8 %copy-start.3 = (bf16[512,768]{1,0:T(8,128)(2,1)}, bf16[512,768]{1,0:T(8,128)(2,1)S(1)}, u32[]{:S(2)}) copy-start(bf16[512,768]{1,0:T(8,128)(2,1)S(1)} %collective-permute-done) | copy-start | bytes 2359300
  83.4 2.9 collective-permute-start.3
  93.3 58.5 %collective-permute-start.5 = (bf16[512,1792]{0,1:T(8,128)(2,1)}, bf16[512,1792]{0,1:T(8,128)(2,1)}, u32[]{:S(2)}, u32[]{:S(2)}) collective-permute-start(bf16[512,1792]{0,1:T(8,128)(2,1)} %pad_maximum_fusion.10), channel_id=1, source_target_pairs={{0,2},{1,3},{2,0},{3,1},{4,6},{5,7},{6,4},{7,5},{8,10},{9,11},{10,... | collective-permute-start | bytes 5505032 | tf_op jit(solution)/shard_map/ppermute | solution.py:58
  93.6 40.7 %collective-permute-start.6 = (bf16[256,6]{0,1:T(8,128)(2,1)S(1)}, bf16[256,6]{0,1:T(8,128)(2,1)S(1)}, u32[]{:S(2)}, u32[]{:S(2)}) collective-permute-start(bf16[256,6]{0,1:T(8,128)(2,1)S(1)} %copy-done.79), channel_id=1, source_target_pairs={{0,1},{1,0},{2,3},{3,2},{4,5},{5,4},{6,7},{7,6},{8,9},{9,8},{10,11... | collective-permute-start | bytes 9224 | tf_op jit(solution)/shard_map/ppermute | solution.py:58
  95.3 52.6 %collective-permute-start.12 = (bf16[768,768]{1,0:T(8,128)(2,1)}, bf16[768,768]{1,0:T(8,128)(2,1)}, u32[]{:S(2)}, u32[]{:S(2)}) collective-permute-start(bf16[768,768]{1,0:T(8,128)(2,1)} %collective-permute-done.11), channel_id=1, source_target_pairs={{0,2},{1,3},{2,0},{3,1},{4,6},{5,7},{6,4},{7,5},{8,10},{9,11},{10,... | collective-permute-start | bytes 3538952 | tf_op jit(solution)/shard_map/ppermute | solution.py:58
  96.0 36.9 %collective-permute-start.7 = (bf16[192,768]{1,0:T(8,128)(2,1)S(1)}, bf16[192,768]{1,0:T(8,128)(2,1)S(1)}, u32[]{:S(2)}, u32[]{:S(2)}) collective-permute-start(bf16[192,768]{1,0:T(8,128)(2,1)S(1)} %constant_dynamic-slice_fusion.2), channel_id=1, source_target_pairs={{0,1},{1,0},{2,3},{3,2},{4,5},{5,4},{6,7},{7,6},{8,9},{9,8},{10,11... | collective-permute-start | bytes 884744 | tf_op jit(solution)/shard_map/ppermute | solution.py:58
  132.9 4.5 collective-permute-start.8
  134.3 78.3 %collective-permute-start.14 = (bf16[512,768]{1,0:T(8,128)(2,1)}, bf16[512,768]{1,0:T(8,128)(2,1)}, u32[]{:S(2)}, u32[]{:S(2)}) collective-permute-start(bf16[512,768]{1,0:T(8,128)(2,1)} %param.34), channel_id=1, source_target_pairs={{0,0},{1,2},{2,1},{3,3},{4,4},{5,6},{6,5},{7,7},{8,8},{9,10},{10,9... | collective-permute-start | bytes 2359304 | tf_op jit(solution)/shard_map/ppermute | solution.py:58
  143.3 93.4 %collective-permute-start.10 = (bf16[2,768,768]{2,1,0:T(8,128)(2,1)}, bf16[2,768,768]{2,1,0:T(8,128)(2,1)}, u32[]{:S(2)}, u32[]{:S(2)}) collective-permute-start(bf16[2,768,768]{2,1,0:T(8,128)(2,1)} %collective-permute-done.9), channel_id=1, source_target_pairs={{0,2},{1,3},{2,0},{3,1},{4,6},{5,7},{6,4},{7,5},{8,10},{9,11},{10,... | collective-permute-start | bytes 7077896 | tf_op jit(solution)/shard_map/ppermute | solution.py:58
  350.7 34.3 %collective-permute-start.29 = (bf16[384,768]{1,0:T(8,128)(2,1)}, bf16[384,768]{1,0:T(8,128)(2,1)}, u32[]{:S(2)}, u32[]{:S(2)}) collective-permute-start(bf16[384,768]{1,0:T(8,128)(2,1)} %convolution_convert_fusion.5), channel_id=1, source_target_pairs={{0,2},{1,3},{2,0},{3,1},{4,6},{5,7},{6,4},{7,5},{8,10},{9,11},{10,... | collective-permute-start | bytes 1769480 | tf_op jit(solution)/shard_map/ppermute | solution.py:58
  351.5 112.7 %collective-permute-start.13 = (bf16[512,768]{1,0:T(8,128)(2,1)}, bf16[512,768]{1,0:T(8,128)(2,1)}, u32[]{:S(2)}, u32[]{:S(2)}) collective-permute-start(bf16[512,768]{1,0:T(8,128)(2,1)} %get-tuple-element.57), channel_id=1, source_target_pairs={{0,0},{1,2},{2,1},{3,3},{4,4},{5,6},{6,5},{7,7},{8,8},{9,10},{10,9... | collective-permute-start | bytes 2359304 | tf_op jit(solution)/shard_map/ppermute | solution.py:58
  357.2 155.4 %collective-permute-start.39 = (bf16[384,3072]{1,0:T(8,128)(2,1)}, bf16[384,3072]{1,0:T(8,128)(2,1)}, u32[]{:S(2)}, u32[]{:S(2)}) collective-permute-start(bf16[384,3072]{1,0:T(8,128)(2,1)} %convolution_convert_fusion.1), channel_id=1, source_target_pairs={{0,2},{1,3},{2,0},{3,1},{4,6},{5,7},{6,4},{7,5},{8,10},{9,11},{10,... | collective-permute-start | bytes 7077896 | tf_op jit(solution)/shard_map/ppermute | solution.py:58
  368.4 197.8 %collective-permute-start.34 = (bf16[384,6144]{1,0:T(8,128)(2,1)}, bf16[384,6144]{1,0:T(8,128)(2,1)}, u32[]{:S(2)}, u32[]{:S(2)}) collective-permute-start(bf16[384,6144]{1,0:T(8,128)(2,1)} %convolution_convert_fusion), channel_id=1, source_target_pairs={{0,2},{1,3},{2,0},{3,1},{4,6},{5,7},{6,4},{7,5},{8,10},{9,11},{10,... | collective-permute-start | bytes 14155784 | tf_op jit(solution)/shard_map/ppermute | solution.py:58
  374.6 90.2 %collective-permute-start.15 = (bf16[512,1792]{0,1:T(8,128)(2,1)}, bf16[512,1792]{0,1:T(8,128)(2,1)}, u32[]{:S(2)}, u32[]{:S(2)}) collective-permute-start(bf16[512,1792]{0,1:T(8,128)(2,1)} %slice.524), channel_id=1, source_target_pairs={{0,2},{1,3},{2,0},{3,1},{4,6},{5,7},{6,4},{7,5},{8,10},{9,11},{10,... | collective-permute-start | bytes 5505032 | tf_op jit(solution)/shard_map/ppermute | solution.py:58
  387.4 10.1 %collective-permute-start.30 = (bf16[192,768]{1,0:T(8,128)(2,1)}, bf16[192,768]{1,0:T(8,128)(2,1)}, u32[]{:S(2)}, u32[]{:S(2)}) collective-permute-start(bf16[192,768]{1,0:T(8,128)(2,1)} %slice.406), channel_id=1, source_target_pairs={{0,4},{1,5},{2,6},{3,7},{4,0},{5,1},{6,2},{7,3},{8,12},{9,13},{10,... | collective-permute-start | bytes 884744 | tf_op jit(solution)/shard_map/ppermute | solution.py:58
  398.7 4.6 collective-permute-start.31
  403.2 2.5 collective-permute-start.28
  405.7 4.1 collective-permute-start.32
  409.9 54.3 %collective-permute-start.33 = (bf16[48,384]{1,0:T(8,128)(2,1)S(1)}, bf16[48,384]{1,0:T(8,128)(2,1)S(1)}, u32[]{:S(2)}, u32[]{:S(2)}) collective-permute-start(bf16[48,384]{1,0:T(8,128)(2,1)S(1)} %slice.412), channel_id=1, source_target_pairs={{0,1},{1,0},{2,3},{3,2},{4,5},{5,4},{6,7},{7,6},{8,9},{9,8},{10,11... | collective-permute-start | bytes 110600 | tf_op jit(solution)/shard_map/ppermute | solution.py:58
  472.0 52.6 %collective-permute-start.17 = (bf16[512,512]{0,1:T(8,128)(2,1)S(1)}, bf16[512,512]{0,1:T(8,128)(2,1)S(1)}, u32[]{:S(2)}, u32[]{:S(2)}) collective-permute-start(bf16[512,512]{0,1:T(8,128)(2,1)S(1)} %pad_maximum_fusion.27), channel_id=1, source_target_pairs={{0,0},{1,2},{2,1},{3,3},{4,4},{5,6},{6,5},{7,7},{8,8},{9,10},{10,9... | collective-permute-start | bytes 1572872 | tf_op jit(solution)/shard_map/ppermute | solution.py:58
  484.8 43.5 %collective-permute-start.16 = (bf16[512,768]{1,0:T(8,128)(2,1)}, bf16[512,768]{1,0:T(8,128)(2,1)}, u32[]{:S(2)}, u32[]{:S(2)}) collective-permute-start(bf16[512,768]{1,0:T(8,128)(2,1)} %fusion.31), channel_id=1, source_target_pairs={{0,0},{1,2},{2,1},{3,3},{4,4},{5,6},{6,5},{7,7},{8,8},{9,10},{10,9... | collective-permute-start | bytes 2359304 | tf_op jit(solution)/shard_map/ppermute | solution.py:58
  492.7 4.2 collective-permute-start.18
  501.2 3.8 collective-permute-start.19
  505.0 4.8 collective-permute-start.20
  509.8 69.2 %collective-permute-start.23 = (bf16[384,2304]{1,0:T(8,128)(2,1)}, bf16[384,2304]{1,0:T(8,128)(2,1)}, u32[]{:S(2)}, u32[]{:S(2)}) collective-permute-start(bf16[384,2304]{1,0:T(8,128)(2,1)} %convolution_convert_fusion.2), channel_id=1, source_target_pairs={{0,2},{1,3},{2,0},{3,1},{4,6},{5,7},{6,4},{7,5},{8,10},{9,11},{10,... | collective-permute-start | bytes 5308424 | tf_op jit(solution)/shard_map/ppermute | solution.py:58
  512.7 9.9 %collective-permute-start.21 = (bf16[32,5419]{1,0:T(8,128)(2,1)S(1)}, bf16[32,5419]{1,0:T(8,128)(2,1)S(1)}, u32[]{:S(2)}, u32[]{:S(2)}) collective-permute-start(bf16[32,5419]{1,0:T(8,128)(2,1)S(1)} %pad_maximum_fusion.28), channel_id=1, source_target_pairs={{0,8},{1,9},{2,10},{3,11},{4,12},{5,13},{6,14},{7,15},{8,0},{9,1},... | collective-permute-start | bytes 1040456 | tf_op jit(solution)/shard_map/ppermute | solution.py:58
  522.6 52.7 %collective-permute-start.40 = (bf16[192,3072]{1,0:T(8,128)(2,1)}, bf16[192,3072]{1,0:T(8,128)(2,1)}, u32[]{:S(2)}, u32[]{:S(2)}) collective-permute-start(bf16[192,3072]{1,0:T(8,128)(2,1)} %slice.432), channel_id=1, source_target_pairs={{0,4},{1,5},{2,6},{3,7},{4,0},{5,1},{6,2},{7,3},{8,12},{9,13},{10,... | collective-permute-start | bytes 3538952 | tf_op jit(solution)/shard_map/ppermute | solution.py:58
  524.6 33.0 %collective-permute-start.22 = (bf16[64,5419]{1,0:T(8,128)(2,1)}, bf16[64,5419]{1,0:T(8,128)(2,1)}, u32[]{:S(2)}, u32[]{:S(2)}) collective-permute-start(bf16[64,5419]{1,0:T(8,128)(2,1)} %pad_maximum_fusion.24), channel_id=1, source_target_pairs={{0,16},{1,17},{2,18},{3,19},{4,20},{5,21},{6,22},{7,23},{8,24},{9,... | collective-permute-start | bytes 2080904 | tf_op jit(solution)/shard_map/ppermute | solution.py:58
  574.9 71.2 %collective-permute-start.35 = (bf16[384,3072]{1,0:T(8,128)(2,1)S(1)}, bf16[384,3072]{1,0:T(8,128)(2,1)S(1)}, u32[]{:S(2)}, u32[]{:S(2)}) collective-permute-start(bf16[384,3072]{1,0:T(8,128)(2,1)S(1)} %slice.420), channel_id=1, source_target_pairs={{0,1},{1,0},{2,3},{3,2},{4,5},{5,4},{6,7},{7,6},{8,9},{9,8},{10,11... | collective-permute-start | bytes 7077896 | tf_op jit(solution)/shard_map/ppermute | solution.py:58
  578.1 13.4 %collective-permute-start.41 = (bf16[96,3072]{1,0:T(8,128)(2,1)S(1)}, bf16[96,3072]{1,0:T(8,128)(2,1)S(1)}, u32[]{:S(2)}, u32[]{:S(2)}) collective-permute-start(bf16[96,3072]{1,0:T(8,128)(2,1)S(1)} %slice.434), channel_id=1, source_target_pairs={{0,8},{1,9},{2,10},{3,11},{4,12},{5,13},{6,14},{7,15},{8,0},{9,1},... | collective-permute-start | bytes 1769480 | tf_op jit(solution)/shard_map/ppermute | solution.py:58
  581.8 63.4 %collective-permute-start.24 = (bf16[384,1152]{1,0:T(8,128)(2,1)S(1)}, bf16[384,1152]{1,0:T(8,128)(2,1)S(1)}, u32[]{:S(2)}, u32[]{:S(2)}) collective-permute-start(bf16[384,1152]{1,0:T(8,128)(2,1)S(1)} %slice.391), channel_id=1, source_target_pairs={{0,1},{1,0},{2,3},{3,2},{4,5},{5,4},{6,7},{7,6},{8,9},{9,8},{10,11... | collective-permute-start | bytes 2654216 | tf_op jit(solution)/shard_map/ppermute | solution.py:58
  591.7 64.8 %collective-permute-start.42 = (bf16[48,3072]{1,0:T(8,128)(2,1)S(1)}, bf16[48,3072]{1,0:T(8,128)(2,1)S(1)}, u32[]{:S(2)}, u32[]{:S(2)}) collective-permute-start(bf16[48,3072]{1,0:T(8,128)(2,1)S(1)} %slice.436), channel_id=1, source_target_pairs={{0,16},{1,17},{2,18},{3,19},{4,20},{5,21},{6,22},{7,23},{8,24},{9,... | collective-permute-start | bytes 884744 | tf_op jit(solution)/shard_map/ppermute | solution.py:58
  645.5 9.3 %collective-permute-start.25 = (bf16[192,1152]{1,0:T(8,128)(2,1)S(1)}, bf16[192,1152]{1,0:T(8,128)(2,1)S(1)}, u32[]{:S(2)}, u32[]{:S(2)}) collective-permute-start(bf16[192,1152]{1,0:T(8,128)(2,1)S(1)} %slice.393), channel_id=1, source_target_pairs={{0,4},{1,5},{2,6},{3,7},{4,0},{5,1},{6,2},{7,3},{8,12},{9,13},{10,... | collective-permute-start | bytes 1327112 | tf_op jit(solution)/shard_map/ppermute | solution.py:58
  647.1 33.0 %collective-permute-start.36 = (bf16[192,3072]{1,0:T(8,128)(2,1)S(1)}, bf16[192,3072]{1,0:T(8,128)(2,1)S(1)}, u32[]{:S(2)}, u32[]{:S(2)}) collective-permute-start(bf16[192,3072]{1,0:T(8,128)(2,1)S(1)} %slice.422), channel_id=1, source_target_pairs={{0,4},{1,5},{2,6},{3,7},{4,0},{5,1},{6,2},{7,3},{8,12},{9,13},{10,... | collective-permute-start | bytes 3538952 | tf_op jit(solution)/shard_map/ppermute | solution.py:58
  654.9 5.2 collective-permute-start.26
  656.6 25.5 %collective-permute-start.43 = (bf16[48,1536]{1,0:T(8,128)(2,1)S(1)}, bf16[48,1536]{1,0:T(8,128)(2,1)S(1)}, u32[]{:S(2)}, u32[]{:S(2)}) collective-permute-start(bf16[48,1536]{1,0:T(8,128)(2,1)S(1)} %slice.438), channel_id=1, source_target_pairs={{0,1},{1,0},{2,3},{3,2},{4,5},{5,4},{6,7},{7,6},{8,9},{9,8},{10,11... | collective-permute-start | bytes 442376 | tf_op jit(solution)/shard_map/ppermute | solution.py:58
  660.2 22.7 %collective-permute-start.27 = (bf16[48,1152]{1,0:T(8,128)(2,1)S(1)}, bf16[48,1152]{1,0:T(8,128)(2,1)S(1)}, u32[]{:S(2)}, u32[]{:S(2)}) collective-permute-start(bf16[48,1152]{1,0:T(8,128)(2,1)S(1)} %slice.397), channel_id=1, source_target_pairs={{0,16},{1,17},{2,18},{3,19},{4,20},{5,21},{6,22},{7,23},{8,24},{9,... | collective-permute-start | bytes 331784 | tf_op jit(solution)/shard_map/ppermute | solution.py:58
  680.5 12.2 %collective-permute-start.37 = (bf16[96,3072]{1,0:T(8,128)(2,1)S(1)}, bf16[96,3072]{1,0:T(8,128)(2,1)S(1)}, u32[]{:S(2)}, u32[]{:S(2)}) collective-permute-start(bf16[96,3072]{1,0:T(8,128)(2,1)S(1)} %slice.424), channel_id=1, source_target_pairs={{0,8},{1,9},{2,10},{3,11},{4,12},{5,13},{6,14},{7,15},{8,0},{9,1},... | collective-permute-start | bytes 1769480 | tf_op jit(solution)/shard_map/ppermute | solution.py:58
  692.9 17.0 %collective-permute-start.38 = (bf16[48,3072]{1,0:T(8,128)(2,1)S(1)}, bf16[48,3072]{1,0:T(8,128)(2,1)S(1)}, u32[]{:S(2)}, u32[]{:S(2)}) collective-permute-start(bf16[48,3072]{1,0:T(8,128)(2,1)S(1)} %slice.426), channel_id=1, source_target_pairs={{0,16},{1,17},{2,18},{3,19},{4,20},{5,21},{6,22},{7,23},{8,24},{9,... | collective-permute-start | bytes 884744 | tf_op jit(solution)/shard_map/ppermute | solution.py:58
  (89 other events, 538.6 us)
Sparse Core Ops, SparseCore 0:
  409.2 53.6 reduce-scatter.3

commit v2 on v1

--- a/solution.py
+++ b/solution.py
@@ -3,12 +3,15 @@
 import jax
 import jax.numpy as jnp
 from jax import lax
+from jax.experimental import pallas as pl
+from jax.experimental.pallas import tpu as pltpu
 from jax.sharding import PartitionSpec as P
 
 EPSILON = 1e-06
 AXES = ("dp", "mp")
 BF16 = jnp.bfloat16
 F32 = jnp.float32
+VMEM_LIMIT = 48 * 1024 * 1024
 
 
 def apply_norm(values):
@@ -41,6 +44,251 @@
 def dot_nt(left_side, right_side):
     return lax.dot_general(
         left_side, right_side, (((1,), (1,)), ((), ())), preferred_element_type=F32
+    )
+
+def lane_mix(first, second, odd):
+    lane = lax.broadcasted_iota(jnp.int32, first.shape, 1)
+    keep = (lane >= 64) if odd else (lane < 64)
+    return jnp.where(keep, first, second)
+
+
+def nt(left_side, right_side):
+    return lax.dot_general(
+        left_side, right_side, (((1,), (1,)), ((), ())), preferred_element_type=F32
+    )
+
+
+def attention_forward_body(
+    pair_mix_ref, q_ref, left_ref, hot_ref, k_own_ref, k_near_ref, v_own_ref, v_near_ref,
+    right_own_ref, right_near_ref, pen_own_ref, pen_near_ref,
+    attended_ref, inverse_ref, probs_ref,
+):
+    rows = q_ref.shape[0]
+    step = 256
+    out_tiles = []
+    left = left_ref[...].astype(F32)
+    for odd in range(2):
+        mix = pair_mix_ref[0, odd : odd + 1, :]
+        left_mixed = (left * mix).astype(BF16)
+        q_side = jnp.concatenate([left_mixed, lane_mix(q_ref[...], hot_ref[...], odd)], axis=1)
+        k_own = jnp.concatenate(
+            [right_own_ref[...], lane_mix(k_own_ref[...], pen_own_ref[...], odd)], axis=1
+        )
+        k_near = jnp.concatenate(
+            [right_near_ref[...], lane_mix(k_near_ref[...], pen_near_ref[...], odd)], axis=1
+        )
+        v_own = lane_mix(v_own_ref[...], jnp.ones_like(v_own_ref[...]), odd)
+        v_near = lane_mix(v_near_ref[...], jnp.ones_like(v_near_ref[...]), odd)
+        tiles = []
+        for start in range(0, rows, step):
+            block = q_side[start : start + step]
+            s_own = nt(block, k_own)
+            s_near = nt(block, k_near)
+            top = jnp.maximum(
+                jnp.max(s_own, axis=1, keepdims=True), jnp.max(s_near, axis=1, keepdims=True)
+            )
+            e_own = jnp.exp(s_own - top).astype(BF16)
+            e_near = jnp.exp(s_near - top).astype(BF16)
+            probs_ref[odd, start : start + step, :rows] = e_own
+            probs_ref[odd, start : start + step, rows:] = e_near
+            tiles.append(
+                jnp.dot(e_own, v_own, preferred_element_type=F32)
+                + jnp.dot(e_near, v_near, preferred_element_type=F32)
+            )
+        out_tiles.append(jnp.concatenate(tiles, axis=0))
+    sums = lane_mix(out_tiles[1], out_tiles[0], False)
+    sums = pltpu.roll(sums, 64, 1)
+    inverse = 1.0 / sums
+    attended_ref[...] = (lane_mix(out_tiles[0], out_tiles[1], False) * inverse).astype(BF16)
+    inverse_ref[...] = inverse
+
+
+def attention_backward_body(
+    pair_mix_ref, grad_ref, attended_ref, inverse_ref, probs_ref, q_ref, left_ref, left_t_ref,
+    k_own_ref, k_near_ref, v_own_ref, v_near_ref, right_own_ref, right_near_ref,
+    pen_own_ref, pen_near_ref,
+    d_q_ref, d_k_ref, d_v_ref, d_right_ref, d_left_ref, d_mix_ref,
+    scores_ref, right_sum_ref, left_sum_ref,
+):
+    pair = pl.program_id(0)
+    rows = q_ref.shape[0]
+    step = 256
+
+    @pl.when(pair == 0)
+    def _():
+        right_sum_ref[...] = jnp.zeros_like(right_sum_ref)
+        left_sum_ref[...] = jnp.zeros_like(left_sum_ref)
+
+    scaled = (grad_ref[...].astype(F32) * inverse_ref[...]).astype(BF16)
+    products = scaled.astype(F32) * attended_ref[...].astype(F32)
+    scaled_t = scaled.T
+    q_t = q_ref[...].T
+    lane = lax.broadcasted_iota(jnp.int32, products.shape, 1)
+    left = left_ref[...].astype(F32)
+    left_t = left_t_ref[...].astype(F32)
+    d_q, dk_t, dv_t = [], [], []
+    for odd in range(2):
+        mine = (lane >= 64) if odd else (lane < 64)
+        delta = -jnp.sum(jnp.where(mine, products, 0.0), axis=1, keepdims=True)
+        high = delta.astype(BF16).astype(F32)
+        low = delta - high
+        first = 0 if odd else 64
+        extra = jnp.where(lane == first, high, jnp.where(lane == first + 1, low, 0.0)).astype(BF16)
+        grad_side = jnp.where(mine, scaled, extra)
+        mix = pair_mix_ref[0, odd : odd + 1, :]
+        k_own = jnp.concatenate(
+            [right_own_ref[...], lane_mix(k_own_ref[...], pen_own_ref[...], odd)], axis=1
+        )
+        k_near = jnp.concatenate(
+            [right_near_ref[...], lane_mix(k_near_ref[...], pen_near_ref[...], odd)], axis=1
+        )
+        v_own = lane_mix(v_own_ref[...], jnp.ones_like(v_own_ref[...]), odd)
+        v_near = lane_mix(v_near_ref[...], jnp.ones_like(v_near_ref[...]), odd)
+        for start in range(0, rows, step):
+            block = grad_side[start : start + step]
+            own = nt(block, v_own).astype(BF16) * probs_ref[odd, start : start + step, :rows]
+            near = nt(block, v_near).astype(BF16) * probs_ref[odd, start : start + step, rows:]
+            scores_ref[start : start + step, :rows] = own
+            scores_ref[start : start + step, rows:] = near
+        d_query = jnp.dot(
+            scores_ref[:, :rows], k_own, preferred_element_type=F32
+        ) + jnp.dot(scores_ref[:, rows:], k_near, preferred_element_type=F32)
+        width = left.shape[1]
+        d_q.append(d_query[:, width:])
+        d_pair = d_query[:, :width]
+        left_sum_ref[...] += d_pair * mix
+        d_mix_ref[0, odd : odd + 1, :] = jnp.sum(d_pair * left, axis=0, keepdims=True)
+        mixed_t = (left_t * jnp.transpose(mix)).astype(BF16)
+        low_row = 64 * odd
+        q_side = jnp.concatenate([mixed_t, q_t[low_row : low_row + 64]], axis=0)
+        d_key = jnp.dot(q_side, scores_ref[...], preferred_element_type=F32)
+        right_sum_ref[...] += d_key[:width]
+        dk_t.append(d_key[width:])
+        dv_t.append(
+            jnp.dot(
+                scaled_t[low_row : low_row + 64], probs_ref[odd], preferred_element_type=F32
+            )
+        )
+    d_q_ref[...] = (lane_mix(d_q[0], d_q[1], False) * 0.125).astype(BF16)
+    d_k_ref[...] = jnp.concatenate(dk_t, axis=0).T.astype(BF16)
+    d_v_ref[...] = jnp.concatenate(dv_t, axis=0).T.astype(BF16)
+
+    @pl.when(pair == pl.num_programs(0) - 1)
+    def _():
+        d_right_ref[...] = right_sum_ref[...].T.astype(BF16)
+        d_left_ref[...] = left_sum_ref[...].astype(BF16)
+
+
+def whole(array):
+    zeros = (0,) * array.ndim
+    return pl.BlockSpec(array.shape, lambda *_: zeros)
+
+
+def attention_forward(pair_mix, queries, left, hot, kvr_own, kvr_near, pen_own, pen_near):
+    rows, width = queries.shape
+    pairs = width // 128
+    pair_width = left.shape[1]
+    column = pl.BlockSpec((rows, 128), lambda p: (0, p))
+    value_column = pl.BlockSpec((rows, 128), lambda p: (0, pairs + p))
+    right = pl.BlockSpec((rows, pair_width), lambda p: (0, 2 * width // pair_width))
+    flops = 2 * 2 * pairs * rows * 2 * rows * 512
+    return pl.pallas_call(
+        attention_forward_body,
+        grid=(pairs,),
+        in_specs=[
+            pl.BlockSpec((1, 2, pair_width), lambda p: (p, 0, 0)),
+            column,
+            whole(left),
+            whole(hot),
+            column,
+            column,
+            value_column,
+            value_column,
+            right,
+            right,
+            whole(pen_own),
+            whole(pen_near),
+        ],
+        out_specs=[column, column, pl.BlockSpec((2, rows, 2 * rows), lambda p: (p, 0, 0))],
+        out_shape=[
+            jax.ShapeDtypeStruct((rows, width), BF16),
+            jax.ShapeDtypeStruct((rows, width), F32),
+            jax.ShapeDtypeStruct((2 * pairs, rows, 2 * rows), BF16),
+        ],
+        compiler_params=pltpu.CompilerParams(vmem_limit_bytes=VMEM_LIMIT),
+        cost_estimate=pl.CostEstimate(
+            flops=flops, bytes_accessed=4 * pairs * rows * rows * 2, transcendentals=0
+        ),
+        name="attention_forward",
+    )(
+        pair_mix, queries, left, hot, kvr_own, kvr_near, kvr_own, kvr_near, kvr_own, kvr_near,
+        pen_own, pen_near,
+    )
+
+
+def attention_backward(
+    pair_mix, grad, attended, inverse, probs, queries, left, kvr_own, kvr_near, pen_own, pen_near
+):
+    rows, width = queries.shape
+    pairs = width // 128
+    pair_width = left.shape[1]
+    left_t = jnp.transpose(left)
+    column = pl.BlockSpec((rows, 128), lambda p: (0, p))
+    value_column = pl.BlockSpec((rows, 128), lambda p: (0, pairs + p))
+    right = pl.BlockSpec((rows, pair_width), lambda p: (0, 2 * width // pair_width))
+    key_column = pl.BlockSpec((2 * rows, 128), lambda p: (0, p))
+    mix = pl.BlockSpec((1, 2, pair_width), lambda p: (p, 0, 0))
+    flops = 2 * 2 * pairs * rows * 2 * rows * 1000
+    return pl.pallas_call(
+        attention_backward_body,
+        grid=(pairs,),
+        in_specs=[
+            mix,
+            column,
+            column,
+            column,
+            pl.BlockSpec((2, rows, 2 * rows), lambda p: (p, 0, 0)),
+            column,
+            whole(left),
+            whole(left_t),
+            column,
+            column,
+            value_column,
+            value_column,
+            right,
+            right,
+            whole(pen_own),
+            whole(pen_near),
+        ],
+        out_specs=[
+            column,
+            key_column,
+            key_column,
+            pl.BlockSpec((2 * rows, pair_width), lambda p: (0, 0)),
+            pl.BlockSpec((rows, pair_width), lambda p: (0, 0)),
+            mix,
+        ],
+        out_shape=[
+            jax.ShapeDtypeStruct((rows, width), BF16),
+            jax.ShapeDtypeStruct((2 * rows, width), BF16),
+            jax.ShapeDtypeStruct((2 * rows, width), BF16),
+            jax.ShapeDtypeStruct((2 * rows, pair_width), BF16),
+            jax.ShapeDtypeStruct((rows, pair_width), BF16),
+            jax.ShapeDtypeStruct((pairs, 2, pair_width), F32),
+        ],
+        scratch_shapes=[
+            pltpu.VMEM((rows, 2 * rows), BF16),
+            pltpu.VMEM((pair_width, 2 * rows), F32),
+            pltpu.VMEM((rows, pair_width), F32),
+        ],
+        compiler_params=pltpu.CompilerParams(vmem_limit_bytes=VMEM_LIMIT),
+        cost_estimate=pl.CostEstimate(
+            flops=flops, bytes_accessed=4 * pairs * rows * rows * 2, transcendentals=0
+        ),
+        name="attention_backward",
+    )(
+        pair_mix, grad, attended, inverse, probs, queries, left, left_t, kvr_own, kvr_near,
+        kvr_own, kvr_near, kvr_own, kvr_near, pen_own, pen_near,
     )
 
 
@@ -161,29 +409,16 @@
     projected = jnp.einsum("td,kdf->ktf", normed_a, qkv_all, preferred_element_type=F32).astype(
         BF16
     )
-    sent = jnp.concatenate([projected[1], projected[2], right_own], axis=1)
-    near = core_swap(sent)
-    keys = jnp.concatenate([projected[1], near[:, :width]]).reshape(-1, heads, head_width)
-    values = jnp.concatenate([projected[2], near[:, width : 2 * width]]).reshape(
-        -1, heads, head_width
-    )
-    right_all = jnp.concatenate([right_own, near[:, 2 * width :]])
-    queries = projected[0].reshape(rows, heads, head_width)
-    pair_query = (
-        left_own.astype(F32)[:, None, :] * jnp.transpose(pair_mix)[None, :, :]
-    ).astype(BF16)
-    scores = score_scale * jnp.einsum("qhd,khd->hqk", queries, keys, preferred_element_type=F32)
-    scores = scores + jnp.einsum(
-        "qhc,kc->hqk", pair_query, right_all, preferred_element_type=F32
-    )
-    allowed = own_ids[:, None] == key_ids[None, :]
-    scores = jnp.where(allowed[None], scores, -1e30)
-    exponent = jnp.exp(scores - jnp.max(scores, axis=-1, keepdims=True))
-    probs = (exponent / jnp.sum(exponent, axis=-1, keepdims=True)).astype(BF16)
-    attended = (
-        jnp.einsum("hqk,khd->qhd", probs, values, preferred_element_type=F32)
-        .astype(BF16)
-        .reshape(rows, width)
+    kvr_own = jnp.concatenate([projected[1], projected[2], right_own], axis=1)
+    kvr_near = core_swap(kvr_own)
+    queries = (projected[0].astype(F32) * score_scale).astype(BF16)
+    mix_rows = jnp.transpose(pair_mix).reshape(half_heads, 2, -1)
+    lanes = jnp.arange(128, dtype=jnp.int32)[None, :] & 63
+    hot = (own_ids[:, None] == lanes).astype(BF16)
+    pens = jnp.where((key_ids[:, None] != lanes) & (lanes <= slots), -1e30, 0.0).astype(BF16)
+    pen_own, pen_near = pens[:rows], pens[rows:]
+    attended, inverse, probs = attention_forward(
+        mix_rows, queries, left_own, hot, kvr_own, kvr_near, pen_own, pen_near
     )
     attn_branch = dot_f32(attended, out_all)
     middle = layer_in + valid * gate_a * attn_branch
@@ -238,41 +473,19 @@
 
     d_middle = dout + norm_backward(d_normed_f * (1.0 + scale_f), m_hat, m_inverse)
     d_attn = (valid * gate_a * d_middle).astype(BF16)
-    d_attended = dot_nt(d_attn, out_all).astype(BF16).reshape(rows, heads, head_width)
+    d_attended = dot_nt(d_attn, out_all).astype(BF16)
     out_sum = reduce_grad(row_blocks(d_attn), attended, False)
-    probs_wide = probs.astype(F32)
-    d_probs = jnp.einsum("qhd,khd->hqk", d_attended, values, preferred_element_type=F32)
-    row_dot = jnp.sum(probs_wide * d_probs, axis=-1, keepdims=True)
-    d_scores = (probs_wide * (d_probs - row_dot)).astype(BF16)
-    d_values = jnp.einsum("hqk,qhd->khd", probs, d_attended, preferred_element_type=F32)
-    d_queries = score_scale * jnp.einsum(
-        "hqk,khd->qhd", d_scores, keys, preferred_element_type=F32
-    )
-    d_keys = score_scale * jnp.einsum(
-        "hqk,qhd->khd", d_scores, queries, preferred_element_type=F32
-    )
-    d_pair_query = jnp.einsum("hqk,kc->qhc", d_scores, right_all, preferred_element_type=F32)
-    d_right = jnp.einsum("hqk,qhc->kc", d_scores, pair_query, preferred_element_type=F32)
-    d_keyed = jnp.concatenate(
-        [d_keys.reshape(-1, width), d_values.reshape(-1, width), d_right], axis=1
-    )
-    d_keyed = d_keyed[:rows] + core_swap(d_keyed[rows:].astype(BF16)).astype(F32)
-    d_keyed = d_keyed.astype(BF16)
-    d_proj = [
-        d_queries.reshape(rows, width).astype(BF16),
-        d_keyed[:, :width],
-        d_keyed[:, width : 2 * width],
-    ]
-    d_left = jnp.sum(d_pair_query * jnp.transpose(pair_mix)[None], axis=1).astype(BF16)
+    d_query, d_keys, d_values, d_right, d_left, d_mix = attention_backward(
+        mix_rows, d_attended, attended, inverse, probs, queries, left_own, kvr_own, kvr_near,
+        pen_own, pen_near,
+    )
+    d_keyed = jnp.concatenate([d_keys, d_values, d_right], axis=1)
+    d_keyed = (
+        d_keyed[:rows].astype(F32) + core_swap(d_keyed[rows:]).astype(F32)
+    ).astype(BF16)
+    d_proj = [d_query, d_keyed[:, :width], d_keyed[:, width : 2 * width]]
     d_pair = turn(jnp.concatenate([d_left, d_keyed[:, 2 * width :]], axis=1))
-    d_pair_weight = jnp.einsum(
-        "thc,tc->ch", d_pair_query, left_own.astype(F32), precision=lax.Precision.HIGHEST
-    )
-    d_pair_weight = jnp.concatenate(
-        [d_pair_weight[:, :half_heads], across(d_pair_weight[:, half_heads:])], axis=1
-    )
-    d_pair_weight = d_pair_weight[:, :half_heads] + d_pair_weight[:, half_heads:]
-    pair_sum = lax.psum_scatter(d_pair_weight, "dp", scatter_dimension=0, tiled=True)
+    d_mix = d_mix.reshape(heads, -1)
     d_normed_a = (
         dot_nt(d_proj[0], qkv_all[0]) + dot_nt(d_proj[1], qkv_all[1]) + dot_nt(d_proj[2], qkv_all[2])
     )
@@ -293,19 +506,30 @@
         axis=1,
     ).astype(BF16)
     d_chain_mod = dot_f32(jnp.transpose(member_low), d_token_mod)
-    d_chain_mod = d_chain_mod + core_swap(d_chain_mod)
+    modded = mod_weight.shape[1]
+    d_mix_own = jnp.concatenate(
+        [jnp.where(mp_at == 0, d_mix[:half_heads], d_mix[half_heads:]),
+         jnp.where(mp_at == 0, d_mix[half_heads:], d_mix[:half_heads])], axis=0
+    )
+    d_mix_own = d_mix_own.reshape(slots, -1)
+    summed = jnp.concatenate([d_chain_mod, d_mix_own], axis=1)
+    summed = summed + core_swap(summed)
     arch_low = (
         arches[:, None] == jnp.arange(cath_table.shape[0], dtype=jnp.int32)[None, :]
     ).astype(BF16)
     gathered = jnp.concatenate(
-        [d_chain_mod.astype(BF16), cond_act, time_embed, cond_slope.astype(BF16), arch_low], axis=1
+        [summed.astype(BF16), cond_act, time_embed, cond_slope.astype(BF16), arch_low], axis=1
     )
     gathered = jnp.concatenate([gathered, across(gathered)], axis=0)
     for bit in range(1, bits):
         gathered = jnp.concatenate([gathered, flip(bit)(gathered)], axis=0)
-    modded = mod_weight.shape[1]
-    cuts = [modded, modded + cond_width, modded + 2 * cond_width, modded + 3 * cond_width]
-    d_all, cond_all, time_all, slope_all, arch_all = jnp.split(gathered, cuts, axis=1)
+    mixed_to = modded + d_mix_own.shape[1]
+    cuts = [modded, mixed_to, mixed_to + cond_width, mixed_to + 2 * cond_width, mixed_to + 3 * cond_width]
+    d_all, mix_all, cond_all, time_all, slope_all, arch_all = jnp.split(gathered, cuts, axis=1)
+    mix_sum = jnp.sum(mix_all.astype(F32).reshape(dp_count, heads, -1), axis=0)
+    mix_sum = jnp.where(mp_at == 0, mix_sum[:half_heads], mix_sum[half_heads:])
+    taken = mix_sum.shape[1] // dp_count
+    pair_sum = jnp.transpose(lax.dynamic_slice_in_dim(mix_sum, dp_at * taken, taken, 1))
     mod_bias_sum = jnp.sum(d_all.astype(F32), axis=0)
     mod_weight_sum = dot_f32(jnp.transpose(cond_all), d_all)
     d_cond_pre = dot_nt(d_all, mod_weight) * slope_all.astype(F32)

time: 734 us -> 570 us (0.78)
  matrix products: 197 us -> 97.7 us
  Pallas kernels: 0 us -> 41.8 us
  other arithmetic: 82 us -> 46 us
  waiting for transfers between devices: 279 us -> 245 us
  local copies, waits for them, and re-layouts: 76.1 us -> 62.7 us
  between operations: 16 us -> 2.86 us
  starting transfers between devices: 71.8 us -> 62.5 us
    dot_general x9 -> x0, matrix products: 79.2 us -> none  [the longest x1 12.9 us: shards(): jnp.einsum('qhd,khd->hqk', d_attended, values, preferred_element_type=F32)]
    unnamed x2 -> x0, waiting for transfers between devices: 51 us -> none
    pallas_call x0 -> x2, Pallas kernels: none -> 41.8 us  [the longest x1 22.4 us: attention_backward(): pl.pallas_call(attention_backward_body, grid=(pairs,), in_specs=[mix, col...]
    convert_element_type x3 -> x4, other arithmetic: 34.6 us -> 4.88 us  [the longest x1 2.62 us: shards(): d_keyed = (d_keyed[:rows].astype(F32) + core_swap(d_keyed[rows:]).astype(...]
    sub x1 -> x0, matrix products: 23.3 us -> none  [shards(): exponent = jnp.exp(scores - jnp.max(scores, axis=-1, keepdims=True))]
    ppermute x44 -> x43, waiting for transfers between devices: 228 us -> 245 us  [mover(): return lambda array: lax.ppermute(array, AXES, table)]
    ppermute x44 -> x43, starting transfers between devices: 71.8 us -> 62.5 us  [mover(): return lambda array: lax.ppermute(array, AXES, table)]
    unnamed x202 -> x216, local copies, waits for them, and re-layouts: 29.6 us -> 22.8 us
  transfers between devices with their start and end apart: 45 -> 43, of which waited for: 19 -> 17; matrix products, arithmetic and copies ran while one was open for 31% -> 24% of each run, Pallas kernels for 0% -> 7%
where the time goes in v2:
time: 570 us; the launch traced here: 559 us
  waiting for transfers between devices  245 us (43%)
  matrix products  97.7 us (17%)
  local copies, waits for them, and re-layouts  62.7 us (11%)
  starting transfers between devices  62.5 us (11%)
  other arithmetic  46 us (8%)
  Pallas kernels  41.8 us (7%)
    ppermute x43, waiting for transfers between devices, mover(): return lambda array: lax.ppermute(array, AXES, table)  245 us
    ppermute x43, starting transfers between devices, mover(): return lambda array: lax.ppermute(array, AXES, table)  62.5 us
    dot_general x16, matrix products, dot_f32(): return jnp.dot(left_side, right_side, preferred_element_type=F32)  62 us
    dot_general x8, matrix products, dot_nt(): lax.dot_general(left_side, right_side, (((1,), (1,)), ((), ())), preferre...  27.6 us
    unnamed x216, local copies, waits for them, and re-layouts  22.8 us
    pallas_call x1, Pallas kernels, attention_backward(): pl.pallas_call(attention_backward_body, grid=(pairs,), in_specs=[mix, col...  22.4 us
    pallas_call x1, Pallas kernels, attention_forward(): pl.pallas_call(attention_forward_body, grid=(pairs,), in_specs=[pl.BlockS...  19.4 us
    select_n x4, other arithmetic, other_half(): jnp.where(core == 0, jnp.concatenate([mine, near], axis=axis), jnp.concat...  12.7 us
  transfers between devices with their start and end apart: 43, of which 17 were waited for; matrix products, arithmetic and copies ran while one was open for 24% of the time, Pallas kernels for 7%

profile of v2, /device:TPU:1, one launch (start us, length us, event | category | flops | bytes accessed | tf_op | source)
XLA Modules:
  0.0 558.8 jit_solution(10374363380694126536)
XLA Ops:
  2.8 4.5 collective-permute-start
  7.4 3.9 copy.43
  16.2 4.9 collective-permute-start.2
  23.0 3.4 constant_dynamic-slice_fusion.1
  30.0 3.9 fusion.62
  33.9 11.2 %collective-permute-done.5 = bf16[512,512]{1,0:T(8,128)(2,1)} collective-permute-done((bf16[512,512]{1,0:T(8,128)(2,1)}, bf16[512,512]{1,0:T(8,128)(2,1)}, u32[]{:S(2)}, u32[]{:S(2)}) %collective-permute-start.5) | collective-permute-done | bytes 524320 | tf_op jit(solution)/shard_map/ppermute | solution.py:306
  58.4 65.7 %collective-permute-done.11 = bf16[768,768]{1,0:T(8,128)(2,1)} collective-permute-done((bf16[768,768]{1,0:T(8,128)(2,1)S(1)}, bf16[768,768]{1,0:T(8,128)(2,1)}, u32[]{:S(2)}, u32[]{:S(2)}) %collective-permute-start.11) | collective-permute-done | bytes 1179680 | tf_op jit(solution)/shard_map/ppermute | solution.py:306
  126.9 3.5 collective-permute-start.14
  138.4 4.5 collective-permute-start.10
  143.0 3.9 maximum_select_fusion.1
  146.9 19.4 %attention_forward.1 = (bf16[512,768]{1,0:T(8,128)(2,1)S(1)}, f32[512,768]{1,0:T(8,128)S(1)}, bf16[12,512,1024]{2,1,0:T(8,128)(2,1)}) custom-call(f32[6,2,256]{2,1,0:T(2,128)S(1)} %reshape.201.pair_mix_ref, bf16[512,768]{1,0:T(8,128)(2,1)S(1)} %fusion.47.q_ref, bf16[512,256]{1,0:T(8,128)(2,1)S(1)} %get-tuple-element.71.left_ref, ...), custom_call_target="tpu_custom_call" | custom-call | flops 6442450944 | bytes 12582912 | tf_op jit(solution)/shard_map/attention_forward/pallas_call | solution.py:195
  166.4 4.7 fusion.98
  171.4 3.4 fusion.25
  177.1 2.8 gather_fusion.2
  182.1 2.7 gather_fusion.3
  184.8 8.0 %fusion.5 = f32[512,3072]{1,0:T(8,128)} fusion(bf16[512,768]{1,0:T(8,128)(2,1)} %get-tuple-element.50, bf16[1536,768]{1,0:T(8,128)(2,1)} %maximum_select_fusion.1, bf16[1536,768]{1,0:T(8,128)(2,1)} %param.33), kind=kOutput, calls=%fused_computation.35 | convolution fusion | flops 2425356288 | bytes 11796480 | tf_op jit(solution)/shard_map/dot_general | solution.py:45
  192.8 4.7 maximum_select_fusion
  197.5 6.9 %fusion.58 = f32[512,3072]{1,0:T(8,128)} fusion(bf16[512,768]{1,0:T(8,128)(2,1)S(1)} %copy-done.33, bf16[2,768,1536]{2,1,0:T(8,128)(2,1)S(1)} %maximum_select_fusion, bf16[2,768,1536]{2,1,0:T(8,128)(2,1)} %param.32), kind=kOutput, calls=%fused_computation.129 | convolution fusion | flops 2425356288 | bytes 16515072 | tf_op jit(solution)/shard_map/dot_general | solution.py:41
  204.4 9.9 %multiply_convert_fusion.1 = (bf16[512,3072]{1,0:T(8,128)(2,1)S(1)}, bf16[512,3072]{1,0:T(8,128)(2,1)S(1)}, bf16[512,3072]{1,0:T(8,128)(2,1)S(1)}) fusion(f32[512,3072]{1,0:T(8,128)} %fusion.5, f32[512,3072]{1,0:T(8,128)} %fusion.58, bf16[512,768]{1,0:T(8,128)(2,1)S(1)} %copy-done.33, bf16[2,768,1536]{2,1,0:T(8,128)(2,1)} %param.32, ...), kind=kOutput, calls=%fused_computation.10 | convolution fusion | flops 2448949248 | bytes 32243712 | tf_op jit(solution)/shard_map/dot_general | solution.py:41
  214.3 6.2 %fusion.56 = f32[512,768]{1,0:T(8,128)S(1)} fusion(bf16[512,3072]{1,0:T(8,128)(2,1)S(1)} %get-tuple-element.47, bf16[2,768,1536]{2,1,0:T(8,128)(2,1)S(1)} %maximum_select_fusion, bf16[2,768,1536]{2,1,0:T(8,128)(2,1)} %param.32), kind=kOutput, calls=%fused_computation.128 | convolution fusion | flops 2425356288 | bytes 14155776 | tf_op jit(solution)/shard_map/dot_general | solution.py:45
  220.6 5.2 fusion.93
  225.9 7.9 %multiply_convert_fusion.5 = (bf16[512,768]{1,0:T(8,128)(2,1)S(1)}, f32[512,768]{1,0:T(8,128)}, bf16[512,768]{1,0:T(8,128)(2,1)}, f32[512,768]{1,0:T(8,128)}) fusion(f32[512,4608]{1,0:T(8,128)} %copy-done.14, f32[512]{0:T(512)S(1)} %copy-done.85, f32[512]{0:T(512)S(1)} %get-tuple-element.100, f32[512,768]{1,0:T(8,128)S(1)} %copy-done.23, ...), kind=kOutput, calls=%fused_computation.78 | convolution fusion | flops 2432040960 | bytes 21243904 | tf_op jit(solution)/shard_map/dot_general | solution.py:41
  237.9 2.8 gather_fusion.1
  243.8 2.8 convolution_convert_fusion.1
  250.2 22.4 %attention_backward.1 = (bf16[512,768]{1,0:T(8,128)(2,1)S(1)}, bf16[1024,768]{1,0:T(8,128)(2,1)}, bf16[1024,768]{1,0:T(8,128)(2,1)}, bf16[1024,256]{1,0:T(8,128)...) custom-call(f32[6,2,256]{2,1,0:T(2,128)S(1)} %reshape.201.pair_mix_ref, ...), custom_call_target="tpu_custom_call" | custom-call | flops 12582912000 | bytes 12582912 | tf_op jit(solution)/shard_map/attention_backward/pallas_call | solution.py:242
  284.2 6.0 %convolution_convert_fusion = bf16[384,6144]{1,0:T(8,128)(2,1)} fusion(bf16[384,512]{1,0:T(8,128)(2,1)S(1)} %bitcast.124, bf16[512,1536]{1,0:T(8,128)(2,1)S(1)} %get-tuple-element.98, bf16[512,1536]{1,0:T(8,128)(2,1)S(1)} %get-tuple-element.52, bf16[512,1536]{1,0:T(8,128)(2,1)S(1)} %get-tuple-element.99, bf16[512,1536]{1,0:T(8,128)(2,1)S(1)} %get-tuple-element.51), kind=kOutput, calls=%fused_computation.7 | convolution fusion | flops 2443444224 | bytes 11403264 | tf_op jit(solution)/shard_map/dot_general | solution.py:41
  296.4 3.7 collective-permute-done.30
  304.5 2.7 collective-permute-done.32
  313.2 2.7 fusion.94
  324.4 4.4 collective-permute-start.18
  337.3 5.1 collective-permute-done.19
  342.6 4.4 collective-permute-done.20
  346.9 6.6 %collective-permute-start.16 = (bf16[512,768]{1,0:T(8,128)(2,1)S(1)}, bf16[512,768]{1,0:T(8,128)(2,1)S(1)}, u32[]{:S(2)}, u32[]{:S(2)}) collective-permute-start(bf16[512,768]{1,0:T(8,128)(2,1)S(1)} %fusion.19), channel_id=1, source_target_pairs={{0,0},{1,2},{2,1},{3,3},{4,4},{5,6},{6,5},{7,7},{8,8},{9,10},{10,9... | collective-permute-start | bytes 2359304 | tf_op jit(solution)/shard_map/ppermute | solution.py:306
  354.0 3.1 add_convert_fusion.1
  358.3 5.0 collective-permute-done.21
  366.1 32.8 %collective-permute-done.22 = bf16[64,5803]{1,0:T(8,128)(2,1)S(1)} collective-permute-done((bf16[64,5803]{1,0:T(8,128)(2,1)S(1)}, bf16[64,5803]{1,0:T(8,128)(2,1)S(1)}, u32[]{:S(2)}, u32[]{:S(2)}) %collective-permute-start.22) | collective-permute-done | bytes 742816 | tf_op jit(solution)/shard_map/ppermute | solution.py:306
  407.7 3.1 fusion.44
  411.6 8.0 %add_convert_fusion = bf16[384,6144]{1,0:T(8,128)(2,1)S(1)} fusion(bf16[384,6144]{1,0:T(8,128)(2,1)} %collective-permute-done.33, bf16[384,512]{1,0:T(8,128)(2,1)S(1)} %bitcast.120, bf16[512,1536]{1,0:T(8,128)(2,1)S(1)} %copy-done.50, bf16[512,1536]{1,0:T(8,128)(2,1)S(1)} %copy-done.48, bf16[512,1536]{1,0:T(8,128)(2,1)S(1)} %copy-done.52, ...), kind=kOutput, calls=%fused_computation.6 | convolution fusion | flops 2448162816 | bytes 16121856 | tf_op jit(solution)/shard_map/dot_general | solution.py:41
  426.4 9.4 %collective-permute-done.40 = bf16[96,3072]{1,0:T(8,128)(2,1)S(1)} collective-permute-done((bf16[96,3072]{1,0:T(8,128)(2,1)S(1)}, bf16[96,3072]{1,0:T(8,128)(2,1)S(1)}, u32[]{:S(2)}, u32[]{:S(2)}) %collective-permute-start.40) | collective-permute-done | bytes 589856 | tf_op jit(solution)/shard_map/ppermute | solution.py:306
  436.0 2.7 collective-permute-start.41
  438.7 52.1 %collective-permute-done.24 = bf16[384,1152]{1,0:T(8,128)(2,1)S(1)} collective-permute-done((bf16[384,1152]{1,0:T(8,128)(2,1)S(1)}, bf16[384,1152]{1,0:T(8,128)(2,1)S(1)}, u32[]{:S(2)}, u32[]{:S(2)}) %collective-permute-start.24) | collective-permute-done | bytes 884768 | tf_op jit(solution)/shard_map/ppermute | solution.py:306
  493.6 7.4 %collective-permute-done.25 = bf16[192,1152]{1,0:T(8,128)(2,1)S(1)} collective-permute-done((bf16[192,1152]{1,0:T(8,128)(2,1)S(1)}, bf16[192,1152]{1,0:T(8,128)(2,1)S(1)}, u32[]{:S(2)}, u32[]{:S(2)}) %collective-permute-start.25) | collective-permute-done | bytes 442400 | tf_op jit(solution)/shard_map/ppermute | solution.py:306
  503.2 3.2 collective-permute-done.26
  506.4 2.9 collective-permute-start.27
  509.3 17.1 %collective-permute-done.35 = bf16[192,3072]{1,0:T(8,128)(2,1)S(1)} collective-permute-done((bf16[192,3072]{1,0:T(8,128)(2,1)S(1)}, bf16[192,3072]{1,0:T(8,128)(2,1)S(1)}, u32[]{:S(2)}, u32[]{:S(2)}) %collective-permute-start.35) | collective-permute-done | bytes 1179680 | tf_op jit(solution)/shard_map/ppermute | solution.py:306
  528.8 10.3 %collective-permute-done.36 = bf16[96,3072]{1,0:T(8,128)(2,1)S(1)} collective-permute-done((bf16[96,3072]{1,0:T(8,128)(2,1)S(1)}, bf16[96,3072]{1,0:T(8,128)(2,1)S(1)}, u32[]{:S(2)}, u32[]{:S(2)}) %collective-permute-start.36) | collective-permute-done | bytes 589856 | tf_op jit(solution)/shard_map/ppermute | solution.py:306
  539.2 3.6 collective-permute-start.37
  543.5 12.1 %collective-permute-done.37 = bf16[48,3072]{1,0:T(8,128)(2,1)S(1)} collective-permute-done((bf16[48,3072]{1,0:T(8,128)(2,1)S(1)}, bf16[48,3072]{1,0:T(8,128)(2,1)S(1)}, u32[]{:S(2)}, u32[]{:S(2)}) %collective-permute-start.37) | collective-permute-done | bytes 294944 | tf_op jit(solution)/shard_map/ppermute | solution.py:306
  (424 shorter events, 128.5 us)
Async XLA Ops:
  0.6 28.7 %copy-start = (bf16[256,4608]{1,0:T(8,128)(2,1)S(1)}, bf16[256,4608]{1,0:T(8,128)(2,1)}, u32[]{:S(2)}) copy-start(bf16[256,4608]{1,0:T(8,128)(2,1)} %param.27) | copy-start | bytes 7077892
  2.8 25.9 %collective-permute-start.1 = (f32[3,8]{1,0:T(4,128)S(1)}, f32[3,8]{1,0:T(4,128)S(1)}, u32[]{:S(2)}, u32[]{:S(2)}) collective-permute-start(f32[3,8]{1,0:T(4,128)S(1)} %pad_maximum_fusion.26), channel_id=1, source_target_pairs={{0,2},{1,3},{2,0},{3,1},{4,6},{5,7},{6,4},{7,5},{8,10},{9,11},{10,... | collective-permute-start | bytes 296 | tf_op jit(solution)/shard_map/ppermute | solution.py:306
  2.8 44.0 %collective-permute-start = (bf16[512,768]{1,0:T(8,128)(2,1)}, bf16[512,768]{1,0:T(8,128)(2,1)S(1)}, u32[]{:S(2)}, u32[]{:S(2)}) collective-permute-start(bf16[512,768]{1,0:T(8,128)(2,1)} %param.19), channel_id=1, source_target_pairs={{0,0},{1,2},{2,1},{3,3},{4,4},{5,6},{6,5},{7,7},{8,8},{9,10},{10,9... | collective-permute-start | bytes 2359304 | tf_op jit(solution)/shard_map/ppermute | solution.py:306
  13.5 35.1 %collective-permute-start.3 = (bf16[3,768,192]{1,2,0:T(8,128)(2,1)}, bf16[3,768,192]{1,2,0:T(8,128)(2,1)}, u32[]{:S(2)}, u32[]{:S(2)}) collective-permute-start(bf16[3,768,192]{1,2,0:T(8,128)(2,1)} %constant_dynamic-slice_fusion.3), channel_id=1, source_target_pairs={{0,1},{1,0},{2,3},{3,2},{4,5},{5,4},{6,7},{7,6},{8,9},{9,8},{10,11... | collective-permute-start | bytes 2654216 | tf_op jit(solution)/shard_map/ppermute | solution.py:306
  14.3 30.8 %collective-permute-start.5 = (bf16[512,512]{1,0:T(8,128)(2,1)}, bf16[512,512]{1,0:T(8,128)(2,1)}, u32[]{:S(2)}, u32[]{:S(2)}) collective-permute-start(bf16[512,512]{1,0:T(8,128)(2,1)} %pad_maximum_fusion.19), channel_id=1, source_target_pairs={{0,0},{1,2},{2,1},{3,3},{4,4},{5,6},{6,5},{7,7},{8,8},{9,10},{10,9... | collective-permute-start | bytes 1572872 | tf_op jit(solution)/shard_map/ppermute | solution.py:306
  16.2 110.7 %collective-permute-start.2 = (bf16[256,6]{0,1:T(8,128)(2,1)}, bf16[256,6]{0,1:T(8,128)(2,1)}, u32[]{:S(2)}, u32[]{:S(2)}) collective-permute-start(bf16[256,6]{0,1:T(8,128)(2,1)} %param.30), channel_id=1, source_target_pairs={{0,1},{1,0},{2,3},{3,2},{4,5},{5,4},{6,7},{7,6},{8,9},{9,8},{10,11... | collective-permute-start | bytes 9224 | tf_op jit(solution)/shard_map/ppermute | solution.py:306
  21.2 37.0 %copy-start.91 = (s32[128]{0:T(128)}, s32[128]{0:T(128)S(1)}, u32[]{:S(2)}) copy-start(s32[128]{0:T(128)S(1)} %iota_and_fusion) | copy-start | bytes 1540
  28.6 97.7 %collective-permute-start.7 = (bf16[192,768]{1,0:T(8,128)(2,1)}, bf16[192,768]{1,0:T(8,128)(2,1)}, u32[]{:S(2)}, u32[]{:S(2)}) collective-permute-start(bf16[192,768]{1,0:T(8,128)(2,1)} %constant_dynamic-slice_fusion.2), channel_id=1, source_target_pairs={{0,1},{1,0},{2,3},{3,2},{4,5},{5,4},{6,7},{7,6},{8,9},{9,8},{10,11... | collective-permute-start | bytes 884744 | tf_op jit(solution)/shard_map/ppermute | solution.py:306
  45.1 93.3 %collective-permute-start.9 = (bf16[2,768,768]{2,1,0:T(8,128)(2,1)}, bf16[2,768,768]{2,1,0:T(8,128)(2,1)}, u32[]{:S(2)}, u32[]{:S(2)}) collective-permute-start(bf16[2,768,768]{2,1,0:T(8,128)(2,1)} %constant_dynamic-slice_fusion.1), channel_id=1, source_target_pairs={{0,1},{1,0},{2,3},{3,2},{4,5},{5,4},{6,7},{7,6},{8,9},{9,8},{10,11... | collective-permute-start | bytes 7077896 | tf_op jit(solution)/shard_map/ppermute | solution.py:306
  46.9 77.1 %collective-permute-start.11 = (bf16[768,768]{1,0:T(8,128)(2,1)S(1)}, bf16[768,768]{1,0:T(8,128)(2,1)}, u32[]{:S(2)}, u32[]{:S(2)}) collective-permute-start(bf16[768,768]{1,0:T(8,128)(2,1)S(1)} %copy-done.58), channel_id=1, source_target_pairs={{0,1},{1,0},{2,3},{3,2},{4,5},{5,4},{6,7},{7,6},{8,9},{9,8},{10,11... | collective-permute-start | bytes 3538952 | tf_op jit(solution)/shard_map/ppermute | solution.py:306
  48.6 3.0 collective-permute-start.4
  55.9 75.2 %copy-start.59 = (bf16[256,512]{0,1:T(8,128)(2,1)S(1)}, bf16[256,512]{0,1:T(8,128)(2,1)}, u32[]{:S(2)}) copy-start(bf16[256,512]{0,1:T(8,128)(2,1)} %get-tuple-element.69) | copy-start | bytes 786436
  57.8 89.1 %collective-permute-start.6 = (bf16[512,1792]{1,0:T(8,128)(2,1)}, bf16[512,1792]{1,0:T(8,128)(2,1)}, u32[]{:S(2)}, u32[]{:S(2)}) collective-permute-start(bf16[512,1792]{1,0:T(8,128)(2,1)} %pad_maximum_fusion.9.k_own_ref.v_own_ref.right_own_ref), channel_id=1, source_target_pairs={{0,2},{1,3},{2,0},{3,1},{4,6},{5,7},{6,4},{7,5},{8,10},{9,11},{10,... | collective-permute-start | bytes 5505032 | tf_op jit(solution)/shard_map/ppermute | solution.py:306
  124.0 18.9 %collective-permute-start.12 = (bf16[768,768]{1,0:T(8,128)(2,1)}, bf16[768,768]{1,0:T(8,128)(2,1)}, u32[]{:S(2)}, u32[]{:S(2)}) collective-permute-start(bf16[768,768]{1,0:T(8,128)(2,1)} %collective-permute-done.11), channel_id=1, source_target_pairs={{0,2},{1,3},{2,0},{3,1},{4,6},{5,7},{6,4},{7,5},{8,10},{9,11},{10,... | collective-permute-start | bytes 3538952 | tf_op jit(solution)/shard_map/ppermute | solution.py:306
  126.3 5.6 %collective-permute-start.8 = (bf16[192,768]{1,0:T(8,128)(2,1)}, bf16[192,768]{1,0:T(8,128)(2,1)S(1)}, u32[]{:S(2)}, u32[]{:S(2)}) collective-permute-start(bf16[192,768]{1,0:T(8,128)(2,1)} %collective-permute-done.7), channel_id=1, source_target_pairs={{0,2},{1,3},{2,0},{3,1},{4,6},{5,7},{6,4},{7,5},{8,10},{9,11},{10,... | collective-permute-start | bytes 884744 | tf_op jit(solution)/shard_map/ppermute | solution.py:306
  126.9 39.4 %collective-permute-start.14 = (bf16[512,768]{1,0:T(8,128)(2,1)}, bf16[512,768]{1,0:T(8,128)(2,1)}, u32[]{:S(2)}, u32[]{:S(2)}) collective-permute-start(bf16[512,768]{1,0:T(8,128)(2,1)} %param.34), channel_id=1, source_target_pairs={{0,0},{1,2},{2,1},{3,3},{4,4},{5,6},{6,5},{7,7},{8,8},{9,10},{10,9... | collective-permute-start | bytes 2359304 | tf_op jit(solution)/shard_map/ppermute | solution.py:306
  138.4 54.4 %collective-permute-start.10 = (bf16[2,768,768]{2,1,0:T(8,128)(2,1)}, bf16[2,768,768]{2,1,0:T(8,128)(2,1)}, u32[]{:S(2)}, u32[]{:S(2)}) collective-permute-start(bf16[2,768,768]{2,1,0:T(8,128)(2,1)} %collective-permute-done.9), channel_id=1, source_target_pairs={{0,2},{1,3},{2,0},{3,1},{4,6},{5,7},{6,4},{7,5},{8,10},{9,11},{10,... | collective-permute-start | bytes 7077896 | tf_op jit(solution)/shard_map/ppermute | solution.py:306
  246.6 107.0 %collective-permute-start.38 = (bf16[384,3072]{1,0:T(8,128)(2,1)}, bf16[384,3072]{1,0:T(8,128)(2,1)}, u32[]{:S(2)}, u32[]{:S(2)}) collective-permute-start(bf16[384,3072]{1,0:T(8,128)(2,1)} %convolution_convert_fusion.1), channel_id=1, source_target_pairs={{0,2},{1,3},{2,0},{3,1},{4,6},{5,7},{6,4},{7,5},{8,10},{9,11},{10,... | collective-permute-start | bytes 7077896 | tf_op jit(solution)/shard_map/ppermute | solution.py:306
  249.7 30.5 %collective-permute-start.28 = (bf16[384,768]{1,0:T(8,128)(2,1)}, bf16[384,768]{1,0:T(8,128)(2,1)}, u32[]{:S(2)}, u32[]{:S(2)}) collective-permute-start(bf16[384,768]{1,0:T(8,128)(2,1)} %convolution_convert_fusion.4), channel_id=1, source_target_pairs={{0,2},{1,3},{2,0},{3,1},{4,6},{5,7},{6,4},{7,5},{8,10},{9,11},{10,... | collective-permute-start | bytes 1769480 | tf_op jit(solution)/shard_map/ppermute | solution.py:306
  272.6 23.0 %copy-start.1 = (bf16[512,768]{1,0:T(8,128)(2,1)}, bf16[512,768]{1,0:T(8,128)(2,1)S(1)}, u32[]{:S(2)}) copy-start(bf16[512,768]{1,0:T(8,128)(2,1)S(1)} %get-tuple-element.26) | copy-start | bytes 2359300
  277.8 30.1 %collective-permute-start.15 = (bf16[512,1792]{1,0:T(8,128)(2,1)}, bf16[512,1792]{1,0:T(8,128)(2,1)}, u32[]{:S(2)}, u32[]{:S(2)}) collective-permute-start(bf16[512,1792]{1,0:T(8,128)(2,1)} %slice.376), channel_id=1, source_target_pairs={{0,2},{1,3},{2,0},{3,1},{4,6},{5,7},{6,4},{7,5},{8,10},{9,11},{10,... | collective-permute-start | bytes 5505032 | tf_op jit(solution)/shard_map/ppermute | solution.py:306
  282.4 11.8 %collective-permute-start.29 = (bf16[192,768]{1,0:T(8,128)(2,1)S(1)}, bf16[192,768]{1,0:T(8,128)(2,1)S(1)}, u32[]{:S(2)}, u32[]{:S(2)}) collective-permute-start(bf16[192,768]{1,0:T(8,128)(2,1)S(1)} %slice.408), channel_id=1, source_target_pairs={{0,4},{1,5},{2,6},{3,7},{4,0},{5,1},{6,2},{7,3},{8,12},{9,13},{10,... | collective-permute-start | bytes 884744 | tf_op jit(solution)/shard_map/ppermute | solution.py:306
  290.2 120.5 %collective-permute-start.33 = (bf16[384,6144]{1,0:T(8,128)(2,1)}, bf16[384,6144]{1,0:T(8,128)(2,1)}, u32[]{:S(2)}, u32[]{:S(2)}) collective-permute-start(bf16[384,6144]{1,0:T(8,128)(2,1)} %convolution_convert_fusion), channel_id=1, source_target_pairs={{0,2},{1,3},{2,0},{3,1},{4,6},{5,7},{6,4},{7,5},{8,10},{9,11},{10,... | collective-permute-start | bytes 14155784 | tf_op jit(solution)/shard_map/ppermute | solution.py:306
  290.6 13.9 %collective-permute-start.13 = (bf16[512,768]{1,0:T(8,128)(2,1)}, bf16[512,768]{1,0:T(8,128)(2,1)S(1)}, u32[]{:S(2)}, u32[]{:S(2)}) collective-permute-start(bf16[512,768]{1,0:T(8,128)(2,1)} %get-tuple-element.49), channel_id=1, source_target_pairs={{0,0},{1,2},{2,1},{3,3},{4,4},{5,6},{6,5},{7,7},{8,8},{9,10},{10,9... | collective-permute-start | bytes 2359304 | tf_op jit(solution)/shard_map/ppermute | solution.py:306
  294.2 5.9 %collective-permute-start.30 = (bf16[96,768]{1,0:T(8,128)(2,1)S(1)}, bf16[96,768]{1,0:T(8,128)(2,1)S(1)}, u32[]{:S(2)}, u32[]{:S(2)}) collective-permute-start(bf16[96,768]{1,0:T(8,128)(2,1)S(1)} %slice.410), channel_id=1, source_target_pairs={{0,8},{1,9},{2,10},{3,11},{4,12},{5,13},{6,14},{7,15},{8,0},{9,1},... | collective-permute-start | bytes 442376 | tf_op jit(solution)/shard_map/ppermute | solution.py:306
  300.2 4.2 collective-permute-start.31
  304.4 2.9 collective-permute-start.32
  324.4 9.9 %collective-permute-start.18 = (f32[8,4992]{1,0:T(8,128)S(1)}, f32[8,4992]{1,0:T(8,128)S(1)}, u32[]{:S(2)}, u32[]{:S(2)}) collective-permute-start(f32[8,4992]{1,0:T(8,128)S(1)} %pad_maximum_fusion.24), channel_id=1, source_target_pairs={{0,2},{1,3},{2,0},{3,1},{4,6},{5,7},{6,4},{7,5},{8,10},{9,11},{10,... | collective-permute-start | bytes 479240 | tf_op jit(solution)/shard_map/ppermute | solution.py:306
  331.6 91.1 %collective-permute-start.23 = (bf16[384,2304]{1,0:T(8,128)(2,1)}, bf16[384,2304]{1,0:T(8,128)(2,1)}, u32[]{:S(2)}, u32[]{:S(2)}) collective-permute-start(bf16[384,2304]{1,0:T(8,128)(2,1)} %convolution_convert_fusion.2), channel_id=1, source_target_pairs={{0,2},{1,3},{2,0},{3,1},{4,6},{5,7},{6,4},{7,5},{8,10},{9,11},{10,... | collective-permute-start | bytes 5308424 | tf_op jit(solution)/shard_map/ppermute | solution.py:306
  332.4 31.0 %collective-permute-start.17 = (bf16[512,512]{1,0:T(8,128)(2,1)S(1)}, bf16[512,512]{1,0:T(8,128)(2,1)S(1)}, u32[]{:S(2)}, u32[]{:S(2)}) collective-permute-start(bf16[512,512]{1,0:T(8,128)(2,1)S(1)} %pad_maximum_fusion.20), channel_id=1, source_target_pairs={{0,0},{1,2},{2,1},{3,3},{4,4},{5,6},{6,5},{7,7},{8,8},{9,10},{10,9... | collective-permute-start | bytes 1572872 | tf_op jit(solution)/shard_map/ppermute | solution.py:306
  335.0 7.4 %collective-permute-start.19 = (bf16[8,5803]{1,0:T(8,128)(2,1)S(1)}, bf16[8,5803]{1,0:T(8,128)(2,1)S(1)}, u32[]{:S(2)}, u32[]{:S(2)}) collective-permute-start(bf16[8,5803]{1,0:T(8,128)(2,1)S(1)} %get-tuple-element.92), channel_id=1, source_target_pairs={{0,1},{1,0},{2,3},{3,2},{4,5},{5,4},{6,7},{7,6},{8,9},{9,8},{10,11... | collective-permute-start | bytes 278552 | tf_op jit(solution)/shard_map/ppermute | solution.py:306
  342.4 4.5 collective-permute-start.20
  346.9 19.2 %collective-permute-start.16 = (bf16[512,768]{1,0:T(8,128)(2,1)S(1)}, bf16[512,768]{1,0:T(8,128)(2,1)S(1)}, u32[]{:S(2)}, u32[]{:S(2)}) collective-permute-start(bf16[512,768]{1,0:T(8,128)(2,1)S(1)} %fusion.19), channel_id=1, source_target_pairs={{0,0},{1,2},{2,1},{3,3},{4,4},{5,6},{6,5},{7,7},{8,8},{9,10},{10,9... | collective-permute-start | bytes 2359304 | tf_op jit(solution)/shard_map/ppermute | solution.py:306
  353.7 9.6 %collective-permute-start.21 = (bf16[32,5803]{1,0:T(8,128)(2,1)S(1)}, bf16[32,5803]{1,0:T(8,128)(2,1)S(1)}, u32[]{:S(2)}, u32[]{:S(2)}) collective-permute-start(bf16[32,5803]{1,0:T(8,128)(2,1)S(1)} %pad_maximum_fusion.21), channel_id=1, source_target_pairs={{0,8},{1,9},{2,10},{3,11},{4,12},{5,13},{6,14},{7,15},{8,0},{9,1},... | collective-permute-start | bytes 1114184 | tf_op jit(solution)/shard_map/ppermute | solution.py:306
  363.3 56.6 %collective-permute-start.39 = (bf16[192,3072]{1,0:T(8,128)(2,1)}, bf16[192,3072]{1,0:T(8,128)(2,1)S(1)}, u32[]{:S(2)}, u32[]{:S(2)}) collective-permute-start(bf16[192,3072]{1,0:T(8,128)(2,1)} %slice.434), channel_id=1, source_target_pairs={{0,4},{1,5},{2,6},{3,7},{4,0},{5,1},{6,2},{7,3},{8,12},{9,13},{10,... | collective-permute-start | bytes 3538952 | tf_op jit(solution)/shard_map/ppermute | solution.py:306
  363.4 35.5 %collective-permute-start.22 = (bf16[64,5803]{1,0:T(8,128)(2,1)S(1)}, bf16[64,5803]{1,0:T(8,128)(2,1)S(1)}, u32[]{:S(2)}, u32[]{:S(2)}) collective-permute-start(bf16[64,5803]{1,0:T(8,128)(2,1)S(1)} %pad_maximum_fusion.17), channel_id=1, source_target_pairs={{0,16},{1,17},{2,18},{3,19},{4,20},{5,21},{6,22},{7,23},{8,24},{9,... | collective-permute-start | bytes 2228360 | tf_op jit(solution)/shard_map/ppermute | solution.py:306
  366.1 32.9 %copy-start.62 = (bf16[512,768]{1,0:T(8,128)(2,1)}, bf16[512,768]{1,0:T(8,128)(2,1)S(1)}, u32[]{:S(2)}) copy-start(bf16[512,768]{1,0:T(8,128)(2,1)S(1)} %collective-permute-done.16) | copy-start | bytes 2359300
  419.8 72.7 %collective-permute-start.34 = (bf16[384,3072]{1,0:T(8,128)(2,1)S(1)}, bf16[384,3072]{1,0:T(8,128)(2,1)S(1)}, u32[]{:S(2)}, u32[]{:S(2)}) collective-permute-start(bf16[384,3072]{1,0:T(8,128)(2,1)S(1)} %slice.422), channel_id=1, source_target_pairs={{0,1},{1,0},{2,3},{3,2},{4,5},{5,4},{6,7},{7,6},{8,9},{9,8},{10,11... | collective-permute-start | bytes 7077896 | tf_op jit(solution)/shard_map/ppermute | solution.py:306
  421.7 14.1 %collective-permute-start.40 = (bf16[96,3072]{1,0:T(8,128)(2,1)S(1)}, bf16[96,3072]{1,0:T(8,128)(2,1)S(1)}, u32[]{:S(2)}, u32[]{:S(2)}) collective-permute-start(bf16[96,3072]{1,0:T(8,128)(2,1)S(1)} %slice.436), channel_id=1, source_target_pairs={{0,8},{1,9},{2,10},{3,11},{4,12},{5,13},{6,14},{7,15},{8,0},{9,1},... | collective-permute-start | bytes 1769480 | tf_op jit(solution)/shard_map/ppermute | solution.py:306
  425.4 65.4 %collective-permute-start.24 = (bf16[384,1152]{1,0:T(8,128)(2,1)S(1)}, bf16[384,1152]{1,0:T(8,128)(2,1)S(1)}, u32[]{:S(2)}, u32[]{:S(2)}) collective-permute-start(bf16[384,1152]{1,0:T(8,128)(2,1)S(1)} %slice.393), channel_id=1, source_target_pairs={{0,1},{1,0},{2,3},{3,2},{4,5},{5,4},{6,7},{7,6},{8,9},{9,8},{10,11... | collective-permute-start | bytes 2654216 | tf_op jit(solution)/shard_map/ppermute | solution.py:306
  436.0 66.4 %collective-permute-start.41 = (bf16[48,3072]{1,0:T(8,128)(2,1)S(1)}, bf16[48,3072]{1,0:T(8,128)(2,1)S(1)}, u32[]{:S(2)}, u32[]{:S(2)}) collective-permute-start(bf16[48,3072]{1,0:T(8,128)(2,1)S(1)} %slice.438), channel_id=1, source_target_pairs={{0,16},{1,17},{2,18},{3,19},{4,20},{5,21},{6,22},{7,23},{8,24},{9,... | collective-permute-start | bytes 884744 | tf_op jit(solution)/shard_map/ppermute | solution.py:306
  491.1 10.0 %collective-permute-start.25 = (bf16[192,1152]{1,0:T(8,128)(2,1)S(1)}, bf16[192,1152]{1,0:T(8,128)(2,1)S(1)}, u32[]{:S(2)}, u32[]{:S(2)}) collective-permute-start(bf16[192,1152]{1,0:T(8,128)(2,1)S(1)} %slice.395), channel_id=1, source_target_pairs={{0,4},{1,5},{2,6},{3,7},{4,0},{5,1},{6,2},{7,3},{8,12},{9,13},{10,... | collective-permute-start | bytes 1327112 | tf_op jit(solution)/shard_map/ppermute | solution.py:306
  493.5 32.8 %collective-permute-start.35 = (bf16[192,3072]{1,0:T(8,128)(2,1)S(1)}, bf16[192,3072]{1,0:T(8,128)(2,1)S(1)}, u32[]{:S(2)}, u32[]{:S(2)}) collective-permute-start(bf16[192,3072]{1,0:T(8,128)(2,1)S(1)} %slice.424), channel_id=1, source_target_pairs={{0,4},{1,5},{2,6},{3,7},{4,0},{5,1},{6,2},{7,3},{8,12},{9,13},{10,... | collective-permute-start | bytes 3538952 | tf_op jit(solution)/shard_map/ppermute | solution.py:306
  501.2 5.1 collective-permute-start.26
  502.5 25.5 %collective-permute-start.42 = (bf16[48,1536]{1,0:T(8,128)(2,1)S(1)}, bf16[48,1536]{1,0:T(8,128)(2,1)S(1)}, u32[]{:S(2)}, u32[]{:S(2)}) collective-permute-start(bf16[48,1536]{1,0:T(8,128)(2,1)S(1)} %slice.440), channel_id=1, source_target_pairs={{0,1},{1,0},{2,3},{3,2},{4,5},{5,4},{6,7},{7,6},{8,9},{9,8},{10,11... | collective-permute-start | bytes 442376 | tf_op jit(solution)/shard_map/ppermute | solution.py:306
  506.4 22.3 %collective-permute-start.27 = (bf16[48,1152]{1,0:T(8,128)(2,1)S(1)}, bf16[48,1152]{1,0:T(8,128)(2,1)S(1)}, u32[]{:S(2)}, u32[]{:S(2)}) collective-permute-start(bf16[48,1152]{1,0:T(8,128)(2,1)S(1)} %slice.399), channel_id=1, source_target_pairs={{0,16},{1,17},{2,18},{3,19},{4,20},{5,21},{6,22},{7,23},{8,24},{9,... | collective-permute-start | bytes 331784 | tf_op jit(solution)/shard_map/ppermute | solution.py:306
  526.8 12.2 %collective-permute-start.36 = (bf16[96,3072]{1,0:T(8,128)(2,1)S(1)}, bf16[96,3072]{1,0:T(8,128)(2,1)S(1)}, u32[]{:S(2)}, u32[]{:S(2)}) collective-permute-start(bf16[96,3072]{1,0:T(8,128)(2,1)S(1)} %slice.426), channel_id=1, source_target_pairs={{0,8},{1,9},{2,10},{3,11},{4,12},{5,13},{6,14},{7,15},{8,0},{9,1},... | collective-permute-start | bytes 1769480 | tf_op jit(solution)/shard_map/ppermute | solution.py:306
  539.2 16.4 %collective-permute-start.37 = (bf16[48,3072]{1,0:T(8,128)(2,1)S(1)}, bf16[48,3072]{1,0:T(8,128)(2,1)S(1)}, u32[]{:S(2)}, u32[]{:S(2)}) collective-permute-start(bf16[48,3072]{1,0:T(8,128)(2,1)S(1)} %slice.428), channel_id=1, source_target_pairs={{0,16},{1,17},{2,18},{3,19},{4,20},{5,21},{6,22},{7,23},{8,24},{9,... | collective-permute-start | bytes 884744 | tf_op jit(solution)/shard_map/ppermute | solution.py:306
  (97 other events, 546.0 us)

commit v3 on v2

v3 whole, which is shorter than its diff:
```python
import functools
import math

import jax
import jax.numpy as jnp
from jax import lax
from jax.experimental import pallas as pl
from jax.experimental.pallas import tpu as pltpu
from jax.sharding import PartitionSpec as P

EPSILON = 1e-06
AXES = ("dp", "mp")
BF16 = jnp.bfloat16
F32 = jnp.float32
VMEM_LIMIT = 60 * 1024 * 1024
FFN_BLOCK = 384
BACK_PARTS = 1
COST_CUT = 20


def highest_dot(left_side, right_side):
    return jnp.dot(left_side, right_side, precision=lax.Precision.HIGHEST)


def silu_parts(values):
    sigma = jax.nn.sigmoid(values)
    return (values * sigma, sigma * (1.0 + values * (1.0 - sigma)))


def dot_f32(left_side, right_side):
    return jnp.dot(left_side, right_side, preferred_element_type=F32)


def dot_nt(left_side, right_side):
    return lax.dot_general(
        left_side, right_side, (((1,), (1,)), ((), ())), preferred_element_type=F32
    )

def lane_mix(first, second, odd):
    lane = lax.broadcasted_iota(jnp.int32, first.shape, 1)
    keep = (lane >= 64) if odd else (lane < 64)
    return jnp.where(keep, first, second)


def nt(left_side, right_side):
    return lax.dot_general(
        left_side, right_side, (((1,), (1,)), ((), ())), preferred_element_type=F32
    )


def attention_forward_body(
    pair_mix_ref, q_ref, left_ref, hot_ref, k_own_ref, k_near_ref, v_own_ref, v_near_ref,
    right_own_ref, right_near_ref, pen_own_ref, pen_near_ref,
    attended_ref, inverse_ref, probs_ref,
):
    rows = q_ref.shape[0]
    step = 256
    out_tiles = []
    left = left_ref[...].astype(F32)
    for odd in range(2):
        mix = pair_mix_ref[0, odd : odd + 1, :]
        left_mixed = (left * mix).astype(BF16)
        q_side = jnp.concatenate([left_mixed, lane_mix(q_ref[...], hot_ref[...], odd)], axis=1)
        k_own = jnp.concatenate(
            [right_own_ref[...], lane_mix(k_own_ref[...], pen_own_ref[...], odd)], axis=1
        )
        k_near = jnp.concatenate(
            [right_near_ref[...], lane_mix(k_near_ref[...], pen_near_ref[...], odd)], axis=1
        )
        v_own = lane_mix(v_own_ref[...], jnp.ones_like(v_own_ref[...]), odd)
        v_near = lane_mix(v_near_ref[...], jnp.ones_like(v_near_ref[...]), odd)
        tiles = []
        for start in range(0, rows, step):
            block = q_side[start : start + step]
            s_own = nt(block, k_own)
            s_near = nt(block, k_near)
            top = jnp.maximum(
                jnp.max(s_own, axis=1, keepdims=True), jnp.max(s_near, axis=1, keepdims=True)
            )
            e_own = jnp.exp(s_own - top).astype(BF16)
            e_near = jnp.exp(s_near - top).astype(BF16)
            probs_ref[odd, start : start + step, :rows] = e_own
            probs_ref[odd, start : start + step, rows:] = e_near
            tiles.append(
                jnp.dot(e_own, v_own, preferred_element_type=F32)
                + jnp.dot(e_near, v_near, preferred_element_type=F32)
            )
        out_tiles.append(jnp.concatenate(tiles, axis=0))
    sums = lane_mix(out_tiles[1], out_tiles[0], False)
    sums = pltpu.roll(sums, 64, 1)
    inverse = 1.0 / sums
    attended_ref[...] = (lane_mix(out_tiles[0], out_tiles[1], False) * inverse).astype(BF16)
    inverse_ref[...] = inverse


def attention_backward_body(
    first, last, pair_mix_ref, grad_ref, attended_ref, inverse_ref, probs_ref, q_ref, left_ref,
    k_own_ref, k_near_ref, v_own_ref, v_near_ref, right_own_ref, right_near_ref,
    pen_own_ref, pen_near_ref, *rest
):
    if not first:
        right_start, left_start = rest[:2]
        rest = rest[2:]
    d_q_ref, own_out, near_out, right_out, left_out, d_mix_ref = rest[:6]
    scores_ref, right_sum_ref, left_sum_ref, left_t_ref = rest[-4:]
    pair = pl.program_id(0)
    rows = q_ref.shape[0]
    step = 256
    wide = own_out.shape[1] // 2

    @pl.when(pair == 0)
    def _():
        left_t_ref[...] = left_ref[...].T
        right_sum_ref[...] = jnp.zeros_like(right_sum_ref) if first else right_start[...]
        left_sum_ref[...] = jnp.zeros_like(left_sum_ref) if first else left_start[...]

    scaled = (grad_ref[...].astype(F32) * inverse_ref[...]).astype(BF16)
    products = scaled.astype(F32) * attended_ref[...].astype(F32)
    scaled_t = scaled.T
    q_t = q_ref[...].T
    lane = lax.broadcasted_iota(jnp.int32, products.shape, 1)
    left = left_ref[...].astype(F32)
    left_t = left_t_ref[...].astype(F32)
    d_q, dk_t, dv_t = [], [], []
    for odd in range(2):
        mine = (lane >= 64) if odd else (lane < 64)
        delta = -jnp.sum(jnp.where(mine, products, 0.0), axis=1, keepdims=True)
        high = delta.astype(BF16).astype(F32)
        low = delta - high
        at = 0 if odd else 64
        extra = jnp.where(lane == at, high, jnp.where(lane == at + 1, low, 0.0)).astype(BF16)
        grad_side = jnp.where(mine, scaled, extra)
        mix = pair_mix_ref[0, odd : odd + 1, :]
        k_own = jnp.concatenate(
            [right_own_ref[...], lane_mix(k_own_ref[...], pen_own_ref[...], odd)], axis=1
        )
        k_near = jnp.concatenate(
            [right_near_ref[...], lane_mix(k_near_ref[...], pen_near_ref[...], odd)], axis=1
        )
        v_own = lane_mix(v_own_ref[...], jnp.ones_like(v_own_ref[...]), odd)
        v_near = lane_mix(v_near_ref[...], jnp.ones_like(v_near_ref[...]), odd)
        for start in range(0, rows, step):
            block = grad_side[start : start + step]
            own = nt(block, v_own).astype(BF16) * probs_ref[odd, start : start + step, :rows]
            near = nt(block, v_near).astype(BF16) * probs_ref[odd, start : start + step, rows:]
            scores_ref[start : start + step, :rows] = own
            scores_ref[start : start + step, rows:] = near
        d_query = jnp.dot(
            scores_ref[:, :rows], k_own, preferred_element_type=F32
        ) + jnp.dot(scores_ref[:, rows:], k_near, preferred_element_type=F32)
        width = left.shape[1]
        d_q.append(d_query[:, width:])
        d_pair = d_query[:, :width]
        left_sum_ref[...] += d_pair * mix
        d_mix_ref[0, odd : odd + 1, :] = jnp.sum(d_pair * left, axis=0, keepdims=True)
        mixed_t = (left_t * jnp.transpose(mix)).astype(BF16)
        low_row = 64 * odd
        q_side = jnp.concatenate([mixed_t, q_t[low_row : low_row + 64]], axis=0)
        d_key = jnp.dot(q_side, scores_ref[...], preferred_element_type=F32)
        right_sum_ref[...] += d_key[:width]
        dk_t.append(d_key[width:])
        dv_t.append(
            jnp.dot(
                scaled_t[low_row : low_row + 64], probs_ref[odd], preferred_element_type=F32
            )
        )
    d_q_ref[...] = (lane_mix(d_q[0], d_q[1], False) * 0.125).astype(BF16)
    for base, parts in ((0, dk_t), (wide, dv_t)):
        both = jnp.concatenate(parts, axis=0).T.astype(BF16)
        column = pl.multiple_of(base + pair * 128, 128)
        own_out[:, pl.ds(column, 128)] = both[:rows]
        near_out[:, pl.ds(column, 128)] = both[rows:]

    @pl.when(pair == pl.num_programs(0) - 1)
    def _():
        if last:
            right_out[...] = right_sum_ref[...].T.astype(BF16)
        else:
            right_out[...] = right_sum_ref[...]
        left_out[...] = left_sum_ref[...].astype(left_out.dtype)


def whole(array):
    zeros = (0,) * array.ndim
    return pl.BlockSpec(array.shape, lambda *_: zeros)


def attention_forward(
    pair_mix, queries, left, hot, kv_own, kv_near, right_own, right_near, pen_own, pen_near
):
    rows, width = queries.shape
    pairs = width // 128
    pair_width = left.shape[1]
    column = pl.BlockSpec((rows, 128), lambda p: (0, p))
    value_column = pl.BlockSpec((rows, 128), lambda p: (0, pairs + p))
    operands = [
        pair_mix, queries, left, hot, kv_own, kv_near, kv_own, kv_near, right_own, right_near,
        pen_own, pen_near,
    ]
    return call(
        attention_forward_body,
        operands,
        [
            pl.BlockSpec((1, 2, pair_width), lambda p: (p, 0, 0)), column, whole(left), whole(hot),
            column, column, value_column, value_column, whole(right_own), whole(right_near),
            whole(pen_own), whole(pen_near),
        ],
        [
            shaped((rows, width)), shaped((rows, width), F32),
            shaped((2 * pairs, rows, 2 * rows)),
        ],
        [column, column, pl.BlockSpec((2, rows, 2 * rows), lambda p: (p, 0, 0))],
        [],
        2 * 2 * pairs * rows * 2 * rows * 512,
        "attention_forward",
        (pairs,),
    )


def attention_backward(
    part, parts, pair_mix, grad, attended, inverse, probs, queries, left, kv_own, kv_near,
    right_own, right_near, pen_own, pen_near, *starts
):
    rows, width = queries.shape
    pairs = width // 128
    here = pairs // parts
    pair_width = left.shape[1]
    first, last = part == 0, part == parts - 1
    at = lambda p: part * here + p
    column = pl.BlockSpec((rows, 128), lambda p: (0, at(p)))
    value_column = pl.BlockSpec((rows, 128), lambda p: (0, pairs + at(p)))
    own_column = pl.BlockSpec((rows, 128), lambda p: (0, p))
    mix = pl.BlockSpec((1, 2, pair_width), lambda p: (at(p), 0, 0))
    mix_out = pl.BlockSpec((1, 2, pair_width), lambda p: (p, 0, 0))
    both = shaped((rows, 2 * 128 * here))
    if last:
        sums = [shaped((2 * rows, pair_width)), shaped((rows, pair_width))]
    else:
        sums = [shaped((pair_width, 2 * rows), F32), shaped((rows, pair_width), F32)]
    operands = [
        pair_mix, grad, attended, inverse, probs, queries, left, kv_own, kv_near, kv_own,
        kv_near, right_own, right_near, pen_own, pen_near, *starts,
    ]
    return call(
        functools.partial(attention_backward_body, first, last),
        operands,
        [
            mix, column, column, column,
            pl.BlockSpec((2, rows, 2 * rows), lambda p: (at(p), 0, 0)),
            column, whole(left), column, column, value_column, value_column,
            whole(right_own), whole(right_near), whole(pen_own), whole(pen_near),
        ]
        + [whole(a) for a in starts],
        [shaped((rows, 128 * here)), both, both, *sums, shaped((here, 2, pair_width), F32)],
        [own_column, whole(both), whole(both), *[whole(a) for a in sums], mix_out],
        [
            pltpu.VMEM((rows, 2 * rows), BF16),
            pltpu.VMEM((pair_width, 2 * rows), F32),
            pltpu.VMEM((rows, pair_width), F32),
            pltpu.VMEM((pair_width, rows), BF16),
        ],
        2 * 2 * here * rows * 2 * rows * 1000,
        "attention_backward",
        (here,),
    )


def norm_parts(values):
    centered = values - jnp.mean(values, axis=-1, keepdims=True)
    inverse = lax.rsqrt(jnp.mean(centered * centered, axis=-1, keepdims=True) + EPSILON)
    return centered * inverse, inverse


def tn(left_side, right_side):
    return lax.dot_general(
        left_side, right_side, (((0,), (0,)), ((), ())), preferred_element_type=F32
    )


def fetch(pieces, target, sems, at_ref, cut):
    copies = []
    for r, piece in enumerate(pieces):
        row = pl.multiple_of((at_ref[0] ^ r) * cut, cut)
        copy = pltpu.make_async_copy(piece, target.at[..., pl.ds(row, cut), :], sems.at[r])
        copy.start()
        copies.append(copy)
    return copies


def qkv_body(at_ref, x_ref, member_ref, mod_ref, own_ref, *rest):
    pieces, (q_ref, kvr_ref, normed_ref), (other, sems) = rest[:2], rest[2:5], rest[5:]
    width = x_ref.shape[1]
    half = width // 2
    copies = fetch(pieces, other, sems, at_ref, width // 2)
    mods = jnp.dot(member_ref[...], mod_ref[...], preferred_element_type=F32)
    x_hat, _ = norm_parts(x_ref[...].astype(F32))
    normed = (x_hat * (1.0 + mods[:, width:]) + mods[:, :width]).astype(BF16)
    normed_ref[...] = normed

    def put(weights, low):
        q = jnp.dot(normed, weights[0], preferred_element_type=F32).astype(BF16)
        q_ref[:, low : low + half] = (q.astype(F32) * 0.125).astype(BF16)
        for k in (1, 2):
            first = (k - 1) * width + low
            kvr_ref[:, first : first + half] = jnp.dot(
                normed, weights[k], preferred_element_type=F32
            ).astype(BF16)

    put(own_ref, 0)
    for copy in copies:
        copy.wait()
    put(other, half)


def branch_body(
    attended_ref, own_ref, other_ref, x_ref, member_ref, mod_ref, middle_ref, branch_ref, normed_ref
):
    width = x_ref.shape[1]
    half = width // 2
    member = member_ref[...]

    def mods(k):
        return jnp.dot(
            member, mod_ref[:, k * width : (k + 1) * width], preferred_element_type=F32
        )

    branch = jnp.dot(attended_ref[:, :half], own_ref[...], preferred_element_type=F32)
    branch += jnp.dot(attended_ref[:, half:], other_ref[...], preferred_element_type=F32)
    branch_ref[...] = branch
    middle = x_ref[...].astype(F32) + mods(2) * branch
    middle_ref[...] = middle
    m_hat, _ = norm_parts(middle)
    normed_ref[...] = (m_hat * (1.0 + mods(4)) + mods(3)).astype(BF16)


def ffn_body(
    normed_ref, dout_ref, member_ref, mod_ref, moved_ref, gate_up_ref, down_ref,
    ffn_out_ref, d_normed_out_ref, normed_t_ref, d_ffn_t_ref, d_gate_ref, d_up_ref, hidden_ref,
    ffn_ref, d_normed_ref, d_ffn_ref,
):
    step = pl.program_id(0)
    last = pl.num_programs(0) - 1

    @pl.when(step == 0)
    def _():
        scale = jnp.dot(member_ref[...], mod_ref[...], preferred_element_type=F32)
        d_ffn_ref[...] = (scale * dout_ref[...].astype(F32)).astype(BF16)
        normed_t_ref[...] = nt(moved_ref[...], normed_ref[...]).astype(BF16)
        d_ffn_t_ref[...] = nt(moved_ref[...], d_ffn_ref[...]).astype(BF16)

    normed, d_ffn = normed_ref[...], d_ffn_ref[...]
    w_gate, w_up, w_down = gate_up_ref[0], gate_up_ref[1], down_ref[...]
    gate = jnp.dot(normed, w_gate, preferred_element_type=F32)
    up = jnp.dot(normed, w_up, preferred_element_type=F32)
    d_hidden = nt(d_ffn, w_down)
    sigma = jax.nn.sigmoid(gate)
    value = gate * sigma
    hid = (value * up).astype(BF16)
    d_up = (d_hidden * value).astype(BF16)
    d_gate = (d_hidden * up * (sigma + value * (1.0 - sigma))).astype(BF16)
    hidden_ref[...] = hid
    d_up_ref[...] = d_up
    d_gate_ref[...] = d_gate
    ffn = jnp.dot(hid, w_down, preferred_element_type=F32)
    d_normed = nt(d_gate, w_gate) + nt(d_up, w_up)

    @pl.when(step == 0)
    def _():
        ffn_ref[...] = ffn
        d_normed_ref[...] = d_normed

    @pl.when(jnp.logical_and(step > 0, step < last))
    def _():
        ffn_ref[...] += ffn
        d_normed_ref[...] += d_normed

    @pl.when(step == last)
    def _():
        ffn_out_ref[...] = (ffn_ref[...] + ffn).astype(ffn_out_ref.dtype)
        d_normed_out_ref[...] = (d_normed_ref[...] + d_normed).astype(d_normed_out_ref.dtype)


def ffn_grad_body(
    normed_t_ref, normed_t_far_ref, d_ffn_t_ref, d_ffn_t_far_ref,
    d_gate_ref, d_gate_far_ref, d_up_ref, d_up_far_ref, hidden_ref, hidden_far_ref,
    keep_ref, send_ref,
):
    half = normed_t_ref.shape[0] // 2
    normed_t = (normed_t_ref, normed_t_far_ref)
    d_ffn_t = (d_ffn_t_ref, d_ffn_t_far_ref)
    for k, (left_t, near, far) in enumerate(
        (
            (normed_t, d_gate_ref, d_gate_far_ref),
            (normed_t, d_up_ref, d_up_far_ref),
            (d_ffn_t, hidden_ref, hidden_far_ref),
        )
    ):
        total = jnp.dot(left_t[0][...], near[...], preferred_element_type=F32) + jnp.dot(
            left_t[1][...], far[...], preferred_element_type=F32
        )
        keep_ref[k] = total[:half].astype(BF16)
        send_ref[k] = total[half:].astype(BF16)


def mix_body(middle_ref, ffn_ref, ffn_far_ref, dout_ref, member_ref, mod_ref, mixed_ref, d_mods_ref):
    member = member_ref[...]
    ffn = ffn_ref[...] + ffn_far_ref[...].astype(F32)
    scale = jnp.dot(member, mod_ref[...], preferred_element_type=F32)
    mixed_ref[...] = (middle_ref[...] + scale * ffn).astype(BF16)
    part = tn(member, (dout_ref[...].astype(F32) * ffn).astype(BF16))

    @pl.when(pl.program_id(0) == 0)
    def _():
        d_mods_ref[...] = part

    @pl.when(pl.program_id(0) > 0)
    def _():
        d_mods_ref[...] += part


def middle_back_body(
    d_normed_ref, d_normed_far_ref, middle_ref, branch_ref, dout_ref, member_ref,
    mod_ref, own_ref, other_ref, d_middle_ref, d_attended_ref, d_attn_ref, d_mods_ref
):
    step = pl.program_id(0)
    rows, width = d_normed_ref.shape
    half = width // 2

    @pl.when(step == 0)
    def _():
        d_mods_ref[...] = jnp.zeros_like(d_mods_ref)

    member = member_ref[...]

    def mods(k):
        return jnp.dot(
            member, mod_ref[:, k * width : (k + 1) * width], preferred_element_type=F32
        )

    def add_mods(k, values):
        d_mods_ref[:, k * width : (k + 1) * width] += tn(member, values.astype(BF16))

    middle = middle_ref[...]
    m_hat, inverse = norm_parts(middle)
    d_normed = d_normed_ref[...] + d_normed_far_ref[...].astype(F32)
    add_mods(1, d_normed)
    add_mods(2, d_normed * m_hat)
    d_hat = d_normed * (1.0 + mods(4))
    d_middle = dout_ref[...].astype(F32) + inverse * (
        d_hat
        - jnp.mean(d_hat, axis=-1, keepdims=True)
        - m_hat * jnp.mean(d_hat * m_hat, axis=-1, keepdims=True)
    )
    d_middle_ref[...] = d_middle
    add_mods(0, d_middle * branch_ref[...])
    d_attn = (mods(2) * d_middle).astype(BF16)
    d_attn_ref[...] = d_attn
    d_attended_ref[:, :half] = nt(d_attn, own_ref[...]).astype(BF16)

    d_attended_ref[:, half:] = nt(d_attn, other_ref[...]).astype(BF16)


def attention_grad_body(
    q_ref, own_ref, far_ref, normed_ref, d_attn_ref, attended_ref, moved_ref,
    d_proj_ref, keep_qk_ref, send_qk_ref, keep_vo_ref, send_vo_ref
):
    width = normed_ref.shape[1]
    half = width // 2
    d_proj_ref[:, :width] = q_ref[...]
    d_proj_ref[:, width:] = (own_ref[...].astype(F32) + far_ref[...].astype(F32)).astype(BF16)
    turned = nt(moved_ref[...], normed_ref[...]).astype(BF16)
    for j in range(4):
        if j == 3:
            turned = nt(moved_ref[...], d_attn_ref[...]).astype(BF16)
            right_side = attended_ref[...]
        else:
            right_side = d_proj_ref[:, j * width : (j + 1) * width]
        total = jnp.dot(turned, right_side, preferred_element_type=F32).astype(BF16)
        keep_ref, send_ref = (keep_qk_ref, send_qk_ref) if j < 2 else (keep_vo_ref, send_vo_ref)
        for k in range(2):
            keep_ref[k, j % 2] = total[:half, k * half : (k + 1) * half]
            send_ref[k, j % 2] = total[half:, k * half : (k + 1) * half]


def deliver_body(*refs):
    count = len(refs) // 2
    for k in range(count):
        refs[count + k][...] = refs[k][...]


def input_back_body(
    at_ref, d_proj_ref, x_ref, d_middle_ref, member_ref, mod_ref, own_ref, *rest
):
    pieces, (grad_ref, d_mods_ref), (other, sems) = rest[:2], rest[2:4], rest[4:]
    width = x_ref.shape[1]
    half = width // 2
    copies = fetch(pieces, other, sems, at_ref, width // 2)
    d_normed = nt(d_proj_ref[:, :half], own_ref[0])
    for j in (1, 2):
        d_normed += nt(d_proj_ref[:, j * width : j * width + half], own_ref[j])
    for copy in copies:
        copy.wait()
    for j in range(3):
        d_normed += nt(d_proj_ref[:, j * width + half : (j + 1) * width], other[j])
    member = member_ref[...]
    scale = jnp.dot(member, mod_ref[:, width:], preferred_element_type=F32)
    x_hat, inverse = norm_parts(x_ref[...].astype(F32))
    d_mods_ref[:, :width] = tn(member, d_normed.astype(BF16))
    d_mods_ref[:, width:] = tn(member, (d_normed * x_hat).astype(BF16))
    d_hat = d_normed * (1.0 + scale)
    grad_ref[...] = (
        d_middle_ref[...]
        + inverse
        * (
            d_hat
            - jnp.mean(d_hat, axis=-1, keepdims=True)
            - x_hat * jnp.mean(d_hat * x_hat, axis=-1, keepdims=True)
        )
    ).astype(BF16)


ANYWHERE = pl.BlockSpec(memory_space=pl.ANY)
IN_SMEM = pl.BlockSpec(memory_space=pltpu.SMEM)


def call(body, operands, specs, outs, out_specs, scratch, flops, name, grid=(1,)):
    moved = sum(math.prod(a.shape) * a.dtype.itemsize for a in operands) + sum(
        math.prod(o.shape) * jnp.dtype(o.dtype).itemsize for o in outs
    )
    return pl.pallas_call(
        body,
        grid=grid,
        in_specs=specs,
        out_specs=out_specs,
        out_shape=outs,
        scratch_shapes=scratch,
        compiler_params=pltpu.CompilerParams(vmem_limit_bytes=VMEM_LIMIT),
        cost_estimate=pl.CostEstimate(
            flops=flops // COST_CUT, bytes_accessed=moved // COST_CUT, transcendentals=0
        ),
        name=name,
    )(*operands)


def shaped(shape, dtype=BF16):
    return jax.ShapeDtypeStruct(shape, dtype)


def make_moves(dp_count):
    def pairs(target):
        moved = []
        for d in range(dp_count):
            for m in range(2):
                to_d, to_m = target(d, m)
                moved.append((d * 2 + m, to_d * 2 + to_m))
        return moved

    def mover(target):
        table = pairs(target)
        return lambda array: lax.ppermute(array, AXES, table)

    turn = mover(lambda d, m: ((d & ~1) | m, d & 1))
    turn_far = mover(lambda d, m: ((d & ~1) | m, 1 - (d & 1)))
    across = mover(lambda d, m: (d, 1 - m))

    def flip(bit):
        return mover(lambda d, m: (d ^ (1 << bit), m))

    def to(mask, over):
        return mover(lambda d, m: (d ^ mask, m ^ over))

    return turn, turn_far, across, flip, to


def shards(
    tokens,
    pair_left,
    pair_right,
    chain_len,
    chain_time,
    chain_arch,
    cath_table,
    time_weight,
    mod_weight,
    mod_bias,
    qkv_weight,
    pair_weight,
    out_weight,
    gate_up_weight,
    down_weight,
    cotangent,
):
    dp_count = lax.axis_size("dp")
    bits = dp_count.bit_length() - 1
    turn, turn_far, across, flip, to = make_moves(dp_count)
    core_swap = flip(0)
    dp_at = lax.axis_index("dp")
    mp_at = lax.axis_index("mp")
    core = dp_at & 1
    rows, width = tokens.shape
    slots = chain_len.shape[1]
    half_heads = pair_weight.shape[1]
    heads = 2 * half_heads
    pair_width = pair_left.shape[1]
    cond_width = time_weight.shape[0]
    half = width // 2
    hidden = down_weight.shape[0]

    def after(array, *earlier):
        return lax.optimization_barrier((array, *earlier))[0]

    def beside(made, *received):
        return lax.optimization_barrier((*made, *received))[: len(made)]

    held_chains = jnp.concatenate(
        [chain_len.astype(F32), chain_time, chain_arch.astype(F32)], axis=0
    )
    near_chains = core_swap(held_chains)

    cut = qkv_weight.shape[1] // 2
    pair_mix_other = across(pair_weight)
    qkv_y = across(lax.dynamic_slice_in_dim(qkv_weight, core * cut, cut, 1))
    x_in = turn(after(tokens, qkv_y, pair_mix_other))
    qkv_pieces = [qkv_y, core_swap(qkv_y)]
    right_own = turn(after(pair_right, x_in))
    left_in = turn(after(pair_left, x_in))
    out_other = across(after(out_weight, right_own))
    dout = turn(after(cotangent, right_own))
    dout_far = turn_far(after(cotangent, out_other))

    def ends_of(chains):
        return jnp.cumsum(chains[0].astype(jnp.int32))

    chains = jnp.where(core == mp_at, held_chains, near_chains)
    far_chains = jnp.where(core == mp_at, near_chains, held_chains)
    arches = chains[2].astype(jnp.int32)
    ends = ends_of(chains)
    times = jnp.concatenate([chains[1], far_chains[1]])

    def ids_of(part, ends=ends):
        positions = jnp.arange(rows, dtype=jnp.int32) + part * rows
        return jnp.sum((positions[:, None] >= ends[None, :]).astype(jnp.int32), axis=1)

    own_ids = ids_of(core)
    key_ids = jnp.concatenate([own_ids, ids_of(1 - core)])
    chain_numbers = jnp.arange(slots, dtype=jnp.int32)
    doubled = jnp.concatenate([chain_numbers, chain_numbers])[None, :]
    member = (own_ids[:, None] == doubled).astype(BF16)
    member_far = (ids_of(core, ends_of(far_chains))[:, None] == doubled).astype(BF16)
    lanes = jnp.arange(128, dtype=jnp.int32)[None, :] & 63
    hot = (own_ids[:, None] == lanes).astype(BF16)
    pens = jnp.where((key_ids[:, None] != lanes) & (lanes <= slots), -1e30, 0.0).astype(BF16)
    pen_own, pen_near = pens[:rows], pens[rows:]

    half_cond = cond_width // 2
    frequency = jnp.exp(jnp.arange(half_cond, dtype=F32) * (-math.log(10000.0) / half_cond))
    angles = times[:, None] * 1000.0 * frequency[None, :]
    time_embed = jnp.concatenate([jnp.sin(angles), jnp.cos(angles)], axis=1).astype(BF16)
    both_arches = jnp.concatenate([arches, far_chains[2].astype(jnp.int32)])
    arch_onehot = (
        both_arches[:, None] == jnp.arange(cath_table.shape[0], dtype=jnp.int32)[None, :]
    ).astype(F32)
    cond_pre = dot_f32(time_embed, time_weight) + highest_dot(arch_onehot, cath_table.astype(F32))
    cond_value, cond_slope = silu_parts(cond_pre)
    cond_act = cond_value.astype(BF16)
    chain_mod = dot_f32(cond_act, mod_weight) + mod_bias.astype(F32)[None, :]
    mod_high = lax.reduce_precision(chain_mod, 8, 7)
    mod_low = (chain_mod - mod_high).astype(BF16)
    mod_high = mod_high.astype(BF16)
    mods = jnp.concatenate([mod_high[:slots], mod_low[:slots]], axis=0)
    gate_far = jnp.concatenate([mod_high[slots:], mod_low[slots:]], axis=0)[:, 5 * width :]
    time_embed, cond_act, cond_slope = time_embed[:slots], cond_act[:slots], cond_slope[:slots]

    order = [int(format(p, "0%db" % bits)[::-1], 2) for p in range(dp_count)]
    block_at = jnp.array(order, jnp.int32) ^ dp_at
    block_rows = width // dp_count
    source = (block_at[:, None] * block_rows + jnp.arange(block_rows)[None, :]).reshape(-1)
    moved = (source[:, None] == jnp.arange(width)[None, :]).astype(BF16)
    at = core.reshape(1).astype(jnp.int32)
    semaphores = pltpu.SemaphoreType.DMA

    mod_a = mods[:, : 2 * width]
    pair_mix = jnp.concatenate([pair_weight, pair_mix_other], axis=1).astype(F32)
    mix_rows = jnp.transpose(pair_mix).reshape(half_heads, 2, -1)
    queries, kv_own, normed_a = call(
        qkv_body,
        [at, after(x_in, moved, mods, hot, pens, member_far, gate_far), member, mod_a, qkv_weight,
         *qkv_pieces],
        [IN_SMEM] + [whole(a) for a in (x_in, member, mod_a, qkv_weight)] + [ANYWHERE] * 2,
        [shaped((rows, width)), shaped((rows, 2 * width)), shaped((rows, width))],
        [whole(shaped((rows, width))), whole(shaped((rows, 2 * width))),
         whole(shaped((rows, width)))],
        [pltpu.VMEM(qkv_weight.shape, BF16), semaphores((2,))],
        6 * rows * width * width,
        "project",
    )
    queries, kv_own = beside((queries, kv_own), right_own, left_in, mix_rows)
    kv_near = core_swap(kv_own)
    right_near = core_swap(right_own)
    keyed = (kv_own, kv_near, right_own, right_near, pen_own, pen_near)
    attended, inverse, probs = attention_forward(mix_rows, queries, left_in, hot, *keyed)
    wide = shaped((rows, width), F32)
    thin = shaped((rows, width))
    middle, branch, normed_f = call(
        branch_body,
        [attended, out_weight, out_other, x_in, member, mods],
        [whole(a) for a in (attended, out_weight, out_other, x_in, member, mods)],
        [wide, wide, thin],
        [whole(thin)] * 3,
        [],
        2 * rows * width * width,
        "branch",
    )

    normed_far = across(normed_f)
    gate_mod = mods[:, 5 * width :]
    block = FFN_BLOCK
    active = shaped((rows, hidden))
    turned = shaped((width, rows))

    def feed_forward(normed, dout, member, gate, sum_type):
        column = pl.BlockSpec((rows, block), lambda i: (0, i))
        summed = shaped((rows, width), sum_type)
        return call(
            ffn_body,
            [normed, dout, member, gate, moved, gate_up_weight, down_weight],
            [whole(a) for a in (normed, dout, member, gate, moved)]
            + [
                pl.BlockSpec((2, width, block), lambda i: (0, 0, i)),
                pl.BlockSpec((block, width), lambda i: (i, 0)),
            ],
            [summed, summed, turned, turned, active, active, active],
            [whole(thin), whole(thin), whole(turned), whole(turned), column, column, column],
            [
                pltpu.VMEM((rows, width), F32), pltpu.VMEM((rows, width), F32),
                pltpu.VMEM((rows, width), BF16),
            ],
            12 * rows * width * hidden,
            "feed_forward",
            (hidden // block,),
        )

    made = feed_forward(normed_f, dout, member, gate_mod, F32)
    ffn, d_normed_f, normed_t, d_ffn_t, d_gate, d_up, hid = made
    (normed_far,) = lax.optimization_barrier((normed_far, *made))[:1]
    ffn_for, d_normed_for, normed_t_far, d_ffn_t_far, d_gate_far, d_up_far, hid_far = feed_forward(
        normed_far, dout_far, member_far, gate_far, BF16
    )
    d_normed_far = across(d_normed_for)

    grad = shaped((3, half, hidden))
    grad_block = pl.BlockSpec((3, half, block), lambda i: (0, 0, i))
    column = pl.BlockSpec((rows, block), lambda i: (0, i))
    operands = [normed_t, normed_t_far, d_ffn_t, d_ffn_t_far]
    made = call(
        ffn_grad_body,
        operands + [d_gate, d_gate_far, d_up, d_up_far, hid, hid_far],
        [whole(a) for a in operands] + [column] * 6,
        [grad, grad],
        [grad_block, grad_block],
        [],
        12 * rows * width * hidden,
        "feed_forward_grads",
        (hidden // block,),
    )
    keep, send = beside(made, d_normed_far)
    far = core_swap(send)
    ffn_far = across(after(ffn_for, send))

    def plus(kept, received):
        return (kept.astype(F32) + received.astype(F32)).astype(BF16)

    def halves(array, upper):
        size = array.shape[-2] // 2
        return array[..., size:, :] if upper else array[..., :size, :]

    def y_part(kept, received):
        return plus(kept[1], received[1])

    def y_rest(kept, received):
        return plus(kept[0], received[0])

    def bit_part(kept, received):
        return plus(halves(kept, True), halves(received, True))

    def bit_rest(kept, received):
        return plus(halves(kept, False), halves(received, False))

    steps = 2
    row_block = pl.BlockSpec((rows // steps, width), lambda i: (i, 0))
    member_block = pl.BlockSpec((rows // steps, 2 * slots), lambda i: (i, 0))
    mods_early = shaped((2 * slots, 3 * width), F32)
    made = call(
        middle_back_body,
        [after(d_normed_f, send), d_normed_far, middle, branch, dout, member, mods, out_weight,
         out_other],
        [row_block] * 5 + [member_block, whole(mods), whole(out_weight), whole(out_other)],
        [wide, thin, thin, mods_early],
        [row_block, row_block, row_block, whole(mods_early)],
        [],
        4 * rows * width * width,
        "middle_back",
        (steps,),
    )
    d_middle, d_attended, d_attn, d_mods = beside(made, far)
    sent, rest = bit_part(keep, far), bit_rest(keep, far)
    got = flip(1)(sent)

    def core_half(summed, others):
        summed = summed + core_swap(summed)
        held = jnp.concatenate([summed.astype(BF16), *others], axis=1)
        cut = held.shape[1] // 2
        return lax.dynamic_slice_in_dim(held, core * cut, cut, 1)

    near_bits = [-1, 1] if bits > 1 else [-1]
    far_bits = list(range(2, bits))

    def several(group):
        moves = []
        for chosen in range(1, 1 << len(group)):
            mask, over = 0, 0
            for k, bit in enumerate(group):
                if chosen >> k & 1:
                    mask, over = (mask, 1) if bit < 0 else (mask | 1 << bit, over)
            moves.append((mask, over))
        return moves

    def gather_step(group, held):
        return jnp.concatenate(
            [held] + [to(mask, over)(held) for mask, over in several(group)], axis=0
        )

    def whole_columns(held):
        near = core_swap(held)
        return jnp.concatenate(
            [jnp.where(core == 0, held, near), jnp.where(core == 0, near, held)], axis=1
        )

    d_query, d_own, d_far, d_right, d_left, d_mix = attention_backward(
        0, 1, mix_rows, after(d_attended, sent), attended, inverse, probs, queries, left_in, *keyed
    )
    d_query, d_own, d_far, d_right, d_left = beside(
        (d_query, d_own, d_far, d_right, d_left), ffn_far
    )
    far_kv = core_swap(d_far)
    far_right = core_swap(d_right[rows:])
    left_grad = turn(d_left)

    mods_gate = shaped((2 * slots, width), F32)
    mixed, d_mods_gate = call(
        mix_body,
        [after(middle, d_far), ffn, ffn_far, dout, member, gate_mod],
        [row_block] * 4 + [member_block, whole(gate_mod)],
        [thin, mods_gate],
        [row_block, whole(mods_gate)],
        [],
        4 * rows * 16 * width,
        "mix",
        (steps,),
    )
    mixed, d_mods_gate = beside((mixed, d_mods_gate), far_kv, far_right)
    mixed = turn(mixed)
    right_grad = turn(plus(d_right[:rows], far_right))

    proj_grad = shaped((rows, 3 * width))
    pair_grad = shaped((2, 2, half, half))
    operands = [d_query, d_own, far_kv, after(normed_a, d_mods_gate), d_attn, attended, moved]
    outs = [proj_grad] + [pair_grad] * 4
    made = call(
        attention_grad_body,
        operands,
        [whole(a) for a in operands],
        outs,
        [whole(a) for a in outs],
        [],
        12 * rows * width * width,
        "attention_grads",
    )
    d_proj, keep_qk, send_qk, keep_vo, send_vo = beside(made, got, left_grad, right_grad)
    far_qk, far_vo = core_swap(send_qk), core_swap(send_vo)
    sent, rest = bit_part(rest, got), bit_rest(rest, got)
    got = flip(2)(after(sent, left_grad))
    sent_qk, sent_vo = y_part(keep_qk, far_qk), bit_part(keep_vo, far_vo)
    rest_qk, rest_vo = y_rest(keep_qk, far_qk), bit_rest(keep_vo, far_vo)
    got_qk, got_vo = across(sent_qk), flip(1)(sent_vo)
    mods_late = shaped((2 * slots, 2 * width), F32)
    operands = [at, after(d_proj, sent_qk, sent_vo), x_in, d_middle, member, mod_a, qkv_weight]
    made = call(
        input_back_body,
        [*operands, *qkv_pieces],
        [IN_SMEM] + [whole(a) for a in operands[1:]] + [ANYWHERE] * 2,
        [thin, mods_late],
        [whole(thin), whole(mods_late)],
        [pltpu.VMEM(qkv_weight.shape, BF16), semaphores((2,))],
        6 * rows * width * width,
        "input_back",
    )
    tokens_out, d_mods_a = beside(made, got_qk, got_vo, got, mixed)
    sent, rest = bit_part(rest, got), bit_rest(rest, got)
    token_gradient = turn(tokens_out)

    d_mix = d_mix.reshape(heads, -1)
    d_mix = jnp.concatenate(
        [
            jnp.where(mp_at == 0, d_mix[:half_heads], d_mix[half_heads:]),
            jnp.where(mp_at == 0, d_mix[half_heads:], d_mix[:half_heads]),
        ],
        axis=0,
    ).reshape(slots, -1)
    arch_low = (arches[:, None] == jnp.arange(128, dtype=jnp.int32)[None, :]).astype(BF16)
    modded = 6 * width
    mixed_to = modded + d_mix.shape[1]
    others = [cond_act, time_embed, cond_slope.astype(BF16), arch_low]
    filler = jnp.zeros((slots, -(mixed_to + 3 * cond_width + 128) % 256), BF16)
    held = core_half(
        jnp.concatenate(
            [d_mods_a[:slots], d_mods[:slots], d_mods_gate[:slots], d_mix], axis=1
        ),
        [*others, filler],
    )

    def together(*arrays):
        return lax.optimization_barrier(arrays)

    vo = plus(rest_vo, got_vo)
    qk = plus(rest_qk, got_qk)
    got_qk, got_vo = flip(1)(halves(qk, True)), across(vo[1])
    held = gather_step(near_bits, held)

    def finish(bit, kept, sent):
        while bit < bits:
            received = flip(bit)(sent)
            bit += 1
            if bit < bits:
                kept, sent = bit_rest(kept, received), bit_part(kept, received)
        return kept.astype(F32) + received.astype(F32)

    qkvo = jnp.concatenate(
        [plus(halves(qk, False), got_qk), plus(vo[0], got_vo)], axis=0
    )
    held, sent, qkvo, token_gradient = together(held, sent, qkvo, token_gradient)
    ffn_sum = finish(3, rest, sent)
    held = gather_step(far_bits, held)
    qkvo_sum = finish(2, halves(qkvo, False), halves(qkvo, True))

    held = whole_columns(held)
    mix_sum = jnp.sum(
        held[:, modded:mixed_to].astype(F32).reshape(dp_count, heads, -1), axis=0
    )
    mix_sum = jnp.where(mp_at == 0, mix_sum[:half_heads], mix_sum[half_heads:])
    taken = mix_sum.shape[1] // dp_count
    pair_sum = jnp.transpose(lax.dynamic_slice_in_dim(mix_sum, dp_at * taken, taken, 1))
    d_all = held[:, :modded]
    cond_all, time_all, slope_all, arch_all, _ = jnp.split(
        held[:, mixed_to:],
        [cond_width, 2 * cond_width, 3 * cond_width, 3 * cond_width + 128],
        axis=1,
    )
    mod_bias_sum = jnp.sum(d_all.astype(F32), axis=0)
    mod_weight_sum = dot_f32(jnp.transpose(cond_all), d_all)
    d_cond_pre = dot_nt(d_all, mod_weight) * slope_all.astype(F32)
    time_sum = highest_dot(jnp.transpose(time_all.astype(F32)), d_cond_pre)
    cath_sum = highest_dot(
        jnp.transpose(arch_all[:, : cath_table.shape[0]].astype(F32)), d_cond_pre
    )

    outs = [mixed, token_gradient, left_grad, right_grad]
    blocks = [pl.BlockSpec((rows // 4, a.shape[1]), lambda i: (i, 0)) for a in outs]
    mixed, token_gradient, left_grad, right_grad = call(
        deliver_body, outs, blocks, [shaped(a.shape) for a in outs], blocks, [], 0, "deliver", (4,)
    )
    return (
        mixed,
        token_gradient,
        left_grad,
        right_grad,
        cath_sum,
        time_sum,
        mod_weight_sum,
        mod_bias_sum,
        qkvo_sum[:3],
        pair_sum,
        jnp.transpose(qkvo_sum[3]),
        ffn_sum[:2],
        jnp.transpose(ffn_sum[2]),
    )


def solution(mesh):
    by_rows = P(AXES, None)
    placed = (
        by_rows,
        by_rows,
        by_rows,
        P("dp", None),
        P("dp", None),
        P("dp", None),
        P(),
        P(),
        P(),
        P(),
        P(None, None, "mp"),
        P(None, "mp"),
        P("mp", None),
        P(None, None, "mp"),
        P("mp", None),
        by_rows,
    )
    return jax.shard_map(
        shards,
        mesh=mesh,
        in_specs=placed,
        out_specs=(
            by_rows,
            by_rows,
            by_rows,
            by_rows,
            P(),
            P(),
            P(),
            P(),
            P(None, "dp", "mp"),
            P("dp", "mp"),
            P("mp", "dp"),
            P(None, "dp", "mp"),
            P("mp", "dp"),
        ),
        check_vma=False,
    )
```

time: 570 us -> 342 us (0.60)
  waiting for transfers between devices: 245 us -> 74.4 us
  Pallas kernels: 41.8 us -> 137 us
  matrix products: 97.7 us -> 7.09 us
  local copies, waits for them, and re-layouts: 62.7 us -> 18.4 us
  other arithmetic: 46 us -> 33.8 us
    ppermute x43 -> x41, waiting for transfers between devices: 245 us -> 74.4 us  [mover(): return lambda array: lax.ppermute(array, AXES, table)]
    pallas_call x2 -> x12, Pallas kernels: 41.8 us -> 137 us  [call(): pl.pallas_call(body, grid=grid, in_specs=specs, out_specs=out_specs, out_...]
    dot_general x16 -> x3, matrix products: 62 us -> 3.54 us  [dot_f32(): return jnp.dot(left_side, right_side, preferred_element_type=F32)]
    dot_general x8 -> x1, matrix products: 27.6 us -> 0.87 us  [dot_nt(): lax.dot_general(left_side, right_side, (((1,), (1,)), ((), ())), preferre...]
    unnamed x216 -> x68, local copies, waits for them, and re-layouts: 22.8 us -> 4.91 us
    select_n x5 -> x1, other arithmetic: 15.1 us -> 0.14 us  [whole_columns(): jnp.where(core == 0, held, near)]
    gather x4 -> x0, local copies, waits for them, and re-layouts: 9.91 us -> none  [row_blocks(): return jnp.take(turned, block_at, axis=0).reshape(width, rows)]
    transpose x6 -> x2, local copies, waits for them, and re-layouts: 10.9 us -> 1.37 us  [the longest x1 0.73 us: shards(): jnp.transpose(ffn_sum[2])]
  transfers between devices with their start and end apart: 43 -> 41, of which waited for: 17 -> 14; matrix products, arithmetic and copies ran while one was open for 24% -> 14% of each run, Pallas kernels for 7% -> 35%
where the time goes in v3:
time: 342 us; the launch traced here: 335 us
  Pallas kernels  137 us (40%)
  waiting for transfers between devices  74.4 us (22%)
  starting transfers between devices  63.2 us (18%)
  other arithmetic  33.8 us (10%)
  local copies, waits for them, and re-layouts  18.4 us (5%)
  matrix products  7.09 us (2%)
    pallas_call x12, Pallas kernels, call(): pl.pallas_call(body, grid=grid, in_specs=specs, out_specs=out_specs, out_...  137 us
    ppermute x41, waiting for transfers between devices, mover(): return lambda array: lax.ppermute(array, AXES, table)  74.4 us
    ppermute x41, starting transfers between devices, mover(): return lambda array: lax.ppermute(array, AXES, table)  63.2 us
    convert_element_type x11, other arithmetic, plus(): return (kept.astype(F32) + received.astype(F32)).astype(BF16)  18.9 us
  transfers between devices with their start and end apart: 41, of which 14 were waited for; matrix products, arithmetic and copies ran while one was open for 14% of the time, Pallas kernels for 35%

profile of v3, /device:TPU:1, one launch (start us, length us, event | category | flops | bytes accessed | tf_op | source)
XLA Modules:
  0.0 335.4 jit_solution(401718733851721589)
XLA Ops:
  4.2 2.8 collective-permute-start.1
  13.3 13.8 %collective-permute-done = bf16[256,6]{0,1:T(8,128)(2,1)S(1)} collective-permute-done((bf16[256,6]{0,1:T(8,128)(2,1)S(1)}, bf16[256,6]{0,1:T(8,128)(2,1)S(1)}, u32[]{:S(2)}, u32[]{:S(2)}) %collective-permute-start) | collective-permute-done | bytes 3104 | tf_op jit(solution)/shard_map/ppermute | solution.py:560
  27.1 3.8 %collective-permute-start.2 = (bf16[512,768]{1,0:T(8,128)(2,1)}, bf16[512,768]{1,0:T(8,128)(2,1)S(1)}, u32[]{:S(2)}, u32[]{:S(2)}) collective-permute-start(bf16[512,768]{1,0:T(8,128)(2,1)} %param.17), channel_id=1, source_target_pairs={{0,0},{1,2},{2,1},{3,3},{4,4},{5,6},{6,5},{7,7},{8,8},{9,10},{10,9... | collective-permute-start | bytes 2359304 | tf_op jit(solution)/shard_map/ppermute | solution.py:560
  32.4 8.4 %collective-permute-done.2.x_ref = bf16[512,768]{1,0:T(8,128)(2,1)S(1)} collective-permute-done((bf16[512,768]{1,0:T(8,128)(2,1)}, bf16[512,768]{1,0:T(8,128)(2,1)S(1)}, u32[]{:S(2)}, u32[]{:S(2)}) %collective-permute-start.2) | collective-permute-done | bytes 786464 | tf_op jit(solution)/shard_map/ppermute | solution.py:560
  40.8 3.6 %collective-permute-start.5 = (bf16[512,256]{1,0:T(8,128)(2,1)}, bf16[512,256]{1,0:T(8,128)(2,1)}, u32[]{:S(2)}, u32[]{:S(2)}) collective-permute-start(bf16[512,256]{1,0:T(8,128)(2,1)} %param.19), channel_id=1, source_target_pairs={{0,0},{1,2},{2,1},{3,3},{4,4},{5,6},{6,5},{7,7},{8,8},{9,10},{10,9... | collective-permute-start | bytes 786440 | tf_op jit(solution)/shard_map/ppermute | solution.py:560
  44.4 1.9 collective-permute-start.6
  48.9 6.5 %project.1 = (bf16[512,768]{1,0:T(8,128)(2,1)}, bf16[512,1536]{1,0:T(8,128)(2,1)}, bf16[512,768]{1,0:T(8,128)(2,1)}) custom-call(s32[1]{0:T(128)} %bitcast.1.at_ref, bf16[512,768]{1,0:T(8,128)(2,1)} %copy-done.2, bf16[512,16]{1,0:T(8,128)(2,1)} %get-tuple-element.224.member_ref, bf16[16,1536]{1,0:T(8,128)(2,1)} %fusion.11.mod_ref, ...), custom_call_target="tpu_custom_call" | custom-call | flops 90596968 | bytes 376832 | tf_op jit(solution)/shard_map/project/pallas_call | solution.py:530
  55.6 1.9 collective-permute-start.9
  57.8 1.9 collective-permute-start.10
  59.7 1.7 fusion.30
  63.4 19.8 %attention_forward.1 = (bf16[512,768]{1,0:T(8,128)(2,1)}, f32[512,768]{1,0:T(8,128)}, bf16[12,512,1024]{2,1,0:T(8,128)(2,1)}) custom-call(f32[6,2,256]{2,1,0:T(2,128)} %reshape.193.pair_mix_ref, bf16[512,768]{1,0:T(8,128)(2,1)} %get-tuple-element.108.q_ref, bf16[512,256]{1,0:T(8,128)(2,1)} %collective-permute-done.6.left_ref, ...), custom_call_target="tpu_custom_call" | custom-call | flops 322122560 | bytes 1160601 | tf_op jit(solution)/shard_map/attention_forward/pallas_call | solution.py:530
  83.2 4.9 %branch.1 = (f32[512,768]{1,0:T(8,128)}, f32[512,768]{1,0:T(8,128)}, bf16[512,768]{1,0:T(8,128)(2,1)}) custom-call(bf16[512,768]{1,0:T(8,128)(2,1)} %get-tuple-element.110.attended_ref, bf16[384,768]{1,0:T(8,128)(2,1)} %own_ref.6, bf16[384,768]{1,0:T(8,128)(2,1)} %collective-permute-done.9.other_ref, bf16[512,768]{1,0:T(8,128)(2,1)} %copy-done.2, ...), custom_call_target="tpu_custom_call" | custom-call | flops 30198988 | bytes 342425 | tf_op jit(solution)/shard_map/branch/pallas_call | solution.py:530
  88.0 5.5 %collective-permute-start.11 = (bf16[512,768]{1,0:T(8,128)(2,1)}, bf16[512,768]{1,0:T(8,128)(2,1)S(1)}, u32[]{:S(2)}, u32[]{:S(2)}) collective-permute-start(bf16[512,768]{1,0:T(8,128)(2,1)} %get-tuple-element.113.normed_ref), channel_id=1, source_target_pairs={{0,1},{1,0},{2,3},{3,2},{4,5},{5,4},{6,7},{7,6},{8,9},{9,8},{10,11... | collective-permute-start | bytes 2359304 | tf_op jit(solution)/shard_map/ppermute | solution.py:560
  94.3 18.5 %feed_forward.2 = (f32[512,768]{1,0:T(8,128)}, f32[512,768]{1,0:T(8,128)}, bf16[768,512]{1,0:T(8,128)(2,1)}, bf16[768,512]{1,0:T(8,128)(2,1)}, bf16[512,1536]{1,...) custom-call(bf16[512,768]{1,0:T(8,128)(2,1)} %get-tuple-element.113.normed_ref, ...), custom_call_target="tpu_custom_call" | custom-call | flops 362387872 | bytes 965427 | tf_op jit(solution)/shard_map/feed_forward/pallas_call | solution.py:530
  112.8 7.2 %collective-permute-done.12.dout_ref = bf16[512,768]{1,0:T(8,128)(2,1)S(1)} collective-permute-done((bf16[512,768]{1,0:T(8,128)(2,1)}, bf16[512,768]{1,0:T(8,128)(2,1)S(1)}, u32[]{:S(2)}, u32[]{:S(2)}) %collective-permute-start.12) | collective-permute-done | bytes 786464 | tf_op jit(solution)/shard_map/ppermute | solution.py:560
  120.9 17.9 %feed_forward.3 = (bf16[512,768]{1,0:T(8,128)(2,1)}, bf16[512,768]{1,0:T(8,128)(2,1)}, bf16[768,512]{1,0:T(8,128)(2,1)}, bf16[768,512]{1,0:T(8,128)(2,1)}, bf16[...) custom-call(bf16[512,768]{1,0:T(8,128)(2,1)} %copy-done.9, ...), custom_call_target="tpu_custom_call" | custom-call | flops 362387872 | bytes 886784 | tf_op jit(solution)/shard_map/feed_forward/pallas_call | solution.py:530
  138.8 14.9 %feed_forward_grads.1 = (bf16[3,384,1536]{2,1,0:T(8,128)(2,1)}, bf16[3,384,1536]{2,1,0:T(8,128)(2,1)}) custom-call(bf16[768,512]{1,0:T(8,128)(2,1)} %get-tuple-element.116.normed_t_ref, bf16[768,512]{1,0:T(8,128)(2,1)} %get-tuple-element.124.normed_t_far_ref, bf16[768,512]{1,0:T(8,128)(2,1)} %get-tuple-element.118.d_ffn_t_ref, ...), custom_call_target="tpu_custom_call" | custom-call | flops 362387872 | bytes 983040 | tf_op jit(solution)/shard_map/feed_forward_grads/pallas_call | solution.py:530
  153.6 4.1 %collective-permute-done.13.d_normed_far_ref = bf16[512,768]{1,0:T(8,128)(2,1)S(1)} collective-permute-done((bf16[512,768]{1,0:T(8,128)(2,1)}, bf16[512,768]{1,0:T(8,128)(2,1)S(1)}, u32[]{:S(2)}, u32[]{:S(2)}) %collective-permute-start.13) | collective-permute-done | bytes 786464 | tf_op jit(solution)/shard_map/ppermute | solution.py:560
  158.9 6.1 %collective-permute-done.14 = bf16[3,384,1536]{2,1,0:T(8,128)(2,1)S(1)} collective-permute-done((bf16[3,384,1536]{2,1,0:T(8,128)(2,1)}, bf16[3,384,1536]{2,1,0:T(8,128)(2,1)S(1)}, u32[]{:S(2)}, u32[]{:S(2)}) %collective-permute-start.14) | collective-permute-done | bytes 3538976 | tf_op jit(solution)/shard_map/ppermute | solution.py:560
  165.0 4.3 %add_convert_fusion = (bf16[3,192,1536]{2,1,0:T(8,128)(2,1)S(1)}, bf16[3,192,1536]{2,1,0:T(8,128)(2,1)}) fusion(bf16[3,384,1536]{2,1,0:T(8,128)(2,1)S(1)} %collective-permute-done.14, bf16[3,384,1536]{2,1,0:T(8,128)(2,1)} %get-tuple-element.140), kind=kLoop, calls=%fused_computation.1 | loop fusion | flops 7077888 | bytes 10616832 | tf_op jit(solution)/shard_map/convert_element_type | solution.py:771
  170.5 6.6 %middle_back.1 = (f32[512,768]{1,0:T(8,128)}, bf16[512,768]{1,0:T(8,128)(2,1)}, bf16[512,768]{1,0:T(8,128)(2,1)}, f32[16,2304]{1,0:T(8,128)}) custom-call(f32[512,768]{1,0:T(8,128)} %get-tuple-element.133.d_normed_ref, bf16[512,768]{1,0:T(8,128)(2,1)} %copy-done.8, f32[512,768]{1,0:T(8,128)} %get-tuple-element.152.middle_ref, ...), custom_call_target="tpu_custom_call" | custom-call | flops 60397976 | bytes 546406 | tf_op jit(solution)/shard_map/middle_back/pallas_call | solution.py:530
  177.0 23.4 %attention_backward.1 = (bf16[512,768]{1,0:T(8,128)(2,1)}, bf16[512,1536]{1,0:T(8,128)(2,1)}, bf16[512,1536]{1,0:T(8,128)(2,1)}, bf16[1024,256]{1,0:T(8,128)(2,1...) custom-call(f32[6,2,256]{2,1,0:T(2,128)} %reshape.193.pair_mix_ref, bf16[512,768]{1,0:T(8,128)(2,1)} %get-tuple-element.141.grad_ref, ...), custom_call_target="tpu_custom_call" | custom-call | flops 629145600 | bytes 1429913 | tf_op jit(solution)/shard_map/attention_backward/pallas_call | solution.py:530
  202.2 2.3 collective-permute-start.20
  204.5 1.7 add_convert_fusion.12
  206.3 3.2 collective-permute-start.21
  209.5 3.4 %mix.1 = (bf16[512,768]{1,0:T(8,128)(2,1)}, f32[16,768]{1,0:T(8,128)}) custom-call(f32[512,768]{1,0:T(8,128)} %get-tuple-element.152.middle_ref, f32[512,768]{1,0:T(8,128)} %get-tuple-element.117.ffn_ref, bf16[512,768]{1,0:T(8,128)(2,1)} %collective-permute-done.15.ffn_far_ref, bf16[512,768]{1,0:T(8,128)(2,1)} %collective-permute-done.10.dout_ref, ...), custom_call_target="tpu_custom_call" | custom-call | flops 1258291 | bytes 279756 | tf_op jit(solution)/shard_map/mix/pallas_call | solution.py:530
  212.9 8.8 %attention_grads.1 = (bf16[512,2304]{1,0:T(8,128)(2,1)}, bf16[2,2,384,384]{3,2,1,0:T(8,128)(2,1)}, bf16[2,2,384,384]{3,2,1,0:T(8,128)(2,1)}, bf16[2,2,384,384]{3,2,1,0:T(8,128)(2,1)}, bf16[2,2,384,384]{3,2,1,0:T(8,128)(2,1)}) custom-call(bf16[512,768]{1,0:T(8,128)(2,1)} %get-tuple-element.157.q_ref, bf16[512,1536]{1,0:T(8,128)(2,1)} %get-tuple-element.158.own_ref, ...), custom_call_target="tpu_custom_call" | custom-call | flops 181193936 | bytes 727449 | tf_op jit(solution)/shard_map/attention_grads/pallas_call | solution.py:530
  221.8 2.2 collective-permute-start.22
  224.0 3.2 add_convert_fusion.2
  232.7 2.5 collective-permute-start.18
  235.3 2.2 fusion.2
  237.5 5.2 %collective-permute-start.24 = (bf16[2,384,384]{2,1,0:T(8,128)(2,1)}, bf16[2,384,384]{2,1,0:T(8,128)(2,1)}, u32[]{:S(2)}, u32[]{:S(2)}) collective-permute-start(bf16[2,384,384]{2,1,0:T(8,128)(2,1)} %fusion.2), channel_id=1, source_target_pairs={{0,1},{1,0},{2,3},{3,2},{4,5},{5,4},{6,7},{7,6},{8,9},{9,8},{10,11... | collective-permute-start | bytes 1769480 | tf_op jit(solution)/shard_map/ppermute | solution.py:560
  242.7 2.2 add_convert_fusion.7
  245.1 3.1 collective-permute-done.26
  249.2 8.2 %input_back.1 = (bf16[512,768]{1,0:T(8,128)(2,1)}, f32[16,1536]{1,0:T(8,128)}) custom-call(s32[1]{0:T(128)} %bitcast.1.at_ref, bf16[512,2304]{1,0:T(8,128)(2,1)} %get-tuple-element.174.d_proj_ref, bf16[512,768]{1,0:T(8,128)(2,1)} %copy-done.2, f32[512,768]{1,0:T(8,128)} %get-tuple-element.175.d_middle_ref, bf16[512,16]{1,0:T(8,128)(2,1)} %get-tuple-element.224.member_ref, ...), custom_call_target="tpu_custom_call" | custom-call | flops 90596968 | bytes 460390 | tf_op jit(solution)/shard_map/input_back/pallas_call | solution.py:530
  257.6 1.7 fusion.1
  259.9 2.5 collective-permute-start.27
  267.3 4.0 %collective-permute-start.33 = (bf16[512,768]{1,0:T(8,128)(2,1)S(1)}, bf16[512,768]{1,0:T(8,128)(2,1)}, u32[]{:S(2)}, u32[]{:S(2)}) collective-permute-start(bf16[512,768]{1,0:T(8,128)(2,1)S(1)} %copy-done.29), channel_id=1, source_target_pairs={{0,0},{1,2},{2,1},{3,3},{4,4},{5,6},{6,5},{7,7},{8,8},{9,10},{10,9... | collective-permute-start | bytes 2359304 | tf_op jit(solution)/shard_map/ppermute | solution.py:560
  271.4 4.2 %collective-permute-done.32 = bf16[2,192,384]{2,1,0:T(8,128)(2,1)S(1)} collective-permute-done((bf16[2,192,384]{2,1,0:T(8,128)(2,1)S(1)}, bf16[2,192,384]{2,1,0:T(8,128)(2,1)S(1)}, u32[]{:S(2)}, u32[]{:S(2)}) %collective-permute-start.32) | collective-permute-done | bytes 294944 | tf_op jit(solution)/shard_map/ppermute | solution.py:560
  275.7 9.2 %collective-permute-done.33.refs_1_ = bf16[512,768]{1,0:T(8,128)(2,1)} collective-permute-done((bf16[512,768]{1,0:T(8,128)(2,1)S(1)}, bf16[512,768]{1,0:T(8,128)(2,1)}, u32[]{:S(2)}, u32[]{:S(2)}) %collective-permute-start.33) | collective-permute-done | bytes 786464 | tf_op jit(solution)/shard_map/ppermute | solution.py:560
  285.7 2.3 collective-permute-start.35
  290.6 1.7 collective-permute-start.38
  292.3 3.7 %deliver.1 = (bf16[512,768]{1,0:T(8,128)(2,1)}, bf16[512,768]{1,0:T(8,128)(2,1)}, bf16[512,256]{1,0:T(8,128)(2,1)}, bf16[512,256]{1,0:T(8,128)(2,1)}) custom-call(bf16[512,768]{1,0:T(8,128)(2,1)} %collective-permute-done.18.refs_0_, bf16[512,768]{1,0:T(8,128)(2,1)} %collective-permute-done.33.refs_1_, bf16[512,256]{1,0:T(8,128)(2,1)} %collective-permute-done.20.refs_2_, ...), custom_call_target="tpu_custom_call" | custom-call | bytes 209715 | tf_op jit(solution)/shard_map/deliver/pallas_call | solution.py:530
  297.1 4.1 %collective-permute-done.35 = bf16[32,2944]{1,0:T(8,128)(2,1)} collective-permute-done((bf16[32,2944]{1,0:T(8,128)(2,1)S(1)}, bf16[32,2944]{1,0:T(8,128)(2,1)}, u32[]{:S(2)}, u32[]{:S(2)}) %collective-permute-start.35) | collective-permute-done | bytes 188448 | tf_op jit(solution)/shard_map/ppermute | solution.py:560
  303.2 4.2 %collective-permute-done.38 = bf16[4,96,384]{2,1,0:T(8,128)(2,1)} collective-permute-done((bf16[4,96,384]{2,1,0:T(8,128)(2,1)}, bf16[4,96,384]{2,1,0:T(8,128)(2,1)}, u32[]{:S(2)}, u32[]{:S(2)}) %collective-permute-start.38) | collective-permute-done | bytes 294944 | tf_op jit(solution)/shard_map/ppermute | solution.py:560
  308.3 4.6 %collective-permute-start.39 = (bf16[4,48,384]{2,1,0:T(8,128)(2,1)S(1)}, bf16[4,48,384]{2,1,0:T(8,128)(2,1)S(1)}, u32[]{:S(2)}, u32[]{:S(2)}) collective-permute-start(bf16[4,48,384]{2,1,0:T(8,128)(2,1)S(1)} %add_convert_fusion.13), channel_id=1, source_target_pairs={{0,16},{1,17},{2,18},{3,19},{4,20},{5,21},{6,22},{7,23},{8,24},{9,... | collective-permute-start | bytes 442376 | tf_op jit(solution)/shard_map/ppermute | solution.py:560
  312.9 9.2 %collective-permute-done.40 = bf16[3,48,1536]{2,1,0:T(8,128)(2,1)} collective-permute-done((bf16[3,48,1536]{2,1,0:T(8,128)(2,1)}, bf16[3,48,1536]{2,1,0:T(8,128)(2,1)}, u32[]{:S(2)}, u32[]{:S(2)}) %collective-permute-start.40) | collective-permute-done | bytes 442400 | tf_op jit(solution)/shard_map/ppermute | solution.py:560
  328.5 3.0 fusion.7
  (203 shorter events, 51.5 us)
Async XLA Ops:
  0.6 9.3 %copy-start = (bf16[256,4608]{1,0:T(8,128)(2,1)S(1)}, bf16[256,4608]{1,0:T(8,128)(2,1)}, u32[]{:S(2)}) copy-start(bf16[256,4608]{1,0:T(8,128)(2,1)} %param.25) | copy-start | bytes 7077892
  0.7 7.9 %copy-start.28 = (f32[1,8]{1,0:T(1,128)S(1)}, f32[1,8]{1,0:T(1,128)}, u32[]{:S(2)}) copy-start(f32[1,8]{1,0:T(1,128)} %param.21) | copy-start | bytes 100
  0.7 8.1 %copy-start.13 = (bf16[256,256]{1,0:T(8,128)(2,1)S(1)}, bf16[256,256]{1,0:T(8,128)(2,1)}, u32[]{:S(2)}) copy-start(bf16[256,256]{1,0:T(8,128)(2,1)} %param.24) | copy-start | bytes 393220
  2.8 5.7 %collective-permute-start.3 = (f32[3,8]{1,0:T(4,128)S(1)}, f32[3,8]{1,0:T(4,128)S(1)}, u32[]{:S(2)}, u32[]{:S(2)}) collective-permute-start(f32[3,8]{1,0:T(4,128)S(1)} %pad_maximum_fusion.9), channel_id=1, source_target_pairs={{0,2},{1,3},{2,0},{3,1},{4,6},{5,7},{6,4},{7,5},{8,10},{9,11},{10,... | collective-permute-start | bytes 296 | tf_op jit(solution)/shard_map/ppermute | solution.py:560
  4.2 22.9 %collective-permute-start.1 = (bf16[3,384,384]{2,1,0:T(8,128)(2,1)S(1)}, bf16[3,384,384]{2,1,0:T(8,128)(2,1)}, u32[]{:S(2)}, u32[]{:S(2)}) collective-permute-start(bf16[3,384,384]{2,1,0:T(8,128)(2,1)S(1)} %constant_dynamic-slice_fusion.1), channel_id=1, source_target_pairs={{0,1},{1,0},{2,3},{3,2},{4,5},{5,4},{6,7},{7,6},{8,9},{9,8},{10,11... | collective-permute-start | bytes 2654216 | tf_op jit(solution)/shard_map/ppermute | solution.py:560
  6.9 20.2 %collective-permute-start = (bf16[256,6]{0,1:T(8,128)(2,1)S(1)}, bf16[256,6]{0,1:T(8,128)(2,1)S(1)}, u32[]{:S(2)}, u32[]{:S(2)}) collective-permute-start(bf16[256,6]{0,1:T(8,128)(2,1)S(1)} %copy-done.27), channel_id=1, source_target_pairs={{0,1},{1,0},{2,3},{3,2},{4,5},{5,4},{6,7},{7,6},{8,9},{9,8},{10,11... | collective-permute-start | bytes 9224 | tf_op jit(solution)/shard_map/ppermute | solution.py:560
  27.1 13.7 %collective-permute-start.2 = (bf16[512,768]{1,0:T(8,128)(2,1)}, bf16[512,768]{1,0:T(8,128)(2,1)S(1)}, u32[]{:S(2)}, u32[]{:S(2)}) collective-permute-start(bf16[512,768]{1,0:T(8,128)(2,1)} %param.17), channel_id=1, source_target_pairs={{0,0},{1,2},{2,1},{3,3},{4,4},{5,6},{6,5},{7,7},{8,8},{9,10},{10,9... | collective-permute-start | bytes 2359304 | tf_op jit(solution)/shard_map/ppermute | solution.py:560
  31.7 17.2 %collective-permute-start.4 = (bf16[3,384,384]{2,1,0:T(8,128)(2,1)}, bf16[3,384,384]{2,1,0:T(8,128)(2,1)}, u32[]{:S(2)}, u32[]{:S(2)}) collective-permute-start(bf16[3,384,384]{2,1,0:T(8,128)(2,1)} %collective-permute-done.1.rest_0_), channel_id=1, source_target_pairs={{0,2},{1,3},{2,0},{3,1},{4,6},{5,7},{6,4},{7,5},{8,10},{9,11},{10,... | collective-permute-start | bytes 2654216 | tf_op jit(solution)/shard_map/ppermute | solution.py:560
  40.8 8.1 %copy-start.2 = (bf16[512,768]{1,0:T(8,128)(2,1)}, bf16[512,768]{1,0:T(8,128)(2,1)S(1)}, u32[]{:S(2)}) copy-start(bf16[512,768]{1,0:T(8,128)(2,1)S(1)} %collective-permute-done.2.x_ref) | copy-start | bytes 2359300
  40.8 14.7 %collective-permute-start.5 = (bf16[512,256]{1,0:T(8,128)(2,1)}, bf16[512,256]{1,0:T(8,128)(2,1)}, u32[]{:S(2)}, u32[]{:S(2)}) collective-permute-start(bf16[512,256]{1,0:T(8,128)(2,1)} %param.19), channel_id=1, source_target_pairs={{0,0},{1,2},{2,1},{3,3},{4,4},{5,6},{6,5},{7,7},{8,8},{9,10},{10,9... | collective-permute-start | bytes 786440 | tf_op jit(solution)/shard_map/ppermute | solution.py:560
  44.4 11.1 %collective-permute-start.6 = (bf16[512,256]{1,0:T(8,128)(2,1)}, bf16[512,256]{1,0:T(8,128)(2,1)}, u32[]{:S(2)}, u32[]{:S(2)}) collective-permute-start(bf16[512,256]{1,0:T(8,128)(2,1)} %param.18), channel_id=1, source_target_pairs={{0,0},{1,2},{2,1},{3,3},{4,4},{5,6},{6,5},{7,7},{8,8},{9,10},{10,9... | collective-permute-start | bytes 786440 | tf_op jit(solution)/shard_map/ppermute | solution.py:560
  55.5 5.9 %collective-permute-start.7 = (bf16[512,1536]{1,0:T(8,128)(2,1)}, bf16[512,1536]{1,0:T(8,128)(2,1)S(1)}, u32[]{:S(2)}, u32[]{:S(2)}) collective-permute-start(bf16[512,1536]{1,0:T(8,128)(2,1)} %get-tuple-element.109.k_own_ref.v_own_ref), channel_id=1, source_target_pairs={{0,2},{1,3},{2,0},{3,1},{4,6},{5,7},{6,4},{7,5},{8,10},{9,11},{10,... | collective-permute-start | bytes 4718600 | tf_op jit(solution)/shard_map/ppermute | solution.py:560
  55.6 27.6 %collective-permute-start.9 = (bf16[384,768]{1,0:T(8,128)(2,1)}, bf16[384,768]{1,0:T(8,128)(2,1)}, u32[]{:S(2)}, u32[]{:S(2)}) collective-permute-start(bf16[384,768]{1,0:T(8,128)(2,1)} %own_ref.6), channel_id=1, source_target_pairs={{0,1},{1,0},{2,3},{3,2},{4,5},{5,4},{6,7},{7,6},{8,9},{9,8},{10,11... | collective-permute-start | bytes 1769480 | tf_op jit(solution)/shard_map/ppermute | solution.py:560
  57.5 4.0 %collective-permute-start.8 = (bf16[512,256]{1,0:T(8,128)(2,1)}, bf16[512,256]{1,0:T(8,128)(2,1)S(1)}, u32[]{:S(2)}, u32[]{:S(2)}) collective-permute-start(bf16[512,256]{1,0:T(8,128)(2,1)} %collective-permute-done.5.right_own_ref), channel_id=1, source_target_pairs={{0,2},{1,3},{2,0},{3,1},{4,6},{5,7},{6,4},{7,5},{8,10},{9,11},{10,... | collective-permute-start | bytes 786440 | tf_op jit(solution)/shard_map/ppermute | solution.py:560
  57.8 36.5 %collective-permute-start.10 = (bf16[512,768]{1,0:T(8,128)(2,1)}, bf16[512,768]{1,0:T(8,128)(2,1)}, u32[]{:S(2)}, u32[]{:S(2)}) collective-permute-start(bf16[512,768]{1,0:T(8,128)(2,1)} %param.32), channel_id=1, source_target_pairs={{0,0},{1,2},{2,1},{3,3},{4,4},{5,6},{6,5},{7,7},{8,8},{9,10},{10,9... | collective-permute-start | bytes 2359304 | tf_op jit(solution)/shard_map/ppermute | solution.py:560
  88.0 24.7 %collective-permute-start.11 = (bf16[512,768]{1,0:T(8,128)(2,1)}, bf16[512,768]{1,0:T(8,128)(2,1)S(1)}, u32[]{:S(2)}, u32[]{:S(2)}) collective-permute-start(bf16[512,768]{1,0:T(8,128)(2,1)} %get-tuple-element.113.normed_ref), channel_id=1, source_target_pairs={{0,1},{1,0},{2,3},{3,2},{4,5},{5,4},{6,7},{7,6},{8,9},{9,8},{10,11... | collective-permute-start | bytes 2359304 | tf_op jit(solution)/shard_map/ppermute | solution.py:560
  93.6 26.4 %collective-permute-start.12 = (bf16[512,768]{1,0:T(8,128)(2,1)}, bf16[512,768]{1,0:T(8,128)(2,1)S(1)}, u32[]{:S(2)}, u32[]{:S(2)}) collective-permute-start(bf16[512,768]{1,0:T(8,128)(2,1)} %param.32), channel_id=1, source_target_pairs={{0,1},{1,3},{2,0},{3,2},{4,5},{5,7},{6,4},{7,6},{8,9},{9,11},{10,8... | collective-permute-start | bytes 2359304 | tf_op jit(solution)/shard_map/ppermute | solution.py:560
  138.7 18.9 %collective-permute-start.13 = (bf16[512,768]{1,0:T(8,128)(2,1)}, bf16[512,768]{1,0:T(8,128)(2,1)S(1)}, u32[]{:S(2)}, u32[]{:S(2)}) collective-permute-start(bf16[512,768]{1,0:T(8,128)(2,1)} %get-tuple-element.131), channel_id=1, source_target_pairs={{0,1},{1,0},{2,3},{3,2},{4,5},{5,4},{6,7},{7,6},{8,9},{9,8},{10,11... | collective-permute-start | bytes 2359304 | tf_op jit(solution)/shard_map/ppermute | solution.py:560
  157.7 7.3 %collective-permute-start.14 = (bf16[3,384,1536]{2,1,0:T(8,128)(2,1)}, bf16[3,384,1536]{2,1,0:T(8,128)(2,1)S(1)}, u32[]{:S(2)}, u32[]{:S(2)}) collective-permute-start(bf16[3,384,1536]{2,1,0:T(8,128)(2,1)} %get-tuple-element.132), channel_id=1, source_target_pairs={{0,2},{1,3},{2,0},{3,1},{4,6},{5,7},{6,4},{7,5},{8,10},{9,11},{10,... | collective-permute-start | bytes 10616840 | tf_op jit(solution)/shard_map/ppermute | solution.py:560
  158.9 41.5 %collective-permute-start.15 = (bf16[512,768]{1,0:T(8,128)(2,1)}, bf16[512,768]{1,0:T(8,128)(2,1)}, u32[]{:S(2)}, u32[]{:S(2)}) collective-permute-start(bf16[512,768]{1,0:T(8,128)(2,1)} %get-tuple-element.150), channel_id=1, source_target_pairs={{0,1},{1,0},{2,3},{3,2},{4,5},{5,4},{6,7},{7,6},{8,9},{9,8},{10,11... | collective-permute-start | bytes 2359304 | tf_op jit(solution)/shard_map/ppermute | solution.py:560
  169.2 52.5 %collective-permute-start.19 = (bf16[3,192,1536]{2,1,0:T(8,128)(2,1)}, bf16[3,192,1536]{2,1,0:T(8,128)(2,1)}, u32[]{:S(2)}, u32[]{:S(2)}) collective-permute-start(bf16[3,192,1536]{2,1,0:T(8,128)(2,1)} %get-tuple-element.195), channel_id=1, source_target_pairs={{0,4},{1,5},{2,6},{3,7},{4,0},{5,1},{6,2},{7,3},{8,12},{9,13},{10,... | collective-permute-start | bytes 5308424 | tf_op jit(solution)/shard_map/ppermute | solution.py:560
  200.4 12.5 %collective-permute-start.16 = (bf16[512,1536]{1,0:T(8,128)(2,1)}, bf16[512,1536]{1,0:T(8,128)(2,1)}, u32[]{:S(2)}, u32[]{:S(2)}) collective-permute-start(bf16[512,1536]{1,0:T(8,128)(2,1)} %get-tuple-element.151), channel_id=1, source_target_pairs={{0,2},{1,3},{2,0},{3,1},{4,6},{5,7},{6,4},{7,5},{8,10},{9,11},{10,... | collective-permute-start | bytes 4718600 | tf_op jit(solution)/shard_map/ppermute | solution.py:560
  202.1 2.4 collective-permute-start.17
  202.2 19.6 %collective-permute-start.20 = (bf16[512,256]{1,0:T(8,128)(2,1)}, bf16[512,256]{1,0:T(8,128)(2,1)}, u32[]{:S(2)}, u32[]{:S(2)}) collective-permute-start(bf16[512,256]{1,0:T(8,128)(2,1)} %get-tuple-element.168), channel_id=1, source_target_pairs={{0,0},{1,2},{2,1},{3,3},{4,4},{5,6},{6,5},{7,7},{8,8},{9,10},{10,9... | collective-permute-start | bytes 786440 | tf_op jit(solution)/shard_map/ppermute | solution.py:560
  206.3 15.5 %collective-permute-start.21 = (bf16[512,256]{1,0:T(8,128)(2,1)}, bf16[512,256]{1,0:T(8,128)(2,1)}, u32[]{:S(2)}, u32[]{:S(2)}) collective-permute-start(bf16[512,256]{1,0:T(8,128)(2,1)} %add_convert_fusion.12), channel_id=1, source_target_pairs={{0,0},{1,2},{2,1},{3,3},{4,4},{5,6},{6,5},{7,7},{8,8},{9,10},{10,9... | collective-permute-start | bytes 786440 | tf_op jit(solution)/shard_map/ppermute | solution.py:560
  221.8 13.5 %collective-permute-start.22 = (bf16[2,2,384,384]{3,2,1,0:T(8,128)(2,1)}, bf16[2,2,384,384]{3,2,1,0:T(8,128)(2,1)}, u32[]{:S(2)}, u32[]{:S(2)}) collective-permute-start(bf16[2,2,384,384]{3,2,1,0:T(8,128)(2,1)} %get-tuple-element.171), channel_id=1, source_target_pairs={{0,2},{1,3},{2,0},{3,1},{4,6},{5,7},{6,4},{7,5},{8,10},{9,11},{10,... | collective-permute-start | bytes 3538952 | tf_op jit(solution)/shard_map/ppermute | solution.py:560
  223.9 18.8 %collective-permute-start.23 = (bf16[2,2,384,384]{3,2,1,0:T(8,128)(2,1)}, bf16[2,2,384,384]{3,2,1,0:T(8,128)(2,1)}, u32[]{:S(2)}, u32[]{:S(2)}) collective-permute-start(bf16[2,2,384,384]{3,2,1,0:T(8,128)(2,1)} %get-tuple-element.173), channel_id=1, source_target_pairs={{0,2},{1,3},{2,0},{3,1},{4,6},{5,7},{6,4},{7,5},{8,10},{9,11},{10,... | collective-permute-start | bytes 3538952 | tf_op jit(solution)/shard_map/ppermute | solution.py:560
  227.2 21.0 %collective-permute-start.26 = (bf16[3,96,1536]{2,1,0:T(8,128)(2,1)}, bf16[3,96,1536]{2,1,0:T(8,128)(2,1)S(1)}, u32[]{:S(2)}, u32[]{:S(2)}) collective-permute-start(bf16[3,96,1536]{2,1,0:T(8,128)(2,1)} %get-tuple-element.178), channel_id=1, source_target_pairs={{0,8},{1,9},{2,10},{3,11},{4,12},{5,13},{6,14},{7,15},{8,0},{9,1},... | collective-permute-start | bytes 2654216 | tf_op jit(solution)/shard_map/ppermute | solution.py:560
  232.7 15.5 %copy-start.3 = (bf16[3,96,1536]{2,1,0:T(8,128)(2,1)S(1)}, bf16[3,96,1536]{2,1,0:T(8,128)(2,1)}, u32[]{:S(2)}) copy-start(bf16[3,96,1536]{2,1,0:T(8,128)(2,1)} %get-tuple-element.196) | copy-start | bytes 2654212
  232.7 27.0 %collective-permute-start.18 = (bf16[512,768]{1,0:T(8,128)(2,1)}, bf16[512,768]{1,0:T(8,128)(2,1)}, u32[]{:S(2)}, u32[]{:S(2)}) collective-permute-start(bf16[512,768]{1,0:T(8,128)(2,1)} %get-tuple-element.156), channel_id=1, source_target_pairs={{0,0},{1,2},{2,1},{3,3},{4,4},{5,6},{6,5},{7,7},{8,8},{9,10},{10,9... | collective-permute-start | bytes 2359304 | tf_op jit(solution)/shard_map/ppermute | solution.py:560
  237.5 20.1 %collective-permute-start.24 = (bf16[2,384,384]{2,1,0:T(8,128)(2,1)}, bf16[2,384,384]{2,1,0:T(8,128)(2,1)}, u32[]{:S(2)}, u32[]{:S(2)}) collective-permute-start(bf16[2,384,384]{2,1,0:T(8,128)(2,1)} %fusion.2), channel_id=1, source_target_pairs={{0,1},{1,0},{2,3},{3,2},{4,5},{5,4},{6,7},{7,6},{8,9},{9,8},{10,11... | collective-permute-start | bytes 1769480 | tf_op jit(solution)/shard_map/ppermute | solution.py:560
  244.9 14.8 %collective-permute-start.25 = (bf16[2,2,192,384]{3,2,1,0:T(8,128)(2,1)}, bf16[2,2,192,384]{3,2,1,0:T(8,128)(2,1)}, u32[]{:S(2)}, u32[]{:S(2)}) collective-permute-start(bf16[2,2,192,384]{3,2,1,0:T(8,128)(2,1)} %add_convert_fusion.7), channel_id=1, source_target_pairs={{0,4},{1,5},{2,6},{3,7},{4,0},{5,1},{6,2},{7,3},{8,12},{9,13},{10,... | collective-permute-start | bytes 1769480 | tf_op jit(solution)/shard_map/ppermute | solution.py:560
  248.2 9.3 %copy-start.6 = (bf16[3,96,1536]{2,1,0:T(8,128)(2,1)}, bf16[3,96,1536]{2,1,0:T(8,128)(2,1)S(1)}, u32[]{:S(2)}) copy-start(bf16[3,96,1536]{2,1,0:T(8,128)(2,1)S(1)} %collective-permute-done.26) | copy-start | bytes 2654212
  259.4 12.0 %collective-permute-start.31 = (bf16[2,192,384]{2,1,0:T(8,128)(2,1)S(1)}, bf16[2,192,384]{2,1,0:T(8,128)(2,1)S(1)}, u32[]{:S(2)}, u32[]{:S(2)}) collective-permute-start(bf16[2,192,384]{2,1,0:T(8,128)(2,1)S(1)} %slice.291), channel_id=1, source_target_pairs={{0,4},{1,5},{2,6},{3,7},{4,0},{5,1},{6,2},{7,3},{8,12},{9,13},{10,... | collective-permute-start | bytes 884744 | tf_op jit(solution)/shard_map/ppermute | solution.py:560
  259.9 4.0 %collective-permute-start.27 = (f32[8,4992]{1,0:T(8,128)S(1)}, f32[8,4992]{1,0:T(8,128)S(1)}, u32[]{:S(2)}, u32[]{:S(2)}) collective-permute-start(f32[8,4992]{1,0:T(8,128)S(1)} %pad_maximum_fusion.4), channel_id=1, source_target_pairs={{0,2},{1,3},{2,0},{3,1},{4,6},{5,7},{6,4},{7,5},{8,10},{9,11},{10,... | collective-permute-start | bytes 479240 | tf_op jit(solution)/shard_map/ppermute | solution.py:560
  264.0 3.3 collective-permute-start.28
  264.1 7.2 %collective-permute-start.29 = (bf16[8,2944]{1,0:T(8,128)(2,1)S(1)}, bf16[8,2944]{1,0:T(8,128)(2,1)S(1)}, u32[]{:S(2)}, u32[]{:S(2)}) collective-permute-start(bf16[8,2944]{1,0:T(8,128)(2,1)S(1)} %constant_dynamic-slice_fusion), channel_id=1, source_target_pairs={{0,4},{1,5},{2,6},{3,7},{4,0},{5,1},{6,2},{7,3},{8,12},{9,13},{10,... | collective-permute-start | bytes 141320 | tf_op jit(solution)/shard_map/ppermute | solution.py:560
  265.3 6.0 %collective-permute-start.30 = (bf16[8,2944]{1,0:T(8,128)(2,1)S(1)}, bf16[8,2944]{1,0:T(8,128)(2,1)S(1)}, u32[]{:S(2)}, u32[]{:S(2)}) collective-permute-start(bf16[8,2944]{1,0:T(8,128)(2,1)S(1)} %constant_dynamic-slice_fusion), channel_id=1, source_target_pairs={{0,5},{1,4},{2,7},{3,6},{4,1},{5,0},{6,3},{7,2},{8,13},{9,12},{10,... | collective-permute-start | bytes 141320 | tf_op jit(solution)/shard_map/ppermute | solution.py:560
  266.8 8.8 %collective-permute-start.32 = (bf16[2,192,384]{2,1,0:T(8,128)(2,1)S(1)}, bf16[2,192,384]{2,1,0:T(8,128)(2,1)S(1)}, u32[]{:S(2)}, u32[]{:S(2)}) collective-permute-start(bf16[2,192,384]{2,1,0:T(8,128)(2,1)S(1)} %slice_bitcast_fusion.1), channel_id=1, source_target_pairs={{0,1},{1,0},{2,3},{3,2},{4,5},{5,4},{6,7},{7,6},{8,9},{9,8},{10,11... | collective-permute-start | bytes 884744 | tf_op jit(solution)/shard_map/ppermute | solution.py:560
  267.3 17.6 %collective-permute-start.33 = (bf16[512,768]{1,0:T(8,128)(2,1)S(1)}, bf16[512,768]{1,0:T(8,128)(2,1)}, u32[]{:S(2)}, u32[]{:S(2)}) collective-permute-start(bf16[512,768]{1,0:T(8,128)(2,1)S(1)} %copy-done.29), channel_id=1, source_target_pairs={{0,0},{1,2},{2,1},{3,3},{4,4},{5,6},{6,5},{7,7},{8,8},{9,10},{10,9... | collective-permute-start | bytes 2359304 | tf_op jit(solution)/shard_map/ppermute | solution.py:560
  284.9 11.1 %collective-permute-start.34 = (bf16[32,2944]{1,0:T(8,128)(2,1)S(1)}, bf16[32,2944]{1,0:T(8,128)(2,1)}, u32[]{:S(2)}, u32[]{:S(2)}) collective-permute-start(bf16[32,2944]{1,0:T(8,128)(2,1)S(1)} %pad_maximum_fusion.2), channel_id=1, source_target_pairs={{0,8},{1,9},{2,10},{3,11},{4,12},{5,13},{6,14},{7,15},{8,0},{9,1},... | collective-permute-start | bytes 565256 | tf_op jit(solution)/shard_map/ppermute | solution.py:560
  285.7 15.5 %collective-permute-start.35 = (bf16[32,2944]{1,0:T(8,128)(2,1)S(1)}, bf16[32,2944]{1,0:T(8,128)(2,1)}, u32[]{:S(2)}, u32[]{:S(2)}) collective-permute-start(bf16[32,2944]{1,0:T(8,128)(2,1)S(1)} %pad_maximum_fusion.2), channel_id=1, source_target_pairs={{0,16},{1,17},{2,18},{3,19},{4,20},{5,21},{6,22},{7,23},{8,24},{9,... | collective-permute-start | bytes 565256 | tf_op jit(solution)/shard_map/ppermute | solution.py:560
  288.0 14.1 %collective-permute-start.36 = (bf16[32,2944]{1,0:T(8,128)(2,1)S(1)}, bf16[32,2944]{1,0:T(8,128)(2,1)}, u32[]{:S(2)}, u32[]{:S(2)}) collective-permute-start(bf16[32,2944]{1,0:T(8,128)(2,1)S(1)} %pad_maximum_fusion.2), channel_id=1, source_target_pairs={{0,24},{1,25},{2,26},{3,27},{4,28},{5,29},{6,30},{7,31},{8,16},{9,... | collective-permute-start | bytes 565256 | tf_op jit(solution)/shard_map/ppermute | solution.py:560
  288.5 33.7 %collective-permute-start.40 = (bf16[3,48,1536]{2,1,0:T(8,128)(2,1)}, bf16[3,48,1536]{2,1,0:T(8,128)(2,1)}, u32[]{:S(2)}, u32[]{:S(2)}) collective-permute-start(bf16[3,48,1536]{2,1,0:T(8,128)(2,1)} %add_convert_fusion.10), channel_id=1, source_target_pairs={{0,16},{1,17},{2,18},{3,19},{4,20},{5,21},{6,22},{7,23},{8,24},{9,... | collective-permute-start | bytes 1327112 | tf_op jit(solution)/shard_map/ppermute | solution.py:560
  290.6 16.8 %collective-permute-start.38 = (bf16[4,96,384]{2,1,0:T(8,128)(2,1)}, bf16[4,96,384]{2,1,0:T(8,128)(2,1)}, u32[]{:S(2)}, u32[]{:S(2)}) collective-permute-start(bf16[4,96,384]{2,1,0:T(8,128)(2,1)} %slice.253), channel_id=1, source_target_pairs={{0,8},{1,9},{2,10},{3,11},{4,12},{5,13},{6,14},{7,15},{8,0},{9,1},... | collective-permute-start | bytes 884744 | tf_op jit(solution)/shard_map/ppermute | solution.py:560
  296.0 26.1 %copy-start.7 = (bf16[3,96,1536]{2,1,0:T(8,128)(2,1)S(1)}, bf16[3,96,1536]{2,1,0:T(8,128)(2,1)}, u32[]{:S(2)}) copy-start(bf16[3,96,1536]{2,1,0:T(8,128)(2,1)} %copy-done.6) | copy-start | bytes 2654212
  303.1 24.4 %collective-permute-start.37 = (bf16[128,2944]{1,0:T(8,128)(2,1)S(1)}, bf16[128,2944]{1,0:T(8,128)(2,1)S(1)}, u32[]{:S(2)}, u32[]{:S(2)}) collective-permute-start(bf16[128,2944]{1,0:T(8,128)(2,1)S(1)} %constant_dynamic-update-slice_fusion.4), channel_id=1, source_target_pairs={{0,2},{1,3},{2,0},{3,1},{4,6},{5,7},{6,4},{7,5},{8,10},{9,11},{10,... | collective-permute-start | bytes 2261000 | tf_op jit(solution)/shard_map/ppermute | solution.py:560
  308.3 15.3 %collective-permute-start.39 = (bf16[4,48,384]{2,1,0:T(8,128)(2,1)S(1)}, bf16[4,48,384]{2,1,0:T(8,128)(2,1)S(1)}, u32[]{:S(2)}, u32[]{:S(2)}) collective-permute-start(bf16[4,48,384]{2,1,0:T(8,128)(2,1)S(1)} %add_convert_fusion.13), channel_id=1, source_target_pairs={{0,16},{1,17},{2,18},{3,19},{4,20},{5,21},{6,22},{7,23},{8,24},{9,... | collective-permute-start | bytes 442376 | tf_op jit(solution)/shard_map/ppermute | solution.py:560
  (25 other events, 88.9 us)
